TPU v7x, 512 devices: a whole 4x8x8 slice. The times are simulated.
512 devices in a mesh: dp: 64 (over y, z), tower: 8 (over x, core).
Axes of the slice: x: 4, y: 8, z: 8, core: 2. Of those that a mesh axis runs over, the one named last changes fastest.
Arguments:
- rep: bfloat16 [16384, 2048], P('dp', 'tower'), may hold values from -6 to 6
- arm_ids: int32 [16384], P('dp'), may hold values from 0 to 63, as said below
- outcome: bfloat16 [16384], P('dp'), may hold values from -6 to 6
- weight: bfloat16 [16384], P('dp'), may hold values from 0.5 to 4
- w_hidden: bfloat16 [64, 2048, 2048], P('dp', None, 'tower'), may hold values from -0.125 to 0.125
- b_hidden: float32 [64, 2048], P('dp', 'tower'), may hold values from -3 to 3
- w_head: float32 [64, 2048], P('dp', 'tower'), may hold values from -0.125 to 0.125
- b_head: float32 [64], P('dp'), may hold values from -4 to 4
Outputs:
- grad_hidden: float32 [64, 2048, 2048], P('dp', None, 'tower')
- grad_hidden_bias: float32 [64, 2048], P('dp', 'tower')
- grad_head: float32 [64, 2048], P('dp', 'tower')
- grad_head_bias: float32 [64], P('dp')
- grad_rep: bfloat16 [16384, 2048], P('dp', 'tower')
- predicted: bfloat16 [16384], P('dp')
Inputs may be any that keep to these rules, and one draw needn't show every extreme that they name: `arm_ids`: among the 256 rows of one index of dp at most 14 name one arm, and in every draw some index has an arm named exactly 14 times; over all 16384 rows at most 512 name one arm, and in every draw some arm is named exactly 512 times.
All inputs are finite; a program needn't handle non-finite values.
Results may differ from a plain program's by a relative error of at most 0.019.
Values may be sent and summed in bfloat16 or wider, within the bound.
No kernel may reach another device: no remote copies, remote signals or barrier semaphores. Data moves between devices by JAX's collectives and lax.ppermute only.
A program may use at most 64 MiB of HBM per device.

v0:
```python
import jax
import jax.numpy as jnp
from jax import lax
from jax.sharding import PartitionSpec as P


def arm_slots(arm_ids, arm_count, slot_depth):
    arm_labels = jnp.arange(arm_count, dtype=jnp.int32)
    one_hot = (arm_ids[:, None] == arm_labels[None, :]).astype(jnp.int32)
    arm_rank = jnp.sum(jnp.cumsum(one_hot, axis=0) * one_hot, axis=1) - 1
    return arm_ids * slot_depth + arm_rank


def fill_slots(values, slot_index, slot_total):
    row_count = values.shape[0]
    source_row = (
        jnp.full((slot_total,), row_count, jnp.int32)
        .at[slot_index]
        .set(jnp.arange(row_count, dtype=jnp.int32))
    )
    padded_rows = jnp.concatenate(
        [values, jnp.zeros((1,) + values.shape[1:], values.dtype)], axis=0
    )
    return padded_rows[source_row]


def tower_step(inputs, targets, weights, matrix, bias_cols, head_cols, head_bias):
    pre_act = jnp.dot(inputs, matrix, preferred_element_type=jnp.float32) + bias_cols
    sigmoid_pre = jax.nn.sigmoid(pre_act)
    activation = pre_act * sigmoid_pre
    pred_share = jnp.sum(activation * head_cols, axis=1)
    full_pred = lax.psum(pred_share, "tower") + head_bias
    resid_grad = weights * (full_pred - targets)
    pre_grad = resid_grad[:, None] * head_cols * sigmoid_pre * (1.0 + pre_act * (1.0 - sigmoid_pre))
    pre_grad_half = pre_grad.astype(jnp.bfloat16)
    grad_matrix = lax.dot_general(
        inputs, pre_grad_half, (((0,), (0,)), ((), ())), preferred_element_type=jnp.float32
    )
    grad_bias = jnp.sum(pre_grad, axis=0)
    grad_vector = jnp.sum(resid_grad[:, None] * activation, axis=0)
    grad_scalar = jnp.sum(resid_grad)
    return (full_pred, pre_grad_half, grad_matrix, grad_bias, grad_vector, grad_scalar)


def body(rep, arm_ids, outcome, weight, w_hidden, b_hidden, w_head, b_head):
    arm_count = lax.axis_size("dp")
    row_count = arm_ids.shape[0]
    slot_depth = 7 * (row_count // (2 * arm_count))
    slot_total = arm_count * slot_depth
    slot_index = arm_slots(arm_ids, arm_count, slot_depth)
    side_data = fill_slots(jnp.stack([outcome, weight], axis=1), slot_index, slot_total).reshape(
        arm_count, slot_depth, 2
    )
    matrix = w_hidden[0]
    bias_cols = b_hidden[0]
    head_cols = w_head[0]
    head_bias = b_head[0]
    wide_rep = lax.all_gather(rep, "tower", axis=1, tiled=True)
    wide_slots = fill_slots(wide_rep, slot_index, slot_total).reshape(
        arm_count, slot_depth, wide_rep.shape[1]
    )
    arrived, arrived_side = (
        lax.all_to_all(wide_slots, "dp", split_axis=0, concat_axis=0, tiled=True),
        lax.all_to_all(side_data, "dp", split_axis=0, concat_axis=0, tiled=True),
    )
    slot_rows = arrived.reshape(slot_total, arrived.shape[2])
    arrived_side = arrived_side.reshape(slot_total, 2).astype(jnp.float32)
    targets = arrived_side[:, 0]
    weights = arrived_side[:, 1]
    full_pred, pre_grad_half, grad_matrix, grad_bias, grad_vector, grad_scalar = tower_step(
        slot_rows, targets, weights, matrix, bias_cols, head_cols, head_bias
    )
    pred_half = full_pred.astype(jnp.bfloat16)
    partial_full = lax.dot_general(
        pre_grad_half, matrix, (((1,), (1,)), ((), ())), preferred_element_type=jnp.float32
    ).astype(jnp.bfloat16)
    full_width = partial_full.shape[1]
    returned, pred_back = (
        lax.all_to_all(
            partial_full.reshape(arm_count, slot_depth, full_width),
            "dp",
            split_axis=0,
            concat_axis=0,
            tiled=True,
        ),
        lax.all_to_all(
            pred_half.reshape(arm_count, slot_depth), "dp", split_axis=0, concat_axis=0, tiled=True
        ),
    )
    row_partial = returned.reshape(slot_total, full_width)[slot_index]
    grad_rep = lax.psum_scatter(
        row_partial.astype(jnp.float32).astype(jnp.bfloat16),
        "tower",
        scatter_dimension=1,
        tiled=True,
    )
    predicted = pred_back.reshape(slot_total)[slot_index]
    return (
        grad_matrix[None],
        grad_bias[None],
        grad_vector[None],
        grad_scalar.reshape(1),
        grad_rep,
        predicted,
    )


def solution(mesh):
    return jax.shard_map(
        body,
        mesh=mesh,
        in_specs=(
            P("dp", "tower"),
            P("dp"),
            P("dp"),
            P("dp"),
            P("dp", None, "tower"),
            P("dp", "tower"),
            P("dp", "tower"),
            P("dp"),
        ),
        out_specs=(
            P("dp", None, "tower"),
            P("dp", "tower"),
            P("dp", "tower"),
            P("dp"),
            P("dp", "tower"),
            P("dp"),
        ),
        check_vma=False,
    )
```

profile of v0, /device:TPU:32, one launch (start us, length us, event | category | flops | bytes accessed | tf_op | source)
XLA Modules:
  0.0 429.7 jit_solution(11687043676716487167)
XLA Ops:
  12.4 1.4 scatter_custom_fusion
  13.9 2.4 gather_fusion.1
  17.2 16.3 %all-to-all-start.1 = ((bf16[64,14,2]{1,2,0:T(2,128)(2,1)}), bf16[64,14,2]{1,2,0:T(2,128)(2,1)S(1)}, u32[]{:S(2)}, u32[]{:S(2)}) async-start(bf16[64,14,2]{1,2,0:T(2,128)(2,1)} %copy.27), calls=%async_computation.1 | async-start | bytes 65536 | tf_op jit(solution)/shard_map/all_to_all | solution.py:64
  33.6 9.6 %all-gather.2.cloned.1.call-done = bf16[256,2048]{1,0:T(8,128)(2,1)} async-done(((bf16[256,256]{1,0:T(8,128)(2,1)}), bf16[256,2048]{1,0:T(8,128)(2,1)}) %all-gather.2.cloned.1.call-update) | async-done | bytes 1048592 | tf_op jit(solution)/shard_map/all_gather | solution.py:58
  43.2 1.3 concatenate.6
  44.5 5.0 %gather_fusion = bf16[896,2048]{1,0:T(8,128)(2,1)} fusion(bf16[257,2048]{1,0:T(8,128)(2,1)S(1)} %concatenate.6, s32[1024]{0:T(1024)S(1)} %pad_clamp_fusion.1), kind=kCustom, calls=%fused_computation | custom fusion | bytes 7343616 | tf_op jit(solution)/shard_map/gather | solution.py:24
  49.5 6.0 %reshape.59 = bf16[64,14,2048]{2,1,0:T(8,128)(2,1)} reshape(bf16[896,2048]{1,0:T(8,128)(2,1)} %gather_fusion) | data formatting | bytes 7340032 | tf_op jit(solution)/shard_map/reshape | solution.py:59
  55.5 13.6 %all-to-all-start = ((bf16[64,14,2048]{2,1,0:T(8,128)(2,1)}), bf16[64,14,2048]{2,1,0:T(8,128)(2,1)}, u32[]{:S(2)}, u32[]{:S(2)}) async-start(bf16[64,14,2048]{2,1,0:T(8,128)(2,1)} %reshape.59), calls=%async_computation | async-start | bytes 8388608 | tf_op jit(solution)/shard_map/all_to_all | solution.py:63
  70.2 123.7 %all-to-all-done = bf16[64,14,2048]{2,1,0:T(8,128)(2,1)} async-done(((bf16[64,14,2048]{2,1,0:T(8,128)(2,1)}), bf16[64,14,2048]{2,1,0:T(8,128)(2,1)}, u32[]{:S(2)}, u32[]{:S(2)}) %all-to-all-start) | async-done | bytes 3670048 | tf_op jit(solution)/shard_map/all_to_all | solution.py:63
  193.8 5.8 %reshape.60 = bf16[896,2048]{1,0:T(8,128)(2,1)} reshape(bf16[64,14,2048]{2,1,0:T(8,128)(2,1)} %all-to-all-done) | data formatting | bytes 7340032 | tf_op jit(solution)/shard_map/reshape | solution.py:66
  199.7 3.3 multiply_reduce_fusion.1
  202.9 12.4 %psum.7 = f32[896]{0:T(1024)S(1)} all-reduce(f32[896]{0:T(1024)S(1)} %get-tuple-element.13), channel_id=1, replica_groups=mesh['dp'=64,'tower'=8] {'tower'}, use_global_device_ids=true, to_apply=%region_5.6 | all-reduce | flops 896 | bytes 7168 | tf_op jit(solution)/shard_map/psum | solution.py:32
  216.0 3.1 convolution_convert_fusion
  219.1 6.0 %reshape.63 = bf16[64,14,2048]{2,1,0:T(8,128)(2,1)} reshape(bf16[896,2048]{1,0:T(8,128)(2,1)} %convolution_convert_fusion) | data formatting | bytes 7340032 | tf_op jit(solution)/shard_map/reshape | solution.py:80
  225.1 19.8 %all-to-all-start.2 = ((bf16[64,14,2048]{2,1,0:T(8,128)(2,1)}), bf16[64,14,2048]{2,1,0:T(8,128)(2,1)}, u32[]{:S(2)}, u32[]{:S(2)}) async-start(bf16[64,14,2048]{2,1,0:T(8,128)(2,1)} %reshape.63), calls=%async_computation.2 | async-start | bytes 8388608 | tf_op jit(solution)/shard_map/all_to_all | solution.py:79
  245.2 119.3 %all-to-all-done.2 = bf16[64,14,2048]{2,1,0:T(8,128)(2,1)} async-done(((bf16[64,14,2048]{2,1,0:T(8,128)(2,1)}), bf16[64,14,2048]{2,1,0:T(8,128)(2,1)}, u32[]{:S(2)}, u32[]{:S(2)}) %all-to-all-start.2) | async-done | bytes 3670048 | tf_op jit(solution)/shard_map/all_to_all | solution.py:79
  364.5 6.0 %reshape.64 = bf16[896,2048]{1,0:T(8,128)(2,1)} reshape(bf16[64,14,2048]{2,1,0:T(8,128)(2,1)} %all-to-all-done.2) | data formatting | bytes 7340032 | tf_op jit(solution)/shard_map/reshape | solution.py:90
  370.5 5.9 %gather_fusion.2 = bf16[256,2048]{1,0:T(8,128)(2,1)} fusion(bf16[896,2048]{1,0:T(8,128)(2,1)} %reshape.64, s32[1024]{0:T(1024)S(1)} %pad_clamp_fusion), kind=kCustom, calls=%fused_computation.2 | custom fusion | bytes 2098176 | tf_op jit(solution)/shard_map/gather | solution.py:90
  377.1 17.7 %all-to-all-start.3 = ((bf16[64,1,14]{2,1,0:T(2,128)(2,1)}), bf16[64,1,14]{2,1,0:T(2,128)(2,1)S(1)}, u32[]{:S(2)}, u32[]{:S(2)}) async-start(bf16[64,1,14]{2,1,0:T(2,128)(2,1)} %all_to_all.20), calls=%async_computation.4 | async-start | bytes 65536 | tf_op jit(solution)/shard_map/all_to_all | solution.py:86
  394.8 4.9 %convolution_bitcast_fusion = f32[1,2048,256]{2,1,0:T(8,128)} fusion(bf16[896,2048]{1,0:T(8,128)(2,1)} %reshape.60, f32[896,256]{1,0:T(8,128)S(1)} %get-tuple-element.14, f32[896]{0:T(1024)S(1)} %get-tuple-element.11, f32[256]{0:T(256)S(1)} %bitcast.41), kind=kOutput, calls=%fused_computation.6 | convolution fusion | flops 941817856 | bytes 6689280 | tf_op jit(solution)/shard_map/dot_general | solution.py:36
  399.8 1.1 multiply_reduce_fusion
  400.8 1.2 all-to-all-done.3
  402.3 2.4 gather_fusion.3
  404.7 18.1 %reduce-scatter.2.cloned.1.call-done = bf16[256,256]{1,0:T(8,128)(2,1)} async-done(((bf16[256,2048]{1,0:T(8,128)(2,1)}), bf16[256,256]{1,0:T(8,128)(2,1)}) %reduce-scatter.2.cloned.1.call-update) | async-done | bytes 131088 | tf_op jit(solution)/shard_map/reduce_scatter | solution.py:91
  (38 shorter events, 8.4 us)
Async XLA Ops:
  7.2 192.5 %copy-start = (bf16[1,2048,256]{2,1,0:T(8,128)(2,1)S(1)}, bf16[1,2048,256]{2,1,0:T(8,128)(2,1)}, u32[]{:S(2)}) copy-start(bf16[1,2048,256]{2,1,0:T(8,128)(2,1)} %param.12) | copy-start | bytes 3145732
  7.2 36.0 %all-gather.2.cloned.1.call-start = ((), (), s32[]{:S(2)}) async-start(), calls=%async_computation.5 | async-start | bytes 1179648 | tf_op jit(solution)/shard_map/all_gather | solution.py:58
  17.2 38.3 %all-to-all-start.1 = ((bf16[64,14,2]{1,2,0:T(2,128)(2,1)}), bf16[64,14,2]{1,2,0:T(2,128)(2,1)S(1)}, u32[]{:S(2)}, u32[]{:S(2)}) async-start(bf16[64,14,2]{1,2,0:T(2,128)(2,1)} %copy.27), calls=%async_computation.1 | async-start | bytes 65536 | tf_op jit(solution)/shard_map/all_to_all | solution.py:64
  55.5 138.3 %all-to-all-start = ((bf16[64,14,2048]{2,1,0:T(8,128)(2,1)}), bf16[64,14,2048]{2,1,0:T(8,128)(2,1)}, u32[]{:S(2)}, u32[]{:S(2)}) async-start(bf16[64,14,2048]{2,1,0:T(8,128)(2,1)} %reshape.59), calls=%async_computation | async-start | bytes 8388608 | tf_op jit(solution)/shard_map/all_to_all | solution.py:63
  70.1 129.5 %copy-start.1 = (f32[1,256]{1,0:T(1,128)S(1)}, f32[1,256]{1,0:T(1,128)}, u32[]{:S(2)}) copy-start(f32[1,256]{1,0:T(1,128)} %param.14) | copy-start | bytes 3076
  70.1 129.5 %copy-start.2 = (f32[1,256]{1,0:T(1,128)S(1)}, f32[1,256]{1,0:T(1,128)}, u32[]{:S(2)}) copy-start(f32[1,256]{1,0:T(1,128)} %param.13) | copy-start | bytes 3076
  225.1 139.4 %all-to-all-start.2 = ((bf16[64,14,2048]{2,1,0:T(8,128)(2,1)}), bf16[64,14,2048]{2,1,0:T(8,128)(2,1)}, u32[]{:S(2)}, u32[]{:S(2)}) async-start(bf16[64,14,2048]{2,1,0:T(8,128)(2,1)} %reshape.63), calls=%async_computation.2 | async-start | bytes 8388608 | tf_op jit(solution)/shard_map/all_to_all | solution.py:79
  244.9 177.9 %reduce-scatter.2.cloned.1.call-start = ((), (), s32[]{:S(2)}) async-start(), calls=%async_computation.6 | async-start | bytes 1179648 | tf_op jit(solution)/shard_map/reduce_scatter | solution.py:91
  377.1 24.9 %all-to-all-start.3 = ((bf16[64,1,14]{2,1,0:T(2,128)(2,1)}), bf16[64,1,14]{2,1,0:T(2,128)(2,1)S(1)}, u32[]{:S(2)}, u32[]{:S(2)}) async-start(bf16[64,1,14]{2,1,0:T(2,128)(2,1)} %all_to_all.20), calls=%async_computation.4 | async-start | bytes 65536 | tf_op jit(solution)/shard_map/all_to_all | solution.py:86
Sparse Core Ops, SparseCore 0:
  10.1 32.9 all-gather.1
  376.5 46.3 reduce-scatter.1
where the time goes:
time: 431 us; the launch traced here: 430 us
  waiting for transfers between devices  273 us (63%)
  starting transfers between devices  67.7 us (16%)
  local copies, waits for them, and re-layouts  46.2 us (11%)
  between operations  14.8 us (3%)
  blocking collectives  12.4 us (3%)
  matrix products  11.4 us (3%)
  other arithmetic  4.59 us (1%)
    all_to_all x1, waiting for transfers between devices, body(): lax.all_to_all(wide_slots, 'dp', split_axis=0, concat_axis=0, tiled=True)  124 us
    all_to_all x1, waiting for transfers between devices, body(): lax.all_to_all(partial_full.reshape(arm_count, slot_depth, full_width), '...  119 us
    all_to_all x1, starting transfers between devices, body(): lax.all_to_all(partial_full.reshape(arm_count, slot_depth, full_width), '...  19.8 us
    reduce_scatter x1, waiting for transfers between devices, body(): lax.psum_scatter(row_partial.astype(jnp.float32).astype(jnp.bfloat16), 't...  18.1 us
    all_to_all x1, starting transfers between devices, body(): lax.all_to_all(pred_half.reshape(arm_count, slot_depth), 'dp', split_axis...  17.7 us
    all_to_all x1, starting transfers between devices, body(): lax.all_to_all(side_data, 'dp', split_axis=0, concat_axis=0, tiled=True)  16.3 us
    all_to_all x1, starting transfers between devices, body(): lax.all_to_all(wide_slots, 'dp', split_axis=0, concat_axis=0, tiled=True)  13.6 us
    psum x1, blocking collectives, tower_step(): full_pred = lax.psum(pred_share, 'tower') + head_bias  12.4 us
  transfers between devices with their start and end apart: 6, of which 5 were waited for; matrix products, arithmetic and copies ran while one was open for 7% of the time, Pallas kernels for 0%

commit v1 on v0

v1 whole, which is shorter than its diff:
```python
import functools

import jax
import jax.numpy as jnp
from jax import lax
from jax.experimental import pallas as pl
from jax.experimental.pallas import tpu as pltpu
from jax.sharding import PartitionSpec as P

F32, BF16, I32 = jnp.float32, jnp.bfloat16, jnp.int32
SLOT = 16
SIDE = 14
EXTRA = 16
INTERPRET = False

NN = (((1,), (0,)), ((), ()))
NT = (((1,), (1,)), ((), ()))
TN = (((0,), (0,)), ((), ()))


def mm(a, b, dims=NN):
    return lax.dot_general(a, b, dims, preferred_element_type=F32)


def iota(shape, dim):
    return lax.broadcasted_iota(I32, shape, dim)


def ones_where(mask):
    return jnp.where(mask, 1.0, 0.0).astype(BF16)


def call(kernel, out_shape, n_smem=0, flops=0, nbytes=0, vmem=32):
    def run(*args):
        specs = [pl.BlockSpec(memory_space=pltpu.SMEM)] * n_smem
        specs += [pl.BlockSpec(memory_space=pltpu.VMEM)] * (len(args) - n_smem)
        many = isinstance(out_shape, (tuple, list))
        out_spec = pl.BlockSpec(memory_space=pltpu.VMEM)
        return pl.pallas_call(
            kernel,
            out_shape=out_shape,
            in_specs=specs,
            out_specs=[out_spec] * len(out_shape) if many else out_spec,
            compiler_params=pltpu.CompilerParams(vmem_limit_bytes=vmem * 2**20),
            cost_estimate=pl.CostEstimate(flops=flops, bytes_accessed=nbytes, transcendentals=0),
            interpret=INTERPRET,
        )(*args)

    return run


def sds(shape, dtype):
    return jax.ShapeDtypeStruct(shape, dtype)


def side_rows(arms):
    shape = (arms * SLOT, arms)
    return ones_where(iota(shape, 0) == iota(shape, 1) * SLOT + SIDE)


def pick_side(arms):
    shape = (arms, arms * SLOT)
    return ones_where(iota(shape, 1) == iota(shape, 0) * SLOT + SIDE)


def pack_kernel(arms, arm_ref, outcome_ref, weight_ref, rep_ref, slots_ref, slot_ref, rank_ref):
    rows, width = rep_ref.shape
    ids = arm_ref[...]
    hot = iota((arms, rows), 0) == ids
    hot_half = ones_where(hot)
    earlier = ones_where(iota((rows, rows), 0) < iota((rows, rows), 1))
    counts = mm(hot_half, earlier)
    rank = jnp.sum(jnp.where(hot, counts, 0.0), axis=0, keepdims=True).astype(I32)
    slot = ids * SLOT + rank
    slot_ref[...] = slot
    rank_ref[...] = rank
    place = ones_where(iota((arms * SLOT, rows), 0) == slot)
    lane = iota((width, rows), 0)
    side_t = jnp.where(lane == rank, outcome_ref[...].astype(F32), 0.0) + jnp.where(
        lane == rank + SLOT, weight_ref[...].astype(F32), 0.0
    )
    side = mm(hot_half, side_t.astype(BF16), NT).astype(BF16)
    slots_ref[...] = (mm(place, rep_ref[...]) + mm(side_rows(arms), side)).astype(BF16)


def compact_kernel(arms, packed, slots_ref, rows_ref, side_ref, pos_ref):
    total, width = slots_ref.shape
    slots = slots_ref[...]
    side = mm(pick_side(arms), slots)
    lane8 = iota((8, width), 1)
    weight_lanes = ones_where((lane8 >= SLOT) & (lane8 < 2 * SLOT))
    counts = mm(weight_lanes, ones_where(side > 0.0), NT).astype(BF16)
    source, owner = iota((arms, total), 0), iota((arms, total), 1) // SLOT
    same = source == owner
    start = mm(counts, ones_where(source < owner))
    count = mm(counts, ones_where(same))
    depth = iota((8, total), 1) % SLOT
    pos = jnp.where(depth < count.astype(I32), start.astype(I32) + depth, 2 * packed)
    pos_ref[...] = pos
    gather = ones_where(iota((packed, total), 0) == pos[0:1])
    rows_ref[...] = mm(gather, slots).astype(BF16)
    side_half = side.astype(BF16)
    lane, place = iota((width, total), 0), iota((width, total), 1) % SLOT
    target = mm(side_half, ones_where(lane == place))
    weight = mm(side_half, ones_where(lane == place + SLOT))
    target = jnp.sum(jnp.where(same, target, 0.0), axis=0, keepdims=True)
    weight = jnp.sum(jnp.where(same, weight, 0.0), axis=0, keepdims=True)
    both = jnp.where(iota((8, total), 0) == 0, target, weight)
    side_ref[...] = mm(both.astype(BF16), gather, NT)


def split_pair(value):
    high = value.astype(BF16)
    return high, (value - high.astype(F32)).astype(BF16)


def forward_kernel(
    block_ref, x0, x1, x2, x3, y0, y1, y2, y3, w_ref, b_ref, head_ref,
    act_ref, g_ref, keep_ref, send_ref, share_ref,
):
    rows, width = x0.shape
    pre = jnp.zeros((rows, b_ref.shape[1]), F32)
    for j, x_ref in enumerate((x0, x1, x2, x3, y0, y1, y2, y3)):
        pre += mm(x_ref[...], w_ref[block_ref[j]])
    pre = pre + b_ref[...]
    sig = jax.nn.sigmoid(pre)
    head = head_ref[...]
    act = pre * sig
    g = head * sig * (1.0 + pre * (1.0 - sig))
    act_ref[...] = act
    g_ref[...] = g
    g_half = g.astype(BF16)
    share = lax.dot_general(
        jnp.broadcast_to(head, (8, head.shape[1])), act, NT,
        precision=lax.Precision.HIGHEST, preferred_element_type=F32,
    )
    for j in range(4):
        keep_ref[j] = mm(g_half, w_ref[block_ref[j]], NT).astype(BF16)
        send_ref[pl.ds(j * rows, rows), :] = mm(g_half, w_ref[block_ref[4 + j]], NT).astype(BF16)
    high, low = split_pair(share)
    share_ref[...] = high.astype(F32) + low.astype(F32)
    send_ref[pl.ds(4 * rows, EXTRA), :] = extra_rows(high, low, width)


def extra_rows(high, low, width):
    parts = high.shape[1] // width
    row = iota((EXTRA, width), 0)
    out = jnp.zeros((EXTRA, width), F32)
    for i in range(parts):
        piece = slice(i * width, (i + 1) * width)
        out = jnp.where(row == i, high[0:1, piece].astype(F32), out)
        out = jnp.where(row == parts + i, low[0:1, piece].astype(F32), out)
    return out.astype(BF16)


def read_extra(extra, parts):
    extra = extra.astype(F32)
    both = [extra[i : i + 1] + extra[parts + i : parts + i + 1] for i in range(parts)]
    return jnp.concatenate(both, axis=1)


def chip_sum_kernel(keep_ref, got_ref, share_ref, own_ref, m1_ref, m2_ref, m3_ref, chip_ref):
    _, rows, width = keep_ref.shape
    parts = rows // width
    share = share_ref[0:1] + read_extra(got_ref[pl.ds(4 * rows, EXTRA), :], parts)
    high, low = split_pair(share)
    chip_ref[...] = jnp.broadcast_to(high.astype(F32) + low.astype(F32), chip_ref.shape)
    extra = extra_rows(high, low, width)
    for j, out in enumerate((own_ref, m1_ref, m2_ref, m3_ref)):
        total = keep_ref[j].astype(F32) + got_ref[pl.ds(j * rows, rows), :].astype(F32)
        if j == 0:
            out[...] = total
        else:
            out[pl.ds(0, rows), :] = total.astype(BF16)
            out[pl.ds(rows, EXTRA), :] = extra


def back_kernel(arms, own_ref, r1_ref, r2_ref, r3_ref, chip_ref, side_ref, pos_ref, bias_ref, slots_ref, resid_ref):
    rows, width = own_ref.shape
    parts = rows // width
    total = arms * SLOT
    tail = pl.ds(rows, EXTRA)
    near = read_extra(r1_ref[tail, :], parts) + read_extra(r2_ref[tail, :], parts)
    pred = ((chip_ref[0:1] + read_extra(r3_ref[tail, :], parts)) + near) + bias_ref[0]
    resid = side_ref[1:2] * (pred - side_ref[0:1])
    resid_col = jnp.transpose(jnp.broadcast_to(resid, (128, rows)))
    resid_ref[...] = resid_col
    body = pl.ds(0, rows)
    grad = own_ref[...] + r1_ref[body, :].astype(F32) + r2_ref[body, :].astype(F32) + r3_ref[body, :].astype(F32)
    grad = (grad * resid_col[:, 0:1]).astype(BF16)
    gather = ones_where(iota((rows, total), 0) == pos_ref[0:1])
    pred_slot = mm(jnp.broadcast_to(pred, (8, rows)).astype(BF16), gather)
    same = iota((arms, total), 0) == iota((arms, total), 1) // SLOT
    spread = jnp.where(same, pred_slot[0:1], 0.0).astype(BF16)
    lane = ones_where(iota((width, total), 0) == iota((width, total), 1) % SLOT)
    pred_side = mm(spread, lane, NT).astype(BF16)
    slots_ref[...] = (mm(gather, grad, TN) + mm(side_rows(arms), pred_side)).astype(BF16)


def unpack_kernel(arms, slots_ref, slot_ref, rank_ref, arm_ref, grad_ref, pred_ref):
    total, width = slots_ref.shape
    rows = slot_ref.shape[1]
    slots = slots_ref[...]
    place = ones_where(iota((total, rows), 0) == slot_ref[...])
    grad_ref[...] = mm(place, slots, TN).astype(BF16)
    pred_side = mm(pick_side(arms), slots).astype(BF16)
    by_arm = mm(pred_side, ones_where(iota((width, rows), 0) == rank_ref[...]))
    hot = iota((arms, rows), 0) == arm_ref[...]
    pred_ref[...] = jnp.sum(jnp.where(hot, by_arm, 0.0), axis=0, keepdims=True).astype(BF16)


def grads_kernel(
    block_ref, x0, x1, x2, x3, y0, y1, y2, y3, act_ref, g_ref, resid_ref,
    matrix_ref, bias_ref, head_ref, scalar_ref,
):
    resid = resid_ref[...]
    resid_col = resid[:, 0:1]
    pre_grad = g_ref[...] * resid_col
    bias_ref[...] = jnp.sum(pre_grad, axis=0, keepdims=True)
    head_ref[...] = jnp.sum(act_ref[...] * resid_col, axis=0, keepdims=True)
    scalar_ref[...] = jnp.sum(resid, axis=0, keepdims=True)
    pre_half = pre_grad.astype(BF16)
    for j, x_ref in enumerate((x0, x1, x2, x3, y0, y1, y2, y3)):
        matrix_ref[block_ref[j]] = mm(x_ref[...], pre_half, TN)


def body(rep, arm_ids, outcome, weight, w_hidden, b_hidden, w_head, b_head):
    arms = lax.axis_size("dp")
    tower = lax.axis_size("tower")
    chips = tower // 2
    rows, width = rep.shape
    packed = 2 * rows
    total = arms * SLOT
    hidden = w_hidden.shape[2]

    t = lax.axis_index("tower")
    chip, core = t // 2, t % 2
    near = [(chip + d) % chips for d in (0, chips - 1, 1, 2)]
    block = jnp.stack([n * 2 + core for n in near] + [n * 2 + 1 - core for n in near]).astype(I32)

    def hop(value, by):
        return lax.ppermute(value, "tower", [(i, (i + 2 * by) % tower) for i in range(tower)])

    def swap(value):
        return lax.ppermute(value, "tower", [(i, i ^ 1) for i in range(tower)])

    def exchange(slots):
        cut = slots.reshape(arms, SLOT, width)
        return lax.all_to_all(cut, "dp", split_axis=0, concat_axis=0, tiled=True).reshape(total, width)

    ids = arm_ids.reshape(1, rows)
    slots, slot, rank = call(
        functools.partial(pack_kernel, arms),
        (sds((total, width), BF16), sds((1, rows), I32), sds((1, rows), I32)),
        flops=2 * total * rows * width,
    )(ids, outcome.reshape(1, rows), weight.reshape(1, rows), rep)
    arrived = exchange(slots)
    x0, side, pos = call(
        functools.partial(compact_kernel, arms, packed),
        (sds((packed, width), BF16), sds((8, packed), F32), sds((8, total), I32)),
        flops=2 * total * packed * width,
    )(arrived)
    x3, x1, x2 = hop(x0, 2), hop(x0, 1), hop(x0, -1)
    xs = (x0, x1, x2, x3)
    ys = tuple(swap(x) for x in xs)
    matrix = w_hidden.reshape(tower, width, hidden)
    act, g, keep, send, share = call(
        forward_kernel,
        (
            sds((packed, hidden), F32),
            sds((packed, hidden), F32),
            sds((chips, packed, width), BF16),
            sds((chips * packed + EXTRA, width), BF16),
            sds((8, packed), F32),
        ),
        n_smem=1,
        flops=4 * packed * tower * width * hidden,
    )(block, *xs, *ys, matrix, b_hidden, w_head)
    got = swap(send)
    own, m1, m2, m3, chip_share = call(
        chip_sum_kernel,
        (sds((packed, width), F32),)
        + (sds((packed + EXTRA, width), BF16),) * 3
        + (sds((8, packed), F32),),
    )(keep, got, share)
    r3, r1, r2 = hop(m3, 2), hop(m1, -1), hop(m2, 1)
    back_slots, resid = call(
        lambda bias, *refs: back_kernel(arms, *refs[:7], bias, *refs[7:]),
        (sds((total, width), BF16), sds((packed, 128), F32)),
        n_smem=1,
        flops=2 * total * packed * width,
    )(b_head, own, r1, r2, r3, chip_share, side, pos)
    returned = exchange(back_slots)
    grad_matrix, grad_bias, grad_vector, grad_scalar = call(
        grads_kernel,
        (
            sds((tower, width, hidden), F32),
            sds((1, hidden), F32),
            sds((1, hidden), F32),
            sds((1, 128), F32),
        ),
        n_smem=1,
        flops=2 * packed * tower * width * hidden,
        nbytes=5 * 2**20,
    )(block, *xs, *ys, act, g, resid)
    grad_rep, predicted = call(
        functools.partial(unpack_kernel, arms),
        (sds((rows, width), BF16), sds((1, rows), BF16)),
        flops=2 * total * rows * width,
    )(returned, slot, rank, ids)
    return (
        grad_matrix.reshape(1, tower * width, hidden),
        grad_bias,
        grad_vector,
        grad_scalar[0, :1],
        grad_rep,
        predicted.reshape(rows),
    )


def solution(mesh):
    return jax.shard_map(
        body,
        mesh=mesh,
        in_specs=(
            P("dp", "tower"),
            P("dp"),
            P("dp"),
            P("dp"),
            P("dp", None, "tower"),
            P("dp", "tower"),
            P("dp", "tower"),
            P("dp"),
        ),
        out_specs=(
            P("dp", None, "tower"),
            P("dp", "tower"),
            P("dp", "tower"),
            P("dp"),
            P("dp", "tower"),
            P("dp"),
        ),
        check_vma=False,
    )
```

time: 431 us -> 122 us (0.28)
  the two profiles are of different devices: /device:TPU:32 before, /device:TPU:22 now
where the time goes in v1:
time: 122 us
  blocking collectives  35.7 us (29%)
  starting transfers between devices  35.2 us (29%)
  waiting for transfers between devices  30.5 us (25%)
  Pallas kernels  11.4 us (9%)
  local copies, waits for them, and re-layouts  6.92 us (6%)
  between operations  1.56 us (1%)
    all_to_all x1, blocking collectives, exchange(): lax.all_to_all(cut, 'dp', split_axis=0, concat_axis=0, tiled=True)  35.7 us
    ppermute x6, starting transfers between devices, hop(): lax.ppermute(value, 'tower', [(i, (i + 2 * by) % tower) for i in range(to...  18.1 us
    all_to_all x1, waiting for transfers between devices, exchange(): lax.all_to_all(cut, 'dp', split_axis=0, concat_axis=0, tiled=True)  15 us
    ppermute x6, waiting for transfers between devices, hop(): lax.ppermute(value, 'tower', [(i, (i + 2 * by) % tower) for i in range(to...  12.3 us
    pallas_call x7, Pallas kernels, run(): pl.pallas_call(kernel, out_shape=out_shape, in_specs=specs, out_specs=[ou...  11.4 us
    ppermute x5, starting transfers between devices, swap(): return lax.ppermute(value, 'tower', [(i, i ^ 1) for i in range(tower)])  10.9 us
    all_to_all x1, starting transfers between devices, exchange(): lax.all_to_all(cut, 'dp', split_axis=0, concat_axis=0, tiled=True)  6.14 us
    unnamed x20, local copies, waits for them, and re-layouts  5.51 us
  transfers between devices with their start and end apart: 12, of which 6 were waited for; matrix products, arithmetic and copies ran while one was open for 0% of the time, Pallas kernels for 2%

profile of v1, /device:TPU:22, one launch (start us, length us, event | category | flops | bytes accessed | tf_op | source)
XLA Modules:
  0.0 121.7 jit_solution(7884437754373543083)
XLA Ops:
  4.4 35.7 %all_to_all.10 = bf16[64,16,256]{2,1,0:T(8,128)(2,1)S(1)} all-to-all(bf16[64,16,256]{2,1,0:T(8,128)(2,1)S(1)} %bitcast.18), channel_id=1, replica_groups=mesh['dp'=64,'tower'=8] {'dp'}, dimensions={0} | all-to-all | bytes 1048576 | tf_op jit(solution)/shard_map/all_to_all | solution.py:249
  40.0 1.2 shard_map.128
  41.2 2.4 %collective-permute-start = (bf16[512,256]{1,0:T(8,128)(2,1)S(1)}, bf16[512,256]{1,0:T(8,128)(2,1)S(1)}, u32[]{:S(2)}, u32[]{:S(2)}) collective-permute-start(bf16[512,256]{1,0:T(8,128)(2,1)S(1)} %get-tuple-element.31.x0), channel_id=1, source_target_pairs={{0,2},{1,3},{2,4},{3,5},{4,6},{5,7},{6,0},{7,1},{8,10},{9,11},{10,... | collective-permute-start | bytes 786440 | tf_op jit(solution)/shard_map/ppermute | solution.py:242
  43.6 3.5 %collective-permute-start.1 = (bf16[512,256]{1,0:T(8,128)(2,1)S(1)}, bf16[512,256]{1,0:T(8,128)(2,1)S(1)}, u32[]{:S(2)}, u32[]{:S(2)}) collective-permute-start(bf16[512,256]{1,0:T(8,128)(2,1)S(1)} %get-tuple-element.31.x0), channel_id=1, source_target_pairs={{0,6},{1,7},{2,0},{3,1},{4,2},{5,3},{6,4},{7,5},{8,14},{9,15},{10,... | collective-permute-start | bytes 786440 | tf_op jit(solution)/shard_map/ppermute | solution.py:242
  47.1 3.3 %collective-permute-start.2 = (bf16[512,256]{1,0:T(8,128)(2,1)S(1)}, bf16[512,256]{1,0:T(8,128)(2,1)S(1)}, u32[]{:S(2)}, u32[]{:S(2)}) collective-permute-start(bf16[512,256]{1,0:T(8,128)(2,1)S(1)} %get-tuple-element.31.x0), channel_id=1, source_target_pairs={{0,4},{1,5},{2,6},{3,7},{4,0},{5,1},{6,2},{7,3},{8,12},{9,13},{10,... | collective-permute-start | bytes 786440 | tf_op jit(solution)/shard_map/ppermute | solution.py:242
  50.4 1.9 %collective-permute-start.3 = (bf16[512,256]{1,0:T(8,128)(2,1)S(1)}, bf16[512,256]{1,0:T(8,128)(2,1)S(1)}, u32[]{:S(2)}, u32[]{:S(2)}) collective-permute-start(bf16[512,256]{1,0:T(8,128)(2,1)S(1)} %get-tuple-element.31.x0), channel_id=1, source_target_pairs={{0,1},{1,0},{2,3},{3,2},{4,5},{5,4},{6,7},{7,6},{8,9},{9,8},{10,11... | collective-permute-start | bytes 786440 | tf_op jit(solution)/shard_map/ppermute | solution.py:245
  52.4 2.4 %collective-permute-start.4 = (bf16[512,256]{1,0:T(8,128)(2,1)S(1)}, bf16[512,256]{1,0:T(8,128)(2,1)S(1)}, u32[]{:S(2)}, u32[]{:S(2)}) collective-permute-start(bf16[512,256]{1,0:T(8,128)(2,1)S(1)} %collective-permute-done.x1), channel_id=1, source_target_pairs={{0,1},{1,0},{2,3},{3,2},{4,5},{5,4},{6,7},{7,6},{8,9},{9,8},{10,11... | collective-permute-start | bytes 786440 | tf_op jit(solution)/shard_map/ppermute | solution.py:245
  54.8 4.0 %collective-permute-done.1.x2 = bf16[512,256]{1,0:T(8,128)(2,1)S(1)} collective-permute-done((bf16[512,256]{1,0:T(8,128)(2,1)S(1)}, bf16[512,256]{1,0:T(8,128)(2,1)S(1)}, u32[]{:S(2)}, u32[]{:S(2)}) %collective-permute-start.1) | collective-permute-done | bytes 262176 | tf_op jit(solution)/shard_map/ppermute | solution.py:242
  58.7 1.9 %collective-permute-start.5 = (bf16[512,256]{1,0:T(8,128)(2,1)S(1)}, bf16[512,256]{1,0:T(8,128)(2,1)S(1)}, u32[]{:S(2)}, u32[]{:S(2)}) collective-permute-start(bf16[512,256]{1,0:T(8,128)(2,1)S(1)} %collective-permute-done.1.x2), channel_id=1, source_target_pairs={{0,1},{1,0},{2,3},{3,2},{4,5},{5,4},{6,7},{7,6},{8,9},{9,8},{10,11... | collective-permute-start | bytes 786440 | tf_op jit(solution)/shard_map/ppermute | solution.py:245
  60.7 2.4 %collective-permute-start.6 = (bf16[512,256]{1,0:T(8,128)(2,1)S(1)}, bf16[512,256]{1,0:T(8,128)(2,1)S(1)}, u32[]{:S(2)}, u32[]{:S(2)}) collective-permute-start(bf16[512,256]{1,0:T(8,128)(2,1)S(1)} %collective-permute-done.2.x3), channel_id=1, source_target_pairs={{0,1},{1,0},{2,3},{3,2},{4,5},{5,4},{6,7},{7,6},{8,9},{9,8},{10,11... | collective-permute-start | bytes 786440 | tf_op jit(solution)/shard_map/ppermute | solution.py:245
  64.2 1.3 %copy-done.6 = bf16[1,2048,256]{2,1,0:T(8,128)(2,1)S(1)} copy-done((bf16[1,2048,256]{2,1,0:T(8,128)(2,1)S(1)}, bf16[1,2048,256]{2,1,0:T(8,128)(2,1)}, u32[]{:S(2)}) %copy-start.6) | copy-done | bytes 1048600
  65.5 3.4 %shard_map.129 = (f32[512,256]{1,0:T(8,128)S(1)}, f32[512,256]{1,0:T(8,128)S(1)}, bf16[4,512,256]{2,1,0:T(8,128)(2,1)S(1)}, bf16[2064,256]{1,0:T(8,128)(2,1)S(1)}, f32[8,512]{1,0:T(8,128)S(1)}) custom-call(s32[8]{0:T(128)S(1)} %stack.35.block_ref, bf16[512,256]{1,0:T(8,128)(2,1)S(1)} %get-tuple-element.31.x0, bf16[512,256]{1,0:T(8,128)(2,1)S(1)} %collective-permute-done.x1, ...), custom_call_target="tpu_custom_call" | custom-call | flops 1073741824 | tf_op jit(solution)/shard_map/pallas_call | solution.py:39
  68.9 2.3 %collective-permute-start.7 = (bf16[2064,256]{1,0:T(8,128)(2,1)S(1)}, bf16[2064,256]{1,0:T(8,128)(2,1)S(1)}, u32[]{:S(2)}, u32[]{:S(2)}) collective-permute-start(bf16[2064,256]{1,0:T(8,128)(2,1)S(1)} %get-tuple-element.35), channel_id=1, source_target_pairs={{0,1},{1,0},{2,3},{3,2},{4,5},{5,4},{6,7},{7,6},{8,9},{9,8},{10,11... | collective-permute-start | bytes 3170312 | tf_op jit(solution)/shard_map/ppermute | solution.py:245
  71.2 2.3 %collective-permute-done.7.got_ref = bf16[2064,256]{1,0:T(8,128)(2,1)S(1)} collective-permute-done((bf16[2064,256]{1,0:T(8,128)(2,1)S(1)}, bf16[2064,256]{1,0:T(8,128)(2,1)S(1)}, u32[]{:S(2)}, u32[]{:S(2)}) %collective-permute-start.7) | collective-permute-done | bytes 1056800 | tf_op jit(solution)/shard_map/ppermute | solution.py:245
  73.8 1.9 %collective-permute-start.10 = (bf16[528,256]{1,0:T(8,128)(2,1)S(1)}, bf16[528,256]{1,0:T(8,128)(2,1)S(1)}, u32[]{:S(2)}, u32[]{:S(2)}) collective-permute-start(bf16[528,256]{1,0:T(8,128)(2,1)S(1)} %get-tuple-element.40), channel_id=1, source_target_pairs={{0,4},{1,5},{2,6},{3,7},{4,0},{5,1},{6,2},{7,3},{8,12},{9,13},{10,... | collective-permute-start | bytes 811016 | tf_op jit(solution)/shard_map/ppermute | solution.py:242
  75.7 2.3 %collective-permute-start.8 = (bf16[528,256]{1,0:T(8,128)(2,1)S(1)}, bf16[528,256]{1,0:T(8,128)(2,1)S(1)}, u32[]{:S(2)}, u32[]{:S(2)}) collective-permute-start(bf16[528,256]{1,0:T(8,128)(2,1)S(1)} %get-tuple-element.38), channel_id=1, source_target_pairs={{0,6},{1,7},{2,0},{3,1},{4,2},{5,3},{6,4},{7,5},{8,14},{9,15},{10,... | collective-permute-start | bytes 811016 | tf_op jit(solution)/shard_map/ppermute | solution.py:242
  78.0 4.7 %collective-permute-start.9 = (bf16[528,256]{1,0:T(8,128)(2,1)S(1)}, bf16[528,256]{1,0:T(8,128)(2,1)S(1)}, u32[]{:S(2)}, u32[]{:S(2)}) collective-permute-start(bf16[528,256]{1,0:T(8,128)(2,1)S(1)} %get-tuple-element.39), channel_id=1, source_target_pairs={{0,2},{1,3},{2,4},{3,5},{4,6},{5,7},{6,0},{7,1},{8,10},{9,11},{10,... | collective-permute-start | bytes 811016 | tf_op jit(solution)/shard_map/ppermute | solution.py:242
  83.4 3.1 %collective-permute-done.10.refs_3_ = bf16[528,256]{1,0:T(8,128)(2,1)S(1)} collective-permute-done((bf16[528,256]{1,0:T(8,128)(2,1)S(1)}, bf16[528,256]{1,0:T(8,128)(2,1)S(1)}, u32[]{:S(2)}, u32[]{:S(2)}) %collective-permute-start.10) | collective-permute-done | bytes 270368 | tf_op jit(solution)/shard_map/ppermute | solution.py:242
  86.5 5.2 %collective-permute-done.8.refs_1_ = bf16[528,256]{1,0:T(8,128)(2,1)S(1)} collective-permute-done((bf16[528,256]{1,0:T(8,128)(2,1)S(1)}, bf16[528,256]{1,0:T(8,128)(2,1)S(1)}, u32[]{:S(2)}, u32[]{:S(2)}) %collective-permute-start.8) | collective-permute-done | bytes 270368 | tf_op jit(solution)/shard_map/ppermute | solution.py:242
  91.7 1.9 %shard_map.131 = (bf16[1024,256]{1,0:T(8,128)(2,1)}, f32[512,128]{1,0:T(8,128)S(1)}) custom-call(f32[1]{0:T(128)S(6)} %copy.14.bias, f32[512,256]{1,0:T(8,128)S(1)} %get-tuple-element.37.refs_0_, bf16[528,256]{1,0:T(8,128)(2,1)S(1)} %collective-permute-done.8.refs_1_, bf16[528,256]{1,0:T(8,128)(2,1)S(1)} %collective-permute-done.9.refs_2_, ...), custom_call_target="tpu_custom_call" | custom-call | flops 268435456 | tf_op jit(solution)/shard_map/pallas_call | solution.py:39
  94.3 6.1 %all-to-all-start.1 = ((bf16[64,16,256]{2,1,0:T(8,128)(2,1)}), bf16[64,16,256]{2,1,0:T(8,128)(2,1)S(1)}, u32[]{:S(2)}, u32[]{:S(2)}) async-start(bf16[64,16,256]{2,1,0:T(8,128)(2,1)} %bitcast.14), calls=%async_computation.1 | async-start | bytes 1048576 | tf_op jit(solution)/shard_map/all_to_all | solution.py:249
  102.4 2.7 %shard_map.132 = (f32[8,256,256]{2,1,0:T(8,128)}, f32[1,256]{1,0:T(1,128)}, f32[1,256]{1,0:T(1,128)}, f32[1,128]{1,0:T(1,128)}) custom-call(s32[8]{0:T(128)S(1)} %stack.35.block_ref, bf16[512,256]{1,0:T(8,128)(2,1)S(1)} %get-tuple-element.31.x0, bf16[512,256]{1,0:T(8,128)(2,1)S(1)} %collective-permute-done.x1, ...), custom_call_target="tpu_custom_call" | custom-call | flops 536870912 | bytes 5242880 | tf_op jit(solution)/shard_map/pallas_call | solution.py:39
  105.1 15.0 %all-to-all-done.1 = bf16[64,16,256]{2,1,0:T(8,128)(2,1)S(1)} async-done(((bf16[64,16,256]{2,1,0:T(8,128)(2,1)}), bf16[64,16,256]{2,1,0:T(8,128)(2,1)S(1)}, u32[]{:S(2)}, u32[]{:S(2)}) %all-to-all-start.1) | async-done | bytes 524320 | tf_op jit(solution)/shard_map/all_to_all | solution.py:249
  120.1 1.1 shard_map.133
  (32 shorter events, 8.1 us)
Async XLA Ops:
  1.9 0.7 copy-start.4
  2.6 0.9 copy-start.7
  4.3 59.9 %copy-start.8 = (f32[1,256]{1,0:T(1,128)S(1)}, f32[1,256]{1,0:T(1,128)}, u32[]{:S(2)}) copy-start(f32[1,256]{1,0:T(1,128)} %b_ref.1) | copy-start | bytes 3076
  4.3 59.9 %copy-start.9 = (f32[1,256]{1,0:T(1,128)S(1)}, f32[1,256]{1,0:T(1,128)}, u32[]{:S(2)}) copy-start(f32[1,256]{1,0:T(1,128)} %head_ref.1) | copy-start | bytes 3076
  41.2 11.1 %collective-permute-start = (bf16[512,256]{1,0:T(8,128)(2,1)S(1)}, bf16[512,256]{1,0:T(8,128)(2,1)S(1)}, u32[]{:S(2)}, u32[]{:S(2)}) collective-permute-start(bf16[512,256]{1,0:T(8,128)(2,1)S(1)} %get-tuple-element.31.x0), channel_id=1, source_target_pairs={{0,2},{1,3},{2,4},{3,5},{4,6},{5,7},{6,0},{7,1},{8,10},{9,11},{10,... | collective-permute-start | bytes 786440 | tf_op jit(solution)/shard_map/ppermute | solution.py:242
  43.6 15.1 %collective-permute-start.1 = (bf16[512,256]{1,0:T(8,128)(2,1)S(1)}, bf16[512,256]{1,0:T(8,128)(2,1)S(1)}, u32[]{:S(2)}, u32[]{:S(2)}) collective-permute-start(bf16[512,256]{1,0:T(8,128)(2,1)S(1)} %get-tuple-element.31.x0), channel_id=1, source_target_pairs={{0,6},{1,7},{2,0},{3,1},{4,2},{5,3},{6,4},{7,5},{8,14},{9,15},{10,... | collective-permute-start | bytes 786440 | tf_op jit(solution)/shard_map/ppermute | solution.py:242
  47.1 13.5 %collective-permute-start.2 = (bf16[512,256]{1,0:T(8,128)(2,1)S(1)}, bf16[512,256]{1,0:T(8,128)(2,1)S(1)}, u32[]{:S(2)}, u32[]{:S(2)}) collective-permute-start(bf16[512,256]{1,0:T(8,128)(2,1)S(1)} %get-tuple-element.31.x0), channel_id=1, source_target_pairs={{0,4},{1,5},{2,6},{3,7},{4,0},{5,1},{6,2},{7,3},{8,12},{9,13},{10,... | collective-permute-start | bytes 786440 | tf_op jit(solution)/shard_map/ppermute | solution.py:242
  50.4 12.8 %collective-permute-start.3 = (bf16[512,256]{1,0:T(8,128)(2,1)S(1)}, bf16[512,256]{1,0:T(8,128)(2,1)S(1)}, u32[]{:S(2)}, u32[]{:S(2)}) collective-permute-start(bf16[512,256]{1,0:T(8,128)(2,1)S(1)} %get-tuple-element.31.x0), channel_id=1, source_target_pairs={{0,1},{1,0},{2,3},{3,2},{4,5},{5,4},{6,7},{7,6},{8,9},{9,8},{10,11... | collective-permute-start | bytes 786440 | tf_op jit(solution)/shard_map/ppermute | solution.py:245
  52.4 10.9 %collective-permute-start.4 = (bf16[512,256]{1,0:T(8,128)(2,1)S(1)}, bf16[512,256]{1,0:T(8,128)(2,1)S(1)}, u32[]{:S(2)}, u32[]{:S(2)}) collective-permute-start(bf16[512,256]{1,0:T(8,128)(2,1)S(1)} %collective-permute-done.x1), channel_id=1, source_target_pairs={{0,1},{1,0},{2,3},{3,2},{4,5},{5,4},{6,7},{7,6},{8,9},{9,8},{10,11... | collective-permute-start | bytes 786440 | tf_op jit(solution)/shard_map/ppermute | solution.py:245
  58.7 4.5 %collective-permute-start.5 = (bf16[512,256]{1,0:T(8,128)(2,1)S(1)}, bf16[512,256]{1,0:T(8,128)(2,1)S(1)}, u32[]{:S(2)}, u32[]{:S(2)}) collective-permute-start(bf16[512,256]{1,0:T(8,128)(2,1)S(1)} %collective-permute-done.1.x2), channel_id=1, source_target_pairs={{0,1},{1,0},{2,3},{3,2},{4,5},{5,4},{6,7},{7,6},{8,9},{9,8},{10,11... | collective-permute-start | bytes 786440 | tf_op jit(solution)/shard_map/ppermute | solution.py:245
  60.7 3.6 %collective-permute-start.6 = (bf16[512,256]{1,0:T(8,128)(2,1)S(1)}, bf16[512,256]{1,0:T(8,128)(2,1)S(1)}, u32[]{:S(2)}, u32[]{:S(2)}) collective-permute-start(bf16[512,256]{1,0:T(8,128)(2,1)S(1)} %collective-permute-done.2.x3), channel_id=1, source_target_pairs={{0,1},{1,0},{2,3},{3,2},{4,5},{5,4},{6,7},{7,6},{8,9},{9,8},{10,11... | collective-permute-start | bytes 786440 | tf_op jit(solution)/shard_map/ppermute | solution.py:245
  64.2 4.7 %copy-start = (bf16[512,256]{1,0:T(8,128)(2,1)}, bf16[512,256]{1,0:T(8,128)(2,1)S(1)}, u32[]{:S(2)}) copy-start(bf16[512,256]{1,0:T(8,128)(2,1)S(1)} %collective-permute-done.6.y3) | copy-start | bytes 786436
  64.2 1.3 %copy-start.6 = (bf16[1,2048,256]{2,1,0:T(8,128)(2,1)S(1)}, bf16[1,2048,256]{2,1,0:T(8,128)(2,1)}, u32[]{:S(2)}) copy-start(bf16[1,2048,256]{2,1,0:T(8,128)(2,1)} %param.12) | copy-start | bytes 3145732
  68.9 4.6 %collective-permute-start.7 = (bf16[2064,256]{1,0:T(8,128)(2,1)S(1)}, bf16[2064,256]{1,0:T(8,128)(2,1)S(1)}, u32[]{:S(2)}, u32[]{:S(2)}) collective-permute-start(bf16[2064,256]{1,0:T(8,128)(2,1)S(1)} %get-tuple-element.35), channel_id=1, source_target_pairs={{0,1},{1,0},{2,3},{3,2},{4,5},{5,4},{6,7},{7,6},{8,9},{9,8},{10,11... | collective-permute-start | bytes 3170312 | tf_op jit(solution)/shard_map/ppermute | solution.py:245
  73.8 12.8 %collective-permute-start.10 = (bf16[528,256]{1,0:T(8,128)(2,1)S(1)}, bf16[528,256]{1,0:T(8,128)(2,1)S(1)}, u32[]{:S(2)}, u32[]{:S(2)}) collective-permute-start(bf16[528,256]{1,0:T(8,128)(2,1)S(1)} %get-tuple-element.40), channel_id=1, source_target_pairs={{0,4},{1,5},{2,6},{3,7},{4,0},{5,1},{6,2},{7,3},{8,12},{9,13},{10,... | collective-permute-start | bytes 811016 | tf_op jit(solution)/shard_map/ppermute | solution.py:242
  75.7 16.0 %collective-permute-start.8 = (bf16[528,256]{1,0:T(8,128)(2,1)S(1)}, bf16[528,256]{1,0:T(8,128)(2,1)S(1)}, u32[]{:S(2)}, u32[]{:S(2)}) collective-permute-start(bf16[528,256]{1,0:T(8,128)(2,1)S(1)} %get-tuple-element.38), channel_id=1, source_target_pairs={{0,6},{1,7},{2,0},{3,1},{4,2},{5,3},{6,4},{7,5},{8,14},{9,15},{10,... | collective-permute-start | bytes 811016 | tf_op jit(solution)/shard_map/ppermute | solution.py:242
  78.0 13.7 %collective-permute-start.9 = (bf16[528,256]{1,0:T(8,128)(2,1)S(1)}, bf16[528,256]{1,0:T(8,128)(2,1)S(1)}, u32[]{:S(2)}, u32[]{:S(2)}) collective-permute-start(bf16[528,256]{1,0:T(8,128)(2,1)S(1)} %get-tuple-element.39), channel_id=1, source_target_pairs={{0,2},{1,3},{2,4},{3,5},{4,6},{5,7},{6,0},{7,1},{8,10},{9,11},{10,... | collective-permute-start | bytes 811016 | tf_op jit(solution)/shard_map/ppermute | solution.py:242
  93.6 0.7 copy-start.2
  94.3 25.8 %all-to-all-start.1 = ((bf16[64,16,256]{2,1,0:T(8,128)(2,1)}), bf16[64,16,256]{2,1,0:T(8,128)(2,1)S(1)}, u32[]{:S(2)}, u32[]{:S(2)}) async-start(bf16[64,16,256]{2,1,0:T(8,128)(2,1)} %bitcast.14), calls=%async_computation.1 | async-start | bytes 1048576 | tf_op jit(solution)/shard_map/all_to_all | solution.py:249
  100.5 1.0 copy-start.1
  101.4 0.9 copy-start.3
  102.4 17.7 %copy-start.5 = (s32[256]{0:T(256)S(1)}, s32[256]{0:T(256)}, u32[]{:S(2)}) copy-start(s32[256]{0:T(256)} %param.9) | copy-start | bytes 3076

commit v2 on v1

v2 whole, which is shorter than its diff:
```python
import functools

import jax
import jax.numpy as jnp
from jax import lax
from jax.experimental import pallas as pl
from jax.experimental.pallas import tpu as pltpu
from jax.sharding import PartitionSpec as P

F32, BF16, I32 = jnp.float32, jnp.bfloat16, jnp.int32
SLOT = 16
SIDE = 14
EXTRA = 16
INTERPRET = False
VMEM, SMEM, ANY = pltpu.VMEM, pltpu.SMEM, pl.ANY

NN = (((1,), (0,)), ((), ()))
NT = (((1,), (1,)), ((), ()))
TN = (((0,), (0,)), ((), ()))


def mm(a, b, dims=NN):
    return lax.dot_general(a, b, dims, preferred_element_type=F32)


def iota(shape, dim):
    return lax.broadcasted_iota(I32, shape, dim)


def ones_where(mask):
    return jnp.where(mask, 1.0, 0.0).astype(BF16)


def call(kernel, out_shape, spaces=None, outs=None, scratch=(), flops=0, nbytes=0, vmem=32):
    def run(*args):
        return pl.pallas_call(
            kernel,
            out_shape=out_shape,
            in_specs=[pl.BlockSpec(memory_space=m) for m in spaces or [VMEM] * len(args)],
            out_specs=[pl.BlockSpec(memory_space=m) for m in outs or [VMEM] * len(out_shape)],
            scratch_shapes=list(scratch),
            compiler_params=pltpu.CompilerParams(vmem_limit_bytes=vmem * 2**20),
            cost_estimate=pl.CostEstimate(flops=flops, bytes_accessed=nbytes, transcendentals=0),
            interpret=INTERPRET,
        )(*args)

    return run


def sds(shape, dtype):
    return jax.ShapeDtypeStruct(shape, dtype)


def side_rows(arms):
    shape = (arms * SLOT, arms)
    return ones_where(iota(shape, 0) == iota(shape, 1) * SLOT + SIDE)


def pick_side(arms):
    shape = (arms, arms * SLOT)
    return ones_where(iota(shape, 1) == iota(shape, 0) * SLOT + SIDE)


def pack_kernel(arms, meta_ref, rep_hbm, slots_ref, aux_ref, rep_ref, sem):
    copy = pltpu.make_async_copy(rep_hbm, rep_ref, sem)
    copy.start()
    rows, width = rep_ref.shape
    ids = meta_ref[0:1].astype(I32)
    hot = iota((arms, rows), 0) == ids
    hot_half = ones_where(hot)
    earlier = ones_where(iota((rows, rows), 0) < iota((rows, rows), 1))
    counts = mm(hot_half, earlier)
    rank = jnp.sum(jnp.where(hot, counts, 0.0), axis=0, keepdims=True).astype(I32)
    slot = ids * SLOT + rank
    row8 = iota((8, rows), 0)
    aux_ref[...] = jnp.where(row8 == 0, slot, jnp.where(row8 == 1, rank, ids))
    place = ones_where(iota((arms * SLOT, rows), 0) == slot)
    lane = iota((width, rows), 0)
    side_t = jnp.where(lane == rank, meta_ref[1:2], 0.0) + jnp.where(lane == rank + SLOT, meta_ref[2:3], 0.0)
    side = mm(hot_half, side_t.astype(BF16), NT).astype(BF16)
    side_part = mm(side_rows(arms), side)
    copy.wait()
    slots_ref[...] = (mm(place, rep_ref[...]) + side_part).astype(BF16)


def compact_kernel(arms, packed, slots_ref, send_ref, side_ref, pos_ref):
    total, width = slots_ref.shape
    slots = slots_ref[...]
    side = mm(pick_side(arms), slots)
    lane8 = iota((8, width), 1)
    weight_lanes = ones_where((lane8 >= SLOT) & (lane8 < 2 * SLOT))
    counts = mm(weight_lanes, ones_where(side > 0.0), NT).astype(BF16)
    source, owner = iota((arms, total), 0), iota((arms, total), 1) // SLOT
    same = source == owner
    start = mm(counts, ones_where(source < owner))
    count = mm(counts, ones_where(same))
    depth = iota((8, total), 1) % SLOT
    pos = jnp.where(depth < count.astype(I32), start.astype(I32) + depth, 2 * packed)
    pos_ref[...] = pos
    gather = ones_where(iota((packed, total), 0) == pos[0:1])
    rows = mm(gather, slots).astype(BF16)
    half = packed // 2
    for d in range(send_ref.shape[0]):
        send_ref[d] = rows[(d % 2) * half : (d % 2 + 1) * half]
    side_half = side.astype(BF16)
    lane, place = iota((width, total), 0), iota((width, total), 1) % SLOT
    target = mm(side_half, ones_where(lane == place))
    weight = mm(side_half, ones_where(lane == place + SLOT))
    target = jnp.sum(jnp.where(same, target, 0.0), axis=0, keepdims=True)
    weight = jnp.sum(jnp.where(same, weight, 0.0), axis=0, keepdims=True)
    both = jnp.where(iota((8, total), 0) == 0, target, weight)
    side_ref[...] = mm(both.astype(BF16), gather, NT)


def column(row):
    return jnp.transpose(jnp.broadcast_to(row, (128, row.shape[1])))


def half_unit(x_ref, w_ref, bias, head):
    pre = jnp.broadcast_to(bias, (x_ref.shape[1], bias.shape[1]))
    for j in range(x_ref.shape[0]):
        pre += mm(x_ref[j], w_ref[j])
    sig = jax.nn.sigmoid(pre)
    return pre * sig, head * sig * (1.0 + pre * (1.0 - sig))


def forward_kernel(x_ref, near_ref, far_ref, bh_ref, far_bh_ref, msg_ref, over_ref, act_ref, g_ref):
    blocks, rows, width = x_ref.shape
    head, far_head = bh_ref[1:2], far_bh_ref[1:2]
    act, g = half_unit(x_ref, near_ref, bh_ref[0:1], head)
    far_act, far_g = half_unit(x_ref, far_ref, far_bh_ref[0:1], far_head)
    act_ref[...] = act
    g_ref[...] = g
    g, far_g = g.astype(BF16), far_g.astype(BF16)
    over_ref[0] = far_act.astype(BF16)
    over_ref[1] = far_g
    share = act * head + far_act * far_head
    cut = min(128, width)
    share = sum(share[:, i : i + cut] for i in range(0, width, cut))
    share = jnp.sum(jnp.transpose(share), axis=0, keepdims=True)
    high = share.astype(BF16).astype(F32)
    row = iota((EXTRA, rows), 0)
    extra = jnp.where(row == 0, high, jnp.where(row == 1, share - high, 0.0)).astype(BF16)
    for j in range(blocks):
        part = mm(g, near_ref[j], NT) + mm(far_g, far_ref[j], NT)
        msg_ref[j, pl.ds(0, rows), :] = part.astype(BF16)
        msg_ref[j, pl.ds(rows, EXTRA), pl.ds(0, rows)] = extra


def back_kernel(arms, bias_ref, got_ref, side_ref, pos_ref, slots_ref, resid_ref):
    blocks, rows, width = got_ref.shape
    rows = rows - EXTRA
    total = arms * SLOT
    preds, grads = [], []
    for half in range(2):
        extra = sum(got_ref[j, pl.ds(rows, EXTRA), pl.ds(0, rows)].astype(F32) for j in range(half, blocks, 2))
        preds.append(extra[0:1] + extra[1:2])
        grads.append(sum(got_ref[j, pl.ds(0, rows), :].astype(F32) for j in range(half, blocks, 2)))
    pred = jnp.concatenate(preds, axis=1) + bias_ref[0]
    resid = side_ref[1:2] * (pred - side_ref[0:1])
    resid_ref[...] = jnp.broadcast_to(resid, resid_ref.shape)
    grad = (jnp.concatenate(grads, axis=0) * column(resid)[:, 0:1]).astype(BF16)
    gather = ones_where(iota((2 * rows, total), 0) == pos_ref[0:1])
    pred_slot = mm(jnp.broadcast_to(pred, (8, 2 * rows)).astype(BF16), gather)
    same = iota((arms, total), 0) == iota((arms, total), 1) // SLOT
    spread = jnp.where(same, pred_slot[0:1], 0.0).astype(BF16)
    lane = ones_where(iota((width, total), 0) == iota((width, total), 1) % SLOT)
    pred_side = mm(spread, lane, NT).astype(BF16)
    slots_ref[...] = (mm(gather, grad, TN) + mm(side_rows(arms), pred_side)).astype(BF16)


def unpack_kernel(arms, slots_ref, aux_ref, grad_ref, pred_ref):
    total, width = slots_ref.shape
    rows = aux_ref.shape[1]
    slots = slots_ref[...]
    place = ones_where(iota((total, rows), 0) == aux_ref[0:1])
    grad_ref[...] = mm(place, slots, TN).astype(BF16)
    pred_side = mm(pick_side(arms), slots).astype(BF16)
    by_arm = mm(pred_side, ones_where(iota((width, rows), 0) == aux_ref[1:2]))
    hot = iota((arms, rows), 0) == aux_ref[2:3]
    pred_ref[...] = jnp.sum(jnp.where(hot, by_arm, 0.0), axis=0, keepdims=True).astype(BF16)


def grads_kernel(
    core_ref, x_ref, far_x_ref, act_ref, g_ref, over_ref, resid_ref, matrix_ref, bias_ref, head_ref, scalar_ref
):
    first = core_ref[0] == 0
    half = act_ref.shape[0]
    low, high = resid_ref[0:1, 0:half], resid_ref[0:1, half : 2 * half]
    scalar_ref[0] = jnp.sum(resid_ref[0:1])
    mine = column(jnp.where(first, low, high))[:, 0:1]
    other = column(jnp.where(first, high, low))[:, 0:1]
    near, far = g_ref[...] * mine, over_ref[1].astype(F32) * other
    bias_ref[...] = jnp.sum(near, axis=0, keepdims=True) + jnp.sum(far, axis=0, keepdims=True)
    head_ref[...] = jnp.sum(act_ref[...] * mine, axis=0, keepdims=True) + jnp.sum(
        over_ref[0].astype(F32) * other, axis=0, keepdims=True
    )
    near, far = near.astype(BF16), far.astype(BF16)
    for j in range(x_ref.shape[0]):
        matrix_ref[j] = mm(x_ref[j], near, TN) + mm(far_x_ref[j], far, TN)


def body(rep, arm_ids, outcome, weight, w_hidden, b_hidden, w_head, b_head):
    arms = lax.axis_size("dp")
    tower = lax.axis_size("tower")
    rows, width = rep.shape
    packed = 2 * rows
    total = arms * SLOT
    hidden = w_hidden.shape[2]
    core = (lax.axis_index("tower") % 2).astype(I32).reshape(1)

    def swap(value):
        return lax.ppermute(value, "tower", [(i, i ^ 1) for i in range(tower)])

    def exchange(slots):
        cut = slots.reshape(arms, SLOT, width)
        return lax.all_to_all(cut, "dp", split_axis=0, concat_axis=0, tiled=True).reshape(total, width)

    def spread(blocks):
        return lax.all_to_all(blocks, "tower", split_axis=0, concat_axis=0, tiled=True)

    meta = jnp.stack([arm_ids.astype(F32), outcome.astype(F32), weight.astype(F32)])
    slots, aux = call(
        functools.partial(pack_kernel, arms),
        (sds((total, width), BF16), sds((8, rows), I32)),
        spaces=[VMEM, ANY],
        scratch=[pltpu.VMEM((rows, width), BF16), pltpu.SemaphoreType.DMA],
        flops=2 * total * rows * width,
    )(meta, rep)
    arrived = exchange(slots)
    send, side, pos = call(
        functools.partial(compact_kernel, arms, packed),
        (sds((tower, rows, width), BF16), sds((8, packed), F32), sds((8, total), I32)),
        flops=2 * total * packed * width,
    )(arrived)
    matrix = w_hidden.reshape(tower, width, hidden)
    both = jnp.concatenate([b_hidden, w_head], axis=0)
    inputs = spread(send)
    far_matrix, far_both = swap(matrix), swap(both)
    msg, over, act, g = call(
        forward_kernel,
        (
            sds((tower, rows + EXTRA, width), BF16),
            sds((2, rows, hidden), BF16),
            sds((rows, hidden), F32),
            sds((rows, hidden), F32),
        ),
        flops=8 * rows * tower * width * hidden,
    )(inputs, matrix, far_matrix, both, far_both)
    got = spread(msg)
    msg, inputs2, over = lax.optimization_barrier((msg, inputs, over))
    far_inputs, far_over = swap(inputs2), swap(over)
    back_slots, resid = call(
        functools.partial(back_kernel, arms),
        (sds((total, width), BF16), sds((8, packed), F32)),
        spaces=[SMEM, VMEM, VMEM, VMEM],
        flops=2 * total * packed * width,
    )(b_head, got, side, pos)
    returned = exchange(back_slots)
    grad_matrix, grad_bias, grad_vector, grad_scalar = call(
        grads_kernel,
        (
            sds((tower, width, hidden), F32),
            sds((1, hidden), F32),
            sds((1, hidden), F32),
            sds((1,), F32),
        ),
        spaces=[SMEM] + [VMEM] * 6,
        outs=[VMEM, VMEM, VMEM, SMEM],
        flops=2 * packed * tower * width * hidden,
        nbytes=5 * 2**20,
    )(core, inputs, far_inputs, act, g, far_over, resid)
    grad_rep, predicted = call(
        functools.partial(unpack_kernel, arms),
        (sds((rows, width), BF16), sds((1, rows), BF16)),
        flops=2 * total * rows * width,
    )(returned, aux)
    return (
        grad_matrix.reshape(1, tower * width, hidden),
        grad_bias,
        grad_vector,
        grad_scalar,
        grad_rep,
        predicted.reshape(rows),
    )


def solution(mesh):
    return jax.shard_map(
        body,
        mesh=mesh,
        in_specs=(
            P("dp", "tower"),
            P("dp"),
            P("dp"),
            P("dp"),
            P("dp", None, "tower"),
            P("dp", "tower"),
            P("dp", "tower"),
            P("dp"),
        ),
        out_specs=(
            P("dp", None, "tower"),
            P("dp", "tower"),
            P("dp", "tower"),
            P("dp"),
            P("dp", "tower"),
            P("dp"),
        ),
        check_vma=False,
    )
```

time: 122 us -> 118 us (0.967)
  the two profiles are of different devices: /device:TPU:22 before, /device:TPU:16 now
where the time goes in v2:
time: 118 us
  waiting for transfers between devices  59.5 us (50%)
  starting transfers between devices  38.4 us (33%)
  Pallas kernels  12.6 us (11%)
  local copies, waits for them, and re-layouts  3.1 us (3%)
  other arithmetic  2.63 us (2%)
  between operations  1.43 us (1%)
    all_to_all x2, waiting for transfers between devices, exchange(): lax.all_to_all(cut, 'dp', split_axis=0, concat_axis=0, tiled=True)  30.7 us
    all_to_all x2, waiting for transfers between devices, spread(): lax.all_to_all(blocks, 'tower', split_axis=0, concat_axis=0, tiled=True)  26.4 us
    all_to_all x2, starting transfers between devices, exchange(): lax.all_to_all(cut, 'dp', split_axis=0, concat_axis=0, tiled=True)  21.8 us
    pallas_call x6, Pallas kernels, run(): pl.pallas_call(kernel, out_shape=out_shape, in_specs=[pl.BlockSpec(memory...  12.6 us
    ppermute x4, starting transfers between devices, swap(): return lax.ppermute(value, 'tower', [(i, i ^ 1) for i in range(tower)])  8.55 us
    all_to_all x2, starting transfers between devices, spread(): lax.all_to_all(blocks, 'tower', split_axis=0, concat_axis=0, tiled=True)  7.99 us
    unnamed x16, local copies, waits for them, and re-layouts  3.1 us
    ppermute x4, waiting for transfers between devices, swap(): return lax.ppermute(value, 'tower', [(i, i ^ 1) for i in range(tower)])  2.51 us
  transfers between devices with their start and end apart: 8, of which 6 were waited for; matrix products, arithmetic and copies ran while one was open for 0% of the time, Pallas kernels for 5%

profile of v2, /device:TPU:16, one launch (start us, length us, event | category | flops | bytes accessed | tf_op | source)
XLA Modules:
  0.0 117.7 jit_solution(17540657613313487841)
XLA Ops:
  0.6 0.8 convert_element_type.2
  2.7 0.9 copy-done.5
  3.6 2.2 %shard_map.127 = (bf16[1024,256]{1,0:T(8,128)(2,1)}, s32[8,256]{1,0:T(8,128)S(1)}) custom-call(f32[3,256]{1,0:T(4,128)S(1)} %pad_maximum_fusion.meta_ref, bf16[256,256]{1,0:T(8,128)(2,1)S(1)} %copy-done.5), custom_call_target="tpu_custom_call" | custom-call | flops 134217728 | tf_op jit(solution)/shard_map/pallas_call | solution.py:36
  5.8 16.5 %all-to-all-start = ((bf16[64,16,256]{2,1,0:T(8,128)(2,1)}), bf16[64,16,256]{2,1,0:T(8,128)(2,1)S(1)}, u32[]{:S(2)}, u32[]{:S(2)}) async-start(bf16[64,16,256]{2,1,0:T(8,128)(2,1)} %bitcast.4), calls=%async_computation | async-start | bytes 1048576 | tf_op jit(solution)/shard_map/all_to_all | solution.py:217
  22.3 1.9 %collective-permute-start = (bf16[8,256,256]{2,1,0:T(8,128)(2,1)S(1)}, bf16[8,256,256]{2,1,0:T(8,128)(2,1)}, u32[]{:S(2)}, u32[]{:S(2)}) collective-permute-start(bf16[8,256,256]{2,1,0:T(8,128)(2,1)S(1)} %bitcast.13), channel_id=1, source_target_pairs={{0,1},{1,0},{2,3},{3,2},{4,5},{5,4},{6,7},{7,6},{8,9},{9,8},{10,11... | collective-permute-start | bytes 3145736 | tf_op jit(solution)/shard_map/ppermute | solution.py:213
  24.3 17.5 %all-to-all-done = bf16[64,16,256]{2,1,0:T(8,128)(2,1)S(1)} async-done(((bf16[64,16,256]{2,1,0:T(8,128)(2,1)}), bf16[64,16,256]{2,1,0:T(8,128)(2,1)S(1)}, u32[]{:S(2)}, u32[]{:S(2)}) %all-to-all-start) | async-done | bytes 524320 | tf_op jit(solution)/shard_map/all_to_all | solution.py:217
  41.7 2.2 %shard_map.128 = (bf16[8,256,256]{2,1,0:T(8,128)(2,1)}, f32[8,512]{1,0:T(8,128)S(1)}, s32[8,1024]{1,0:T(8,128)S(1)}) custom-call(bf16[1024,256]{1,0:T(8,128)(2,1)S(1)} %bitcast.12), custom_call_target="tpu_custom_call" | custom-call | flops 268435456 | tf_op jit(solution)/shard_map/pallas_call | solution.py:36
  43.9 4.4 %all-to-all-start.1 = ((bf16[8,256,256]{2,1,0:T(8,128)(2,1)}), bf16[8,256,256]{2,1,0:T(8,128)(2,1)S(1)}, u32[]{:S(2)}, u32[]{:S(2)}) async-start(bf16[8,256,256]{2,1,0:T(8,128)(2,1)} %get-tuple-element.26), calls=%async_computation.1 | async-start | bytes 2097152 | tf_op jit(solution)/shard_map/all_to_all | solution.py:220
  48.4 2.4 %collective-permute-start.1 = (f32[2,256]{1,0:T(2,128)S(1)}, f32[2,256]{1,0:T(2,128)S(1)}, u32[]{:S(2)}, u32[]{:S(2)}) collective-permute-start(f32[2,256]{1,0:T(2,128)S(1)} %pad_maximum_fusion.1.bh_ref), channel_id=1, source_target_pairs={{0,1},{1,0},{2,3},{3,2},{4,5},{5,4},{6,7},{7,6},{8,9},{9,8},{10,11... | collective-permute-start | bytes 6152 | tf_op jit(solution)/shard_map/ppermute | solution.py:213
  50.8 0.8 collective-permute-done.1.far_bh_ref
  51.6 12.7 %all-to-all-done.1.x_ref = bf16[8,256,256]{2,1,0:T(8,128)(2,1)S(1)} async-done(((bf16[8,256,256]{2,1,0:T(8,128)(2,1)}), bf16[8,256,256]{2,1,0:T(8,128)(2,1)S(1)}, u32[]{:S(2)}, u32[]{:S(2)}) %all-to-all-start.1) | async-done | bytes 1048608 | tf_op jit(solution)/shard_map/all_to_all | solution.py:220
  64.3 3.7 %shard_map.129 = (bf16[8,272,256]{2,1,0:T(8,128)(2,1)}, bf16[2,256,256]{2,1,0:T(8,128)(2,1)S(1)}, f32[256,256]{1,0:T(8,128)S(1)}, f32[256,256]{1,0:T(8,128)S(1)}) custom-call(bf16[8,256,256]{2,1,0:T(8,128)(2,1)S(1)} %all-to-all-done.1.x_ref, bf16[8,256,256]{2,1,0:T(8,128)(2,1)S(1)} %bitcast.14, bf16[8,256,256]{2,1,0:T(8,128)(2,1)} %collective-permute-done.far_ref, ...), custom_call_target="tpu_custom_call" | custom-call | flops 1073741824 | tf_op jit(solution)/shard_map/pallas_call | solution.py:36
  68.7 0.7 copy-done.4
  69.4 3.6 %all-to-all-start.2 = ((bf16[8,272,256]{2,1,0:T(8,128)(2,1)}), bf16[8,272,256]{2,1,0:T(8,128)(2,1)S(1)}, u32[]{:S(2)}, u32[]{:S(2)}) async-start(bf16[8,272,256]{2,1,0:T(8,128)(2,1)} %get-tuple-element.27), calls=%async_computation.2 | async-start | bytes 2228224 | tf_op jit(solution)/shard_map/all_to_all | solution.py:220
  73.0 2.3 %collective-permute-start.2 = (bf16[8,256,256]{2,1,0:T(8,128)(2,1)S(1)}, bf16[8,256,256]{2,1,0:T(8,128)(2,1)S(1)}, u32[]{:S(2)}, u32[]{:S(2)}) collective-permute-start(bf16[8,256,256]{2,1,0:T(8,128)(2,1)S(1)} %all-to-all-done.1.x_ref), channel_id=1, source_target_pairs={{0,1},{1,0},{2,3},{3,2},{4,5},{5,4},{6,7},{7,6},{8,9},{9,8},{10,11... | collective-permute-start | bytes 3145736 | tf_op jit(solution)/shard_map/ppermute | solution.py:213
  76.0 13.6 %all-to-all-done.2.got_ref = bf16[8,272,256]{2,1,0:T(8,128)(2,1)S(1)} async-done(((bf16[8,272,256]{2,1,0:T(8,128)(2,1)}), bf16[8,272,256]{2,1,0:T(8,128)(2,1)S(1)}, u32[]{:S(2)}, u32[]{:S(2)}) %all-to-all-start.2) | async-done | bytes 1114144 | tf_op jit(solution)/shard_map/all_to_all | solution.py:220
  89.6 1.1 shard_map.130
  90.7 0.8 copy-done
  91.5 5.3 %all-to-all-start.3 = ((bf16[64,16,256]{2,1,0:T(8,128)(2,1)}), bf16[64,16,256]{2,1,0:T(8,128)(2,1)S(1)}, u32[]{:S(2)}, u32[]{:S(2)}) async-start(bf16[64,16,256]{2,1,0:T(8,128)(2,1)} %bitcast.11), calls=%async_computation.3 | async-start | bytes 1048576 | tf_op jit(solution)/shard_map/all_to_all | solution.py:217
  96.8 1.9 %collective-permute-start.3 = (bf16[2,256,256]{2,1,0:T(8,128)(2,1)}, bf16[2,256,256]{2,1,0:T(8,128)(2,1)S(1)}, u32[]{:S(2)}, u32[]{:S(2)}) collective-permute-start(bf16[2,256,256]{2,1,0:T(8,128)(2,1)} %copy-done.4), channel_id=1, source_target_pairs={{0,1},{1,0},{2,3},{3,2},{4,5},{5,4},{6,7},{7,6},{8,9},{9,8},{10,11... | collective-permute-start | bytes 786440 | tf_op jit(solution)/shard_map/ppermute | solution.py:213
  98.8 1.7 %collective-permute-done.3.over_ref = bf16[2,256,256]{2,1,0:T(8,128)(2,1)S(1)} collective-permute-done((bf16[2,256,256]{2,1,0:T(8,128)(2,1)}, bf16[2,256,256]{2,1,0:T(8,128)(2,1)S(1)}, u32[]{:S(2)}, u32[]{:S(2)}) %collective-permute-start.3) | collective-permute-done | bytes 262176 | tf_op jit(solution)/shard_map/ppermute | solution.py:213
  100.5 2.4 %shard_map.131 = (f32[8,256,256]{2,1,0:T(8,128)}, f32[1,256]{1,0:T(1,128)}, f32[1,256]{1,0:T(1,128)}, f32[1]{0:T(128)}) custom-call(s32[1]{0:T(128)} %bitcast.core_ref, bf16[8,256,256]{2,1,0:T(8,128)(2,1)S(1)} %all-to-all-done.1.x_ref, bf16[8,256,256]{2,1,0:T(8,128)(2,1)S(1)} %collective-permute-done.2.far_x_ref, f32[256,256]{1,0:T(8,128)S(1)} %get-tuple-element.30.act_ref, ...), custom_call_target="tpu_custom_call" | custom-call | flops 536870912 | bytes 5242880 | tf_op jit(solution)/shard_map/pallas_call | solution.py:36
  102.9 13.2 %all-to-all-done.3 = bf16[64,16,256]{2,1,0:T(8,128)(2,1)S(1)} async-done(((bf16[64,16,256]{2,1,0:T(8,128)(2,1)}), bf16[64,16,256]{2,1,0:T(8,128)(2,1)S(1)}, u32[]{:S(2)}, u32[]{:S(2)}) %all-to-all-start.3) | async-done | bytes 524320 | tf_op jit(solution)/shard_map/all_to_all | solution.py:217
  116.1 1.1 shard_map.132
  (20 shorter events, 2.6 us)
Async XLA Ops:
  0.6 21.7 %copy-start.3 = (bf16[1,2048,256]{2,1,0:T(8,128)(2,1)S(1)}, bf16[1,2048,256]{2,1,0:T(8,128)(2,1)}, u32[]{:S(2)}) copy-start(bf16[1,2048,256]{2,1,0:T(8,128)(2,1)} %param.12) | copy-start | bytes 3145732
  2.7 0.9 copy-start.5
  5.8 35.9 %all-to-all-start = ((bf16[64,16,256]{2,1,0:T(8,128)(2,1)}), bf16[64,16,256]{2,1,0:T(8,128)(2,1)S(1)}, u32[]{:S(2)}, u32[]{:S(2)}) async-start(bf16[64,16,256]{2,1,0:T(8,128)(2,1)} %bitcast.4), calls=%async_computation | async-start | bytes 1048576 | tf_op jit(solution)/shard_map/all_to_all | solution.py:217
  22.3 29.3 %collective-permute-start = (bf16[8,256,256]{2,1,0:T(8,128)(2,1)S(1)}, bf16[8,256,256]{2,1,0:T(8,128)(2,1)}, u32[]{:S(2)}, u32[]{:S(2)}) collective-permute-start(bf16[8,256,256]{2,1,0:T(8,128)(2,1)S(1)} %bitcast.13), channel_id=1, source_target_pairs={{0,1},{1,0},{2,3},{3,2},{4,5},{5,4},{6,7},{7,6},{8,9},{9,8},{10,11... | collective-permute-start | bytes 3145736 | tf_op jit(solution)/shard_map/ppermute | solution.py:213
  43.9 4.4 %copy-start.6 = (f32[1,256]{1,0:T(1,128)S(1)}, f32[1,256]{1,0:T(1,128)}, u32[]{:S(2)}) copy-start(f32[1,256]{1,0:T(1,128)} %param.14) | copy-start | bytes 3076
  43.9 4.4 %copy-start.7 = (f32[1,256]{1,0:T(1,128)S(1)}, f32[1,256]{1,0:T(1,128)}, u32[]{:S(2)}) copy-start(f32[1,256]{1,0:T(1,128)} %param.13) | copy-start | bytes 3076
  43.9 20.4 %all-to-all-start.1 = ((bf16[8,256,256]{2,1,0:T(8,128)(2,1)}), bf16[8,256,256]{2,1,0:T(8,128)(2,1)S(1)}, u32[]{:S(2)}, u32[]{:S(2)}) async-start(bf16[8,256,256]{2,1,0:T(8,128)(2,1)} %get-tuple-element.26), calls=%async_computation.1 | async-start | bytes 2097152 | tf_op jit(solution)/shard_map/all_to_all | solution.py:220
  48.4 3.2 %collective-permute-start.1 = (f32[2,256]{1,0:T(2,128)S(1)}, f32[2,256]{1,0:T(2,128)S(1)}, u32[]{:S(2)}, u32[]{:S(2)}) collective-permute-start(f32[2,256]{1,0:T(2,128)S(1)} %pad_maximum_fusion.1.bh_ref), channel_id=1, source_target_pairs={{0,1},{1,0},{2,3},{3,2},{4,5},{5,4},{6,7},{7,6},{8,9},{9,8},{10,11... | collective-permute-start | bytes 6152 | tf_op jit(solution)/shard_map/ppermute | solution.py:213
  68.0 0.7 copy-start.1
  68.7 0.7 copy-start.4
  69.4 20.2 %all-to-all-start.2 = ((bf16[8,272,256]{2,1,0:T(8,128)(2,1)}), bf16[8,272,256]{2,1,0:T(8,128)(2,1)S(1)}, u32[]{:S(2)}, u32[]{:S(2)}) async-start(bf16[8,272,256]{2,1,0:T(8,128)(2,1)} %get-tuple-element.27), calls=%async_computation.2 | async-start | bytes 2228224 | tf_op jit(solution)/shard_map/all_to_all | solution.py:220
  73.0 27.5 %collective-permute-start.2 = (bf16[8,256,256]{2,1,0:T(8,128)(2,1)S(1)}, bf16[8,256,256]{2,1,0:T(8,128)(2,1)S(1)}, u32[]{:S(2)}, u32[]{:S(2)}) collective-permute-start(bf16[8,256,256]{2,1,0:T(8,128)(2,1)S(1)} %all-to-all-done.1.x_ref), channel_id=1, source_target_pairs={{0,1},{1,0},{2,3},{3,2},{4,5},{5,4},{6,7},{7,6},{8,9},{9,8},{10,11... | collective-permute-start | bytes 3145736 | tf_op jit(solution)/shard_map/ppermute | solution.py:213
  90.7 0.8 copy-start
  91.5 9.0 %copy-start.2 = (f32[256,256]{1,0:T(8,128)S(1)}, f32[256,256]{1,0:T(8,128)}, u32[]{:S(2)}) copy-start(f32[256,256]{1,0:T(8,128)} %copy-done.1) | copy-start | bytes 786436
  91.5 24.6 %all-to-all-start.3 = ((bf16[64,16,256]{2,1,0:T(8,128)(2,1)}), bf16[64,16,256]{2,1,0:T(8,128)(2,1)S(1)}, u32[]{:S(2)}, u32[]{:S(2)}) async-start(bf16[64,16,256]{2,1,0:T(8,128)(2,1)} %bitcast.11), calls=%async_computation.3 | async-start | bytes 1048576 | tf_op jit(solution)/shard_map/all_to_all | solution.py:217
  96.8 3.6 %collective-permute-start.3 = (bf16[2,256,256]{2,1,0:T(8,128)(2,1)}, bf16[2,256,256]{2,1,0:T(8,128)(2,1)S(1)}, u32[]{:S(2)}, u32[]{:S(2)}) collective-permute-start(bf16[2,256,256]{2,1,0:T(8,128)(2,1)} %copy-done.4), channel_id=1, source_target_pairs={{0,1},{1,0},{2,3},{3,2},{4,5},{5,4},{6,7},{7,6},{8,9},{9,8},{10,11... | collective-permute-start | bytes 786440 | tf_op jit(solution)/shard_map/ppermute | solution.py:213

commit v3 on v2

v3 whole, which is shorter than its diff:
```python
import functools

import jax
import jax.numpy as jnp
from jax import lax
from jax.experimental import pallas as pl
from jax.experimental.pallas import tpu as pltpu
from jax.sharding import PartitionSpec as P

F32, BF16, I32 = jnp.float32, jnp.bfloat16, jnp.int32
SLOT = 16
SIDE = 14
EXTRA = 16
INTERPRET = False
VMEM, SMEM, HBM = pltpu.VMEM, pltpu.SMEM, pltpu.HBM
DMA = pltpu.SemaphoreType.DMA
LANES = 128
PARTS = 4

NN = (((1,), (0,)), ((), ()))
NT = (((1,), (1,)), ((), ()))
TN = (((0,), (0,)), ((), ()))


def mm(a, b, dims=NN):
    return lax.dot_general(a, b, dims, preferred_element_type=F32)


def iota(shape, dim):
    return lax.broadcasted_iota(I32, shape, dim)


def ones_where(mask):
    return jnp.where(mask, 1.0, 0.0).astype(BF16)


def call(kernel, out_shape, ins=None, outs=None, scratch=(), flops=0, nbytes=0, vmem=32):
    kinds = outs or [VMEM] * len(out_shape)

    def run(*args):
        spaces = ins or [VMEM] * len(args)
        args = [pltpu.with_memory_space_constraint(a, HBM) if m is HBM else a for a, m in zip(args, spaces)]
        return pl.pallas_call(
            kernel,
            out_shape=[HBM(o.shape, o.dtype) if m is HBM else o for o, m in zip(out_shape, kinds)],
            in_specs=[pl.BlockSpec(memory_space=m) for m in spaces],
            out_specs=[pl.BlockSpec(memory_space=m) for m in kinds],
            scratch_shapes=list(scratch),
            compiler_params=pltpu.CompilerParams(vmem_limit_bytes=vmem * 2**20),
            cost_estimate=pl.CostEstimate(flops=flops, bytes_accessed=nbytes, transcendentals=0),
            interpret=INTERPRET,
        )(*args)

    return run


def sds(shape, dtype):
    return jax.ShapeDtypeStruct(shape, dtype)


def pick_side(arms):
    shape = (arms, arms * SLOT)
    return ones_where(iota(shape, 1) == iota(shape, 0) * SLOT + SIDE)


def column(row):
    return jnp.transpose(jnp.broadcast_to(row, (LANES, row.shape[1])))


def pack_kernel(
    arms, ids_hbm, outcome_hbm, weight_hbm, rep_hbm, slots_hbm, aux_ref,
    ids_ref, outcome_ref, weight_ref, rep_ref, slots_ref, in_sem, out_sem,
):
    pairs = ((ids_hbm, ids_ref), (outcome_hbm, outcome_ref), (weight_hbm, weight_ref), (rep_hbm, rep_ref))
    loads = [pltpu.make_async_copy(a, b, in_sem.at[i]) for i, (a, b) in enumerate(pairs)]
    for load in loads:
        load.start()
    rows, width = rep_ref.shape
    earlier = ones_where(iota((rows, rows), 0) < iota((rows, rows), 1))
    loads[0].wait()
    ids = ids_ref[...]
    hot = iota((arms, rows), 0) == ids
    hot_half = ones_where(hot)
    counts = mm(hot_half, earlier)
    rank = jnp.sum(jnp.where(hot, counts, 0.0), axis=0, keepdims=True).astype(I32)
    slot = ids * SLOT + rank
    row8 = iota((8, rows), 0)
    aux_ref[...] = jnp.where(row8 == 0, slot, jnp.where(row8 == 1, rank, ids))
    lane = iota((width, rows), 0)
    loads[1].wait()
    loads[2].wait()
    outcome = outcome_ref[...].astype(F32).reshape(1, rows)
    weight = weight_ref[...].astype(F32).reshape(1, rows)
    side_t = jnp.where(lane == rank, outcome, 0.0) + jnp.where(lane == rank + SLOT, weight, 0.0)
    side = mm(hot_half, side_t.astype(BF16), NT).astype(BF16)
    loads[3].wait()
    rep = rep_ref[...]
    stores = []
    part = arms * SLOT // PARTS
    for i in range(PARTS):
        place = ones_where(iota((part, rows), 0) + i * part == slot)
        mark = ones_where(iota((part, arms), 0) + i * part == iota((part, arms), 1) * SLOT + SIDE)
        cut = pl.ds(i * part, part)
        slots_ref[cut, :] = (mm(place, rep) + mm(mark, side)).astype(BF16)
        stores.append(pltpu.make_async_copy(slots_ref.at[cut], slots_hbm.at[cut], out_sem.at[i]))
        stores[-1].start()
    for store in stores:
        store.wait()


def side_of(slots, arms):
    return mm(pick_side(arms), slots)


def compact_kernel(arms, packed, slots_ref, send_hbm, pos_ref, side_ref, rows_ref, sem):
    total, width = slots_ref.shape
    slots = slots_ref[...]
    side = side_of(slots, arms)
    side_ref[...] = side.astype(BF16)
    lane8 = iota((8, width), 1)
    weight_lanes = ones_where((lane8 >= SLOT) & (lane8 < 2 * SLOT))
    counts = mm(weight_lanes, ones_where(side > 0.0), NT).astype(BF16)
    source, owner = iota((arms, total), 0), iota((arms, total), 1) // SLOT
    start = mm(counts, ones_where(source < owner))
    count = mm(counts, ones_where(source == owner))
    depth = iota((8, total), 1) % SLOT
    pos = jnp.where(depth < count.astype(I32), start.astype(I32) + depth, 2 * packed)
    pos_ref[...] = pos
    half = packed // 2
    blocks = send_hbm.shape[0]
    stores = []
    for h in range(2):
        gather = ones_where(iota((half, total), 0) + h * half == pos[0:1])
        rows_ref[h] = mm(gather, slots).astype(BF16)
        for d in range(h, blocks, 2):
            stores.append(pltpu.make_async_copy(rows_ref.at[h], send_hbm.at[d], sem.at[d]))
            stores[-1].start()
    for store in stores:
        store.wait()


def prepare_kernel(arms, packed, given_ref, pos_ref, side_ref):
    total, width = arms * SLOT, given_ref.shape[1]
    side = given_ref[...]
    gather = ones_where(iota((packed, total), 0) == pos_ref[0:1])
    same = iota((arms, total), 0) == iota((arms, total), 1) // SLOT
    lane, place = iota((width, total), 0), iota((width, total), 1) % SLOT
    target = mm(side, ones_where(lane == place))
    weight = mm(side, ones_where(lane == place + SLOT))
    target = jnp.sum(jnp.where(same, target, 0.0), axis=0, keepdims=True)
    weight = jnp.sum(jnp.where(same, weight, 0.0), axis=0, keepdims=True)
    both = jnp.where(iota((8, total), 0) == 0, target, weight)
    side_ref[...] = mm(both.astype(BF16), gather, NT)


def unit(pre, head):
    sig = jax.nn.sigmoid(pre)
    return pre * sig, head * sig * (1.0 + pre * (1.0 - sig))


def forward_kernel(
    x_ref, near_ref, far_hbm, bh_ref, far_bh_ref, msg_hbm, over_hbm, act_hbm, g_hbm,
    far_ref, msg_ref, over_ref, act_ref, g_ref, in_sem, msg_sem, out_sem,
):
    blocks, rows, width = x_ref.shape
    loads = [pltpu.make_async_copy(far_hbm.at[j], far_ref.at[j], in_sem.at[j]) for j in range(blocks)]
    for load in loads:
        load.start()
    head, far_head = bh_ref[1:2], far_bh_ref[1:2]
    pre = sum(mm(x_ref[j], near_ref[j]) for j in range(blocks)) + bh_ref[0:1]
    act, g = unit(pre, head)
    act_ref[...] = act
    g_ref[...] = g
    g = g.astype(BF16)
    pre = jnp.broadcast_to(far_bh_ref[0:1], pre.shape)
    for j in range(blocks):
        loads[j].wait()
        pre += mm(x_ref[j], far_ref[j])
    far_act, far_g = unit(pre, far_head)
    far_g = far_g.astype(BF16)
    over_ref[0] = far_act.astype(BF16)
    over_ref[1] = far_g
    stores = [
        pltpu.make_async_copy(a, b, out_sem.at[i])
        for i, (a, b) in enumerate(((act_ref, act_hbm), (g_ref, g_hbm), (over_ref, over_hbm)))
    ]
    share = act * head + far_act * far_head
    cut = min(LANES, width)
    share = sum(share[:, i : i + cut] for i in range(0, width, cut))
    share = jnp.sum(jnp.transpose(share), axis=0, keepdims=True)
    high = share.astype(BF16).astype(F32)
    row = iota((EXTRA, rows), 0)
    extra = jnp.where(row == 0, high, jnp.where(row == 1, share - high, 0.0)).astype(BF16)
    for j in range(blocks):
        part = mm(g, near_ref[j], NT) + mm(far_g, far_ref[j], NT)
        msg_ref[j, pl.ds(0, rows), :] = part.astype(BF16)
        msg_ref[j, pl.ds(rows, EXTRA), pl.ds(0, rows)] = extra
        stores.append(pltpu.make_async_copy(msg_ref.at[j], msg_hbm.at[j], msg_sem.at[j]))
        stores[-1].start()
    for store in stores[:3]:
        store.start()
    for store in stores:
        store.wait()


def back_kernel(arms, bias_ref, got_ref, side_ref, pos_ref, slots_hbm, resid_ref, slots_ref, sem):
    blocks, rows, width = got_ref.shape
    rows = rows - EXTRA
    total = arms * SLOT
    preds, grads = [], []
    for half in range(2):
        extra = sum(got_ref[j, pl.ds(rows, EXTRA), pl.ds(0, rows)].astype(F32) for j in range(half, blocks, 2))
        preds.append(extra[0:1] + extra[1:2])
        grads.append(sum(got_ref[j, pl.ds(0, rows), :].astype(F32) for j in range(half, blocks, 2)))
    pred = jnp.concatenate(preds, axis=1) + bias_ref[0]
    resid = side_ref[1:2] * (pred - side_ref[0:1])
    resid_ref[...] = jnp.broadcast_to(resid, resid_ref.shape)
    grad = (jnp.concatenate(grads, axis=0) * column(resid)[:, 0:1]).astype(BF16)
    pred = jnp.broadcast_to(pred, (8, 2 * rows)).astype(BF16)
    stores = []
    part = total // PARTS
    for i in range(PARTS):
        cut = pl.ds(i * part, part)
        gather = ones_where(iota((2 * rows, part), 0) == pos_ref[0:1, i * part : (i + 1) * part])
        pred_slot = mm(pred, gather)[0:1]
        row, slot = iota((part, part), 0), iota((part, part), 1)
        spread = jnp.where((row % SLOT == SIDE) & (row // SLOT == slot // SLOT), pred_slot, 0.0).astype(BF16)
        lane = ones_where(iota((width, part), 0) == iota((width, part), 1) % SLOT)
        slots_ref[cut, :] = (mm(gather, grad, TN) + mm(spread, lane, NT)).astype(BF16)
        stores.append(pltpu.make_async_copy(slots_ref.at[cut], slots_hbm.at[cut], sem.at[i]))
        stores[-1].start()
    for store in stores:
        store.wait()


def unpack_kernel(arms, slots_ref, aux_ref, grad_ref, pred_ref):
    total, width = slots_ref.shape
    rows = aux_ref.shape[1]
    slots = slots_ref[...]
    place = ones_where(iota((total, rows), 0) == aux_ref[0:1])
    grad_ref[...] = mm(place, slots, TN).astype(BF16)
    pred_side = side_of(slots, arms).astype(BF16)
    by_arm = mm(pred_side, ones_where(iota((width, rows), 0) == aux_ref[1:2]))
    hot = iota((arms, rows), 0) == aux_ref[2:3]
    pred = jnp.sum(jnp.where(hot, by_arm, 0.0), axis=0, keepdims=True)
    pred_ref[...] = pred.reshape(rows).astype(BF16)


def grads_kernel(
    core_ref, x_ref, far_x_ref, act_ref, g_ref, over_ref, resid_ref, matrix_ref, bias_ref, head_ref, scalar_ref
):
    first = core_ref[0] == 0
    half = act_ref.shape[0]
    low, high = resid_ref[0:1, 0:half], resid_ref[0:1, half : 2 * half]
    scalar_ref[0] = jnp.sum(resid_ref[0:1])
    mine = column(jnp.where(first, low, high))[:, 0:1]
    other = column(jnp.where(first, high, low))[:, 0:1]
    near, far = g_ref[...] * mine, over_ref[1].astype(F32) * other
    bias_ref[...] = jnp.sum(near, axis=0, keepdims=True) + jnp.sum(far, axis=0, keepdims=True)
    head_ref[...] = jnp.sum(act_ref[...] * mine, axis=0, keepdims=True) + jnp.sum(
        over_ref[0].astype(F32) * other, axis=0, keepdims=True
    )
    near, far = near.astype(BF16), far.astype(BF16)
    for j in range(x_ref.shape[0]):
        matrix_ref[j] = mm(x_ref[j], near, TN) + mm(far_x_ref[j], far, TN)


def body(rep, arm_ids, outcome, weight, w_hidden, b_hidden, w_head, b_head):
    arms = lax.axis_size("dp")
    tower = lax.axis_size("tower")
    rows, width = rep.shape
    packed = 2 * rows
    total = arms * SLOT
    hidden = w_hidden.shape[2]
    core = (lax.axis_index("tower") % 2).astype(I32).reshape(1)

    def swap(value):
        return lax.ppermute(value, "tower", [(i, i ^ 1) for i in range(tower)])

    def exchange(slots):
        cut = slots.reshape(arms, SLOT, width)
        return lax.all_to_all(cut, "dp", split_axis=0, concat_axis=0, tiled=True).reshape(total, width)

    def spread(blocks):
        return lax.all_to_all(blocks, "tower", split_axis=0, concat_axis=0, tiled=True)

    slots, aux = call(
        functools.partial(pack_kernel, arms),
        (sds((total, width), BF16), sds((8, rows), I32)),
        ins=[HBM] * 4,
        outs=[HBM, VMEM],
        scratch=[
            VMEM((1, rows), I32), VMEM((rows,), BF16), VMEM((rows,), BF16), VMEM((rows, width), BF16),
            VMEM((total, width), BF16), DMA((4,)), DMA((PARTS,)),
        ],
        flops=2 * total * rows * width,
    )(arm_ids.reshape(1, rows), outcome, weight, rep)
    arrived = exchange(slots)
    send, pos, given = call(
        functools.partial(compact_kernel, arms, packed),
        (sds((tower, rows, width), BF16), sds((8, total), I32), sds((arms, width), BF16)),
        outs=[HBM, VMEM, VMEM],
        scratch=[VMEM((2, rows, width), BF16), DMA((tower,))],
        flops=2 * total * packed * width,
    )(arrived)
    matrix = w_hidden.reshape(tower, width, hidden)
    both = jnp.concatenate([b_hidden, w_head], axis=0)
    inputs = spread(send)
    far_matrix, far_both = swap(matrix), swap(both)
    (side,) = call(
        functools.partial(prepare_kernel, arms, packed),
        (sds((8, packed), F32),),
        flops=4 * total * packed * arms,
    )(given, pos)
    msg, over, act, g = call(
        forward_kernel,
        (
            sds((tower, rows + EXTRA, width), BF16),
            sds((2, rows, hidden), BF16),
            sds((rows, hidden), F32),
            sds((rows, hidden), F32),
        ),
        ins=[VMEM, VMEM, HBM, VMEM, VMEM],
        outs=[HBM] * 4,
        scratch=[
            VMEM((tower, width, hidden), BF16), VMEM((tower, rows + EXTRA, width), BF16),
            VMEM((2, rows, hidden), BF16), VMEM((rows, hidden), F32), VMEM((rows, hidden), F32),
            DMA((tower,)), DMA((tower,)), DMA((3,)),
        ],
        flops=8 * rows * tower * width * hidden,
    )(inputs, matrix, far_matrix, both, far_both)
    got = spread(msg)
    msg, inputs2, over = lax.optimization_barrier((msg, inputs, over))
    far_inputs, far_over = swap(inputs2), swap(over)
    back_slots, resid = call(
        functools.partial(back_kernel, arms),
        (sds((total, width), BF16), sds((8, packed), F32)),
        ins=[SMEM, VMEM, VMEM, VMEM],
        outs=[HBM, VMEM],
        scratch=[VMEM((total, width), BF16), DMA((PARTS,))],
        flops=2 * total * packed * width,
    )(b_head, got, side, pos)
    returned = exchange(back_slots)
    grad_matrix, grad_bias, grad_vector, grad_scalar = call(
        grads_kernel,
        (
            sds((tower, width, hidden), F32),
            sds((1, hidden), F32),
            sds((1, hidden), F32),
            sds((1,), F32),
        ),
        ins=[SMEM] + [VMEM] * 6,
        outs=[VMEM, VMEM, VMEM, SMEM],
        flops=2 * packed * tower * width * hidden,
        nbytes=5 * 2**20,
    )(core, inputs, far_inputs, act, g, far_over, resid)
    grad_rep, predicted = call(
        functools.partial(unpack_kernel, arms),
        (sds((rows, width), BF16), sds((rows,), BF16)),
        flops=2 * total * rows * width,
    )(returned, aux)
    return (
        grad_matrix.reshape(1, tower * width, hidden),
        grad_bias,
        grad_vector,
        grad_scalar,
        grad_rep,
        predicted,
    )


def solution(mesh):
    return jax.shard_map(
        body,
        mesh=mesh,
        in_specs=(
            P("dp", "tower"),
            P("dp"),
            P("dp"),
            P("dp"),
            P("dp", None, "tower"),
            P("dp", "tower"),
            P("dp", "tower"),
            P("dp"),
        ),
        out_specs=(
            P("dp", None, "tower"),
            P("dp", "tower"),
            P("dp", "tower"),
            P("dp"),
            P("dp", "tower"),
            P("dp"),
        ),
        check_vma=False,
    )
```

time: 118 us -> 113 us (0.958)
  local copies, waits for them, and re-layouts: 3.1 us -> 0.03 us
  other arithmetic: 2.63 us -> 0.01 us
    unnamed x16 -> x12, local copies, waits for them, and re-layouts: 3.1 us -> 0.03 us
    another operation x3 -> x0, other arithmetic: 1.32 us -> none  [body(): jnp.stack([arm_ids.astype(F32), outcome.astype(F32), weight.astype(F32)])]
    pallas_call x6 -> x7, Pallas kernels: 12.6 us -> 13.5 us  [run(): pl.pallas_call(kernel, out_shape=[HBM(o.shape, o.dtype) if m is HBM else...]
  transfers between devices with their start and end apart: 8 -> 8, of which waited for: 6 -> 6; matrix products, arithmetic and copies ran while one was open for 0% -> 0% of each run, Pallas kernels for 5% -> 6%
where the time goes in v3:
time: 113 us; the launch traced here: 112 us
  waiting for transfers between devices  59 us (52%)
  starting transfers between devices  38.3 us (34%)
  Pallas kernels  13.5 us (12%)
  between operations  1.45 us (1%)
    all_to_all x2, waiting for transfers between devices, exchange(): lax.all_to_all(cut, 'dp', split_axis=0, concat_axis=0, tiled=True)  30.7 us
    all_to_all x2, waiting for transfers between devices, spread(): lax.all_to_all(blocks, 'tower', split_axis=0, concat_axis=0, tiled=True)  25.8 us
    all_to_all x2, starting transfers between devices, exchange(): lax.all_to_all(cut, 'dp', split_axis=0, concat_axis=0, tiled=True)  21.8 us
    pallas_call x7, Pallas kernels, run(): pl.pallas_call(kernel, out_shape=[HBM(o.shape, o.dtype) if m is HBM else...  13.5 us
    ppermute x4, starting transfers between devices, swap(): return lax.ppermute(value, 'tower', [(i, i ^ 1) for i in range(tower)])  8.55 us
    all_to_all x2, starting transfers between devices, spread(): lax.all_to_all(blocks, 'tower', split_axis=0, concat_axis=0, tiled=True)  7.89 us
    ppermute x4, waiting for transfers between devices, swap(): return lax.ppermute(value, 'tower', [(i, i ^ 1) for i in range(tower)])  2.51 us
  transfers between devices with their start and end apart: 8, of which 6 were waited for; matrix products, arithmetic and copies ran while one was open for 0% of the time, Pallas kernels for 6%

profile of v3, /device:TPU:16, one launch (start us, length us, event | category | flops | bytes accessed | tf_op | source)
XLA Modules:
  0.0 112.3 jit_solution(877911585522921900)
XLA Ops:
  0.6 2.4 %shard_map.127 = (bf16[1024,256]{1,0:T(8,128)(2,1)}, s32[8,256]{1,0:T(8,128)S(1)}) custom-call(s32[1,256]{1,0:T(1,128)} %bitcast.15, bf16[256]{0:T(256)(128)(2,1)} %outcome_hbm.1, bf16[256]{0:T(256)(128)(2,1)} %weight_hbm.1, bf16[256,256]{1,0:T(8,128)(2,1)} %rep_hbm.1), custom_call_target="tpu_custom_call" | custom-call | flops 134217728 | tf_op jit(solution)/shard_map/pallas_call | solution.py:43
  3.0 16.5 %all-to-all-start = ((bf16[64,16,256]{2,1,0:T(8,128)(2,1)}), bf16[64,16,256]{2,1,0:T(8,128)(2,1)S(1)}, u32[]{:S(2)}, u32[]{:S(2)}) async-start(bf16[64,16,256]{2,1,0:T(8,128)(2,1)} %bitcast.13), calls=%async_computation | async-start | bytes 1048576 | tf_op jit(solution)/shard_map/all_to_all | solution.py:282
  19.5 1.9 %collective-permute-start = (bf16[8,256,256]{2,1,0:T(8,128)(2,1)S(1)}, bf16[8,256,256]{2,1,0:T(8,128)(2,1)S(1)}, u32[]{:S(2)}, u32[]{:S(2)}) collective-permute-start(bf16[8,256,256]{2,1,0:T(8,128)(2,1)S(1)} %bitcast.10), channel_id=1, source_target_pairs={{0,1},{1,0},{2,3},{3,2},{4,5},{5,4},{6,7},{7,6},{8,9},{9,8},{10,11... | collective-permute-start | bytes 3145736 | tf_op jit(solution)/shard_map/ppermute | solution.py:278
  21.4 17.5 %all-to-all-done = bf16[64,16,256]{2,1,0:T(8,128)(2,1)S(1)} async-done(((bf16[64,16,256]{2,1,0:T(8,128)(2,1)}), bf16[64,16,256]{2,1,0:T(8,128)(2,1)S(1)}, u32[]{:S(2)}, u32[]{:S(2)}) %all-to-all-start) | async-done | bytes 524320 | tf_op jit(solution)/shard_map/all_to_all | solution.py:282
  38.9 1.9 %shard_map.128 = (bf16[8,256,256]{2,1,0:T(8,128)(2,1)}, s32[8,1024]{1,0:T(8,128)S(1)}, bf16[64,256]{1,0:T(8,128)(2,1)S(1)}) custom-call(bf16[1024,256]{1,0:T(8,128)(2,1)S(1)} %bitcast.9), custom_call_target="tpu_custom_call" | custom-call | flops 268435456 | tf_op jit(solution)/shard_map/pallas_call | solution.py:43
  40.8 0.0 copy-start.3
  40.9 0.0 copy-start.4
  40.9 4.3 %all-to-all-start.1 = ((bf16[8,256,256]{2,1,0:T(8,128)(2,1)}), bf16[8,256,256]{2,1,0:T(8,128)(2,1)S(1)}, u32[]{:S(2)}, u32[]{:S(2)}) async-start(bf16[8,256,256]{2,1,0:T(8,128)(2,1)} %get-tuple-element.26), calls=%async_computation.1 | async-start | bytes 2097152 | tf_op jit(solution)/shard_map/all_to_all | solution.py:285
  45.2 2.4 %collective-permute-start.1 = (f32[2,256]{1,0:T(2,128)S(1)}, f32[2,256]{1,0:T(2,128)S(1)}, u32[]{:S(2)}, u32[]{:S(2)}) collective-permute-start(f32[2,256]{1,0:T(2,128)S(1)} %pad_maximum_fusion.bh_ref), channel_id=1, source_target_pairs={{0,1},{1,0},{2,3},{3,2},{4,5},{5,4},{6,7},{7,6},{8,9},{9,8},{10,11... | collective-permute-start | bytes 6152 | tf_op jit(solution)/shard_map/ppermute | solution.py:278
  47.6 0.8 collective-permute-done.1.far_bh_ref
  48.4 0.0 collective-permute-done.far_hbm
  48.4 12.7 %all-to-all-done.1.x_ref = bf16[8,256,256]{2,1,0:T(8,128)(2,1)S(1)} async-done(((bf16[8,256,256]{2,1,0:T(8,128)(2,1)}), bf16[8,256,256]{2,1,0:T(8,128)(2,1)S(1)}, u32[]{:S(2)}, u32[]{:S(2)}) %all-to-all-start.1) | async-done | bytes 1048608 | tf_op jit(solution)/shard_map/all_to_all | solution.py:285
  61.2 3.4 %shard_map.129 = (bf16[8,272,256]{2,1,0:T(8,128)(2,1)}, bf16[2,256,256]{2,1,0:T(8,128)(2,1)}, f32[256,256]{1,0:T(8,128)}, f32[256,256]{1,0:T(8,128)}) custom-call(bf16[8,256,256]{2,1,0:T(8,128)(2,1)S(1)} %all-to-all-done.1.x_ref, bf16[8,256,256]{2,1,0:T(8,128)(2,1)S(1)} %bitcast.11, bf16[8,256,256]{2,1,0:T(8,128)(2,1)} %copy-done.5, ...), custom_call_target="tpu_custom_call" | custom-call | flops 1073741824 | tf_op jit(solution)/shard_map/pallas_call | solution.py:43
  64.6 3.6 %all-to-all-start.2 = ((bf16[8,272,256]{2,1,0:T(8,128)(2,1)}), bf16[8,272,256]{2,1,0:T(8,128)(2,1)S(1)}, u32[]{:S(2)}, u32[]{:S(2)}) async-start(bf16[8,272,256]{2,1,0:T(8,128)(2,1)} %get-tuple-element.27), calls=%async_computation.2 | async-start | bytes 2228224 | tf_op jit(solution)/shard_map/all_to_all | solution.py:285
  68.2 2.3 %collective-permute-start.2 = (bf16[8,256,256]{2,1,0:T(8,128)(2,1)S(1)}, bf16[8,256,256]{2,1,0:T(8,128)(2,1)S(1)}, u32[]{:S(2)}, u32[]{:S(2)}) collective-permute-start(bf16[8,256,256]{2,1,0:T(8,128)(2,1)S(1)} %all-to-all-done.1.x_ref), channel_id=1, source_target_pairs={{0,1},{1,0},{2,3},{3,2},{4,5},{5,4},{6,7},{7,6},{8,9},{9,8},{10,11... | collective-permute-start | bytes 3145736 | tf_op jit(solution)/shard_map/ppermute | solution.py:278
  71.1 0.5 shard_map.130.side_ref
  71.6 13.1 %all-to-all-done.2.got_ref = bf16[8,272,256]{2,1,0:T(8,128)(2,1)S(1)} async-done(((bf16[8,272,256]{2,1,0:T(8,128)(2,1)}), bf16[8,272,256]{2,1,0:T(8,128)(2,1)S(1)}, u32[]{:S(2)}, u32[]{:S(2)}) %all-to-all-start.2) | async-done | bytes 1114144 | tf_op jit(solution)/shard_map/all_to_all | solution.py:285
  84.8 1.8 %shard_map.131 = (bf16[1024,256]{1,0:T(8,128)(2,1)}, f32[8,512]{1,0:T(8,128)S(1)}) custom-call(f32[1]{0:T(128)S(6)} %copy.14.bias_ref, bf16[8,272,256]{2,1,0:T(8,128)(2,1)S(1)} %all-to-all-done.2.got_ref, f32[8,512]{1,0:T(8,128)S(1)} %shard_map.130.side_ref, s32[8,1024]{1,0:T(8,128)S(1)} %get-tuple-element.34.pos_ref), custom_call_target="tpu_custom_call" | custom-call | flops 268435456 | tf_op jit(solution)/shard_map/pallas_call | solution.py:43
  86.6 5.4 %all-to-all-start.3 = ((bf16[64,16,256]{2,1,0:T(8,128)(2,1)}), bf16[64,16,256]{2,1,0:T(8,128)(2,1)S(1)}, u32[]{:S(2)}, u32[]{:S(2)}) async-start(bf16[64,16,256]{2,1,0:T(8,128)(2,1)} %bitcast.12), calls=%async_computation.3 | async-start | bytes 1048576 | tf_op jit(solution)/shard_map/all_to_all | solution.py:282
  92.0 1.9 %collective-permute-start.3 = (bf16[2,256,256]{2,1,0:T(8,128)(2,1)}, bf16[2,256,256]{2,1,0:T(8,128)(2,1)S(1)}, u32[]{:S(2)}, u32[]{:S(2)}) collective-permute-start(bf16[2,256,256]{2,1,0:T(8,128)(2,1)} %get-tuple-element.32), channel_id=1, source_target_pairs={{0,1},{1,0},{2,3},{3,2},{4,5},{5,4},{6,7},{7,6},{8,9},{9,8},{10,11... | collective-permute-start | bytes 786440 | tf_op jit(solution)/shard_map/ppermute | solution.py:278
  93.9 1.7 %collective-permute-done.3.over_ref = bf16[2,256,256]{2,1,0:T(8,128)(2,1)S(1)} collective-permute-done((bf16[2,256,256]{2,1,0:T(8,128)(2,1)}, bf16[2,256,256]{2,1,0:T(8,128)(2,1)S(1)}, u32[]{:S(2)}, u32[]{:S(2)}) %collective-permute-start.3) | collective-permute-done | bytes 262176 | tf_op jit(solution)/shard_map/ppermute | solution.py:278
  95.6 2.4 %shard_map.132 = (f32[8,256,256]{2,1,0:T(8,128)}, f32[1,256]{1,0:T(1,128)}, f32[1,256]{1,0:T(1,128)}, f32[1]{0:T(128)}) custom-call(s32[1]{0:T(128)} %bitcast.core_ref, bf16[8,256,256]{2,1,0:T(8,128)(2,1)S(1)} %all-to-all-done.1.x_ref, bf16[8,256,256]{2,1,0:T(8,128)(2,1)S(1)} %collective-permute-done.2.far_x_ref, f32[256,256]{1,0:T(8,128)S(1)} %copy-done, ...), custom_call_target="tpu_custom_call" | custom-call | flops 536870912 | bytes 5242880 | tf_op jit(solution)/shard_map/pallas_call | solution.py:43
  98.0 13.2 %all-to-all-done.3 = bf16[64,16,256]{2,1,0:T(8,128)(2,1)S(1)} async-done(((bf16[64,16,256]{2,1,0:T(8,128)(2,1)}), bf16[64,16,256]{2,1,0:T(8,128)(2,1)S(1)}, u32[]{:S(2)}, u32[]{:S(2)}) %all-to-all-start.3) | async-done | bytes 524320 | tf_op jit(solution)/shard_map/all_to_all | solution.py:282
  111.2 1.1 shard_map.133
  (12 shorter events, 0.0 us)
Async XLA Ops:
  0.6 18.9 %copy-start.2 = (bf16[1,2048,256]{2,1,0:T(8,128)(2,1)S(1)}, bf16[1,2048,256]{2,1,0:T(8,128)(2,1)}, u32[]{:S(2)}) copy-start(bf16[1,2048,256]{2,1,0:T(8,128)(2,1)} %param.12) | copy-start | bytes 3145732
  3.0 35.9 %all-to-all-start = ((bf16[64,16,256]{2,1,0:T(8,128)(2,1)}), bf16[64,16,256]{2,1,0:T(8,128)(2,1)S(1)}, u32[]{:S(2)}, u32[]{:S(2)}) async-start(bf16[64,16,256]{2,1,0:T(8,128)(2,1)} %bitcast.13), calls=%async_computation | async-start | bytes 1048576 | tf_op jit(solution)/shard_map/all_to_all | solution.py:282
  19.5 28.9 %collective-permute-start = (bf16[8,256,256]{2,1,0:T(8,128)(2,1)S(1)}, bf16[8,256,256]{2,1,0:T(8,128)(2,1)S(1)}, u32[]{:S(2)}, u32[]{:S(2)}) collective-permute-start(bf16[8,256,256]{2,1,0:T(8,128)(2,1)S(1)} %bitcast.10), channel_id=1, source_target_pairs={{0,1},{1,0},{2,3},{3,2},{4,5},{5,4},{6,7},{7,6},{8,9},{9,8},{10,11... | collective-permute-start | bytes 3145736 | tf_op jit(solution)/shard_map/ppermute | solution.py:278
  40.8 4.3 %copy-start.3 = (f32[1,256]{1,0:T(1,128)S(1)}, f32[1,256]{1,0:T(1,128)}, u32[]{:S(2)}) copy-start(f32[1,256]{1,0:T(1,128)} %param.14) | copy-start | bytes 3076
  40.9 4.3 %copy-start.4 = (f32[1,256]{1,0:T(1,128)S(1)}, f32[1,256]{1,0:T(1,128)}, u32[]{:S(2)}) copy-start(f32[1,256]{1,0:T(1,128)} %param.13) | copy-start | bytes 3076
  40.9 20.3 %all-to-all-start.1 = ((bf16[8,256,256]{2,1,0:T(8,128)(2,1)}), bf16[8,256,256]{2,1,0:T(8,128)(2,1)S(1)}, u32[]{:S(2)}, u32[]{:S(2)}) async-start(bf16[8,256,256]{2,1,0:T(8,128)(2,1)} %get-tuple-element.26), calls=%async_computation.1 | async-start | bytes 2097152 | tf_op jit(solution)/shard_map/all_to_all | solution.py:285
  45.2 3.2 %collective-permute-start.1 = (f32[2,256]{1,0:T(2,128)S(1)}, f32[2,256]{1,0:T(2,128)S(1)}, u32[]{:S(2)}, u32[]{:S(2)}) collective-permute-start(f32[2,256]{1,0:T(2,128)S(1)} %pad_maximum_fusion.bh_ref), channel_id=1, source_target_pairs={{0,1},{1,0},{2,3},{3,2},{4,5},{5,4},{6,7},{7,6},{8,9},{9,8},{10,11... | collective-permute-start | bytes 6152 | tf_op jit(solution)/shard_map/ppermute | solution.py:278
  48.4 12.7 %copy-start.5 = (bf16[8,256,256]{2,1,0:T(8,128)(2,1)}, bf16[8,256,256]{2,1,0:T(8,128)(2,1)S(1)}, u32[]{:S(2)}) copy-start(bf16[8,256,256]{2,1,0:T(8,128)(2,1)S(1)} %collective-permute-done.far_hbm) | copy-start | bytes 3145732
  64.6 20.2 %all-to-all-start.2 = ((bf16[8,272,256]{2,1,0:T(8,128)(2,1)}), bf16[8,272,256]{2,1,0:T(8,128)(2,1)S(1)}, u32[]{:S(2)}, u32[]{:S(2)}) async-start(bf16[8,272,256]{2,1,0:T(8,128)(2,1)} %get-tuple-element.27), calls=%async_computation.2 | async-start | bytes 2228224 | tf_op jit(solution)/shard_map/all_to_all | solution.py:285
  68.2 27.4 %collective-permute-start.2 = (bf16[8,256,256]{2,1,0:T(8,128)(2,1)S(1)}, bf16[8,256,256]{2,1,0:T(8,128)(2,1)S(1)}, u32[]{:S(2)}, u32[]{:S(2)}) collective-permute-start(bf16[8,256,256]{2,1,0:T(8,128)(2,1)S(1)} %all-to-all-done.1.x_ref), channel_id=1, source_target_pairs={{0,1},{1,0},{2,3},{3,2},{4,5},{5,4},{6,7},{7,6},{8,9},{9,8},{10,11... | collective-permute-start | bytes 3145736 | tf_op jit(solution)/shard_map/ppermute | solution.py:278
  71.6 24.0 %copy-start = (f32[256,256]{1,0:T(8,128)S(1)}, f32[256,256]{1,0:T(8,128)}, u32[]{:S(2)}) copy-start(f32[256,256]{1,0:T(8,128)} %get-tuple-element.30.act_ref) | copy-start | bytes 786436
  86.6 9.0 %copy-start.1 = (f32[256,256]{1,0:T(8,128)S(1)}, f32[256,256]{1,0:T(8,128)}, u32[]{:S(2)}) copy-start(f32[256,256]{1,0:T(8,128)} %get-tuple-element.31.g_ref) | copy-start | bytes 786436
  86.6 24.6 %all-to-all-start.3 = ((bf16[64,16,256]{2,1,0:T(8,128)(2,1)}), bf16[64,16,256]{2,1,0:T(8,128)(2,1)S(1)}, u32[]{:S(2)}, u32[]{:S(2)}) async-start(bf16[64,16,256]{2,1,0:T(8,128)(2,1)} %bitcast.12), calls=%async_computation.3 | async-start | bytes 1048576 | tf_op jit(solution)/shard_map/all_to_all | solution.py:282
  92.0 3.6 %collective-permute-start.3 = (bf16[2,256,256]{2,1,0:T(8,128)(2,1)}, bf16[2,256,256]{2,1,0:T(8,128)(2,1)S(1)}, u32[]{:S(2)}, u32[]{:S(2)}) collective-permute-start(bf16[2,256,256]{2,1,0:T(8,128)(2,1)} %get-tuple-element.32), channel_id=1, source_target_pairs={{0,1},{1,0},{2,3},{3,2},{4,5},{5,4},{6,7},{7,6},{8,9},{9,8},{10,11... | collective-permute-start | bytes 786440 | tf_op jit(solution)/shard_map/ppermute | solution.py:278

commit v4 on v3

--- a/solution.py
+++ b/solution.py
@@ -13,6 +13,7 @@
 EXTRA = 16
 INTERPRET = False
 VMEM, SMEM, HBM = pltpu.VMEM, pltpu.SMEM, pltpu.HBM
+PIN = object()
 DMA = pltpu.SemaphoreType.DMA
 LANES = 128
 PARTS = 4
@@ -36,15 +37,16 @@
 
 def call(kernel, out_shape, ins=None, outs=None, scratch=(), flops=0, nbytes=0, vmem=32):
     kinds = outs or [VMEM] * len(out_shape)
+    forced = {HBM: HBM, PIN: VMEM}
 
     def run(*args):
         spaces = ins or [VMEM] * len(args)
-        args = [pltpu.with_memory_space_constraint(a, HBM) if m is HBM else a for a, m in zip(args, spaces)]
+        args = [pltpu.with_memory_space_constraint(a, forced[m]) if m in forced else a for a, m in zip(args, spaces)]
         return pl.pallas_call(
             kernel,
-            out_shape=[HBM(o.shape, o.dtype) if m is HBM else o for o, m in zip(out_shape, kinds)],
-            in_specs=[pl.BlockSpec(memory_space=m) for m in spaces],
-            out_specs=[pl.BlockSpec(memory_space=m) for m in kinds],
+            out_shape=[forced[m](o.shape, o.dtype) if m in forced else o for o, m in zip(out_shape, kinds)],
+            in_specs=[pl.BlockSpec(memory_space=forced.get(m, m)) for m in spaces],
+            out_specs=[pl.BlockSpec(memory_space=forced.get(m, m)) for m in kinds],
             scratch_shapes=list(scratch),
             compiler_params=pltpu.CompilerParams(vmem_limit_bytes=vmem * 2**20),
             cost_estimate=pl.CostEstimate(flops=flops, bytes_accessed=nbytes, transcendentals=0),
@@ -113,9 +115,9 @@
 
 
 def compact_kernel(arms, packed, slots_ref, send_hbm, pos_ref, side_ref, rows_ref, sem):
-    total, width = slots_ref.shape
-    slots = slots_ref[...]
-    side = side_of(slots, arms)
+    total, width = arms * SLOT, slots_ref.shape[2]
+    side = slots_ref[:, SIDE, :].astype(F32)
+    slots = slots_ref[...].reshape(total, width)
     side_ref[...] = side.astype(BF16)
     lane8 = iota((8, width), 1)
     weight_lanes = ones_where((lane8 >= SLOT) & (lane8 < 2 * SLOT))
@@ -139,7 +141,9 @@
         store.wait()
 
 
-def prepare_kernel(arms, packed, given_ref, pos_ref, side_ref):
+def prepare_kernel(arms, packed, given_ref, pos_ref, far_hbm, side_ref, far_ref, sem):
+    copy = pltpu.make_async_copy(far_hbm, far_ref, sem)
+    copy.start()
     total, width = arms * SLOT, given_ref.shape[1]
     side = given_ref[...]
     gather = ones_where(iota((packed, total), 0) == pos_ref[0:1])
@@ -151,6 +155,7 @@
     weight = jnp.sum(jnp.where(same, weight, 0.0), axis=0, keepdims=True)
     both = jnp.where(iota((8, total), 0) == 0, target, weight)
     side_ref[...] = mm(both.astype(BF16), gather, NT)
+    copy.wait()
 
 
 def unit(pre, head):
@@ -159,31 +164,18 @@
 
 
 def forward_kernel(
-    x_ref, near_ref, far_hbm, bh_ref, far_bh_ref, msg_hbm, over_hbm, act_hbm, g_hbm,
-    far_ref, msg_ref, over_ref, act_ref, g_ref, in_sem, msg_sem, out_sem,
+    x_ref, near_ref, far_ref, bh_ref, far_bh_ref, msg_hbm,
+    msg_ref, out_sem,
 ):
     blocks, rows, width = x_ref.shape
-    loads = [pltpu.make_async_copy(far_hbm.at[j], far_ref.at[j], in_sem.at[j]) for j in range(blocks)]
-    for load in loads:
-        load.start()
     head, far_head = bh_ref[1:2], far_bh_ref[1:2]
     pre = sum(mm(x_ref[j], near_ref[j]) for j in range(blocks)) + bh_ref[0:1]
     act, g = unit(pre, head)
-    act_ref[...] = act
-    g_ref[...] = g
     g = g.astype(BF16)
-    pre = jnp.broadcast_to(far_bh_ref[0:1], pre.shape)
-    for j in range(blocks):
-        loads[j].wait()
-        pre += mm(x_ref[j], far_ref[j])
+    pre = sum(mm(x_ref[j], far_ref[j]) for j in range(blocks)) + far_bh_ref[0:1]
     far_act, far_g = unit(pre, far_head)
     far_g = far_g.astype(BF16)
-    over_ref[0] = far_act.astype(BF16)
-    over_ref[1] = far_g
-    stores = [
-        pltpu.make_async_copy(a, b, out_sem.at[i])
-        for i, (a, b) in enumerate(((act_ref, act_hbm), (g_ref, g_hbm), (over_ref, over_hbm)))
-    ]
+    stores = []
     share = act * head + far_act * far_head
     cut = min(LANES, width)
     share = sum(share[:, i : i + cut] for i in range(0, width, cut))
@@ -195,10 +187,8 @@
         part = mm(g, near_ref[j], NT) + mm(far_g, far_ref[j], NT)
         msg_ref[j, pl.ds(0, rows), :] = part.astype(BF16)
         msg_ref[j, pl.ds(rows, EXTRA), pl.ds(0, rows)] = extra
-        stores.append(pltpu.make_async_copy(msg_ref.at[j], msg_hbm.at[j], msg_sem.at[j]))
+        stores.append(pltpu.make_async_copy(msg_ref.at[j], msg_hbm.at[j], out_sem.at[j]))
         stores[-1].start()
-    for store in stores[:3]:
-        store.start()
     for store in stores:
         store.wait()
 
@@ -246,23 +236,25 @@
     pred_ref[...] = pred.reshape(rows).astype(BF16)
 
 
-def grads_kernel(
-    core_ref, x_ref, far_x_ref, act_ref, g_ref, over_ref, resid_ref, matrix_ref, bias_ref, head_ref, scalar_ref
-):
+def grads_kernel(core_ref, x_ref, far_x_ref, near_ref, bh_ref, resid_ref, matrix_ref, bias_ref, head_ref, scalar_ref):
     first = core_ref[0] == 0
-    half = act_ref.shape[0]
+    blocks, half, _ = x_ref.shape
     low, high = resid_ref[0:1, 0:half], resid_ref[0:1, half : 2 * half]
     scalar_ref[0] = jnp.sum(resid_ref[0:1])
     mine = column(jnp.where(first, low, high))[:, 0:1]
     other = column(jnp.where(first, high, low))[:, 0:1]
-    near, far = g_ref[...] * mine, over_ref[1].astype(F32) * other
-    bias_ref[...] = jnp.sum(near, axis=0, keepdims=True) + jnp.sum(far, axis=0, keepdims=True)
-    head_ref[...] = jnp.sum(act_ref[...] * mine, axis=0, keepdims=True) + jnp.sum(
-        over_ref[0].astype(F32) * other, axis=0, keepdims=True
-    )
-    near, far = near.astype(BF16), far.astype(BF16)
-    for j in range(x_ref.shape[0]):
-        matrix_ref[j] = mm(x_ref[j], near, TN) + mm(far_x_ref[j], far, TN)
+    pre_half, bias, head = [], 0.0, 0.0
+    for rows_ref, resid in ((x_ref, mine), (far_x_ref, other)):
+        pre = sum(mm(rows_ref[j], near_ref[j]) for j in range(blocks)) + bh_ref[0:1]
+        act, g = unit(pre, bh_ref[1:2])
+        pre_grad = g * resid
+        bias += jnp.sum(pre_grad, axis=0, keepdims=True)
+        head += jnp.sum(act * resid, axis=0, keepdims=True)
+        pre_half.append(pre_grad.astype(BF16))
+    bias_ref[...] = bias
+    head_ref[...] = head
+    for j in range(blocks):
+        matrix_ref[j] = mm(x_ref[j], pre_half[0], TN) + mm(far_x_ref[j], pre_half[1], TN)
 
 
 def body(rep, arm_ids, outcome, weight, w_hidden, b_hidden, w_head, b_head):
@@ -302,36 +294,32 @@
         outs=[HBM, VMEM, VMEM],
         scratch=[VMEM((2, rows, width), BF16), DMA((tower,))],
         flops=2 * total * packed * width,
-    )(arrived)
+    )(arrived.reshape(arms, SLOT, width))
     matrix = w_hidden.reshape(tower, width, hidden)
     both = jnp.concatenate([b_hidden, w_head], axis=0)
     inputs = spread(send)
     far_matrix, far_both = swap(matrix), swap(both)
-    (side,) = call(
+    side, far_matrix = call(
         functools.partial(prepare_kernel, arms, packed),
-        (sds((8, packed), F32),),
+        (sds((8, packed), F32), sds((tower, width, hidden), BF16)),
+        ins=[VMEM, VMEM, HBM],
+        outs=[VMEM, PIN],
+        scratch=[DMA],
         flops=4 * total * packed * arms,
-    )(given, pos)
-    msg, over, act, g = call(
+    )(given, pos, far_matrix)
+    (msg,) = call(
         forward_kernel,
-        (
-            sds((tower, rows + EXTRA, width), BF16),
-            sds((2, rows, hidden), BF16),
-            sds((rows, hidden), F32),
-            sds((rows, hidden), F32),
-        ),
-        ins=[VMEM, VMEM, HBM, VMEM, VMEM],
-        outs=[HBM] * 4,
+        (sds((tower, rows + EXTRA, width), BF16),),
+        ins=[VMEM, VMEM, PIN, VMEM, VMEM],
+        outs=[HBM],
         scratch=[
-            VMEM((tower, width, hidden), BF16), VMEM((tower, rows + EXTRA, width), BF16),
-            VMEM((2, rows, hidden), BF16), VMEM((rows, hidden), F32), VMEM((rows, hidden), F32),
-            DMA((tower,)), DMA((tower,)), DMA((3,)),
+            VMEM((tower, rows + EXTRA, width), BF16), DMA((tower,)),
         ],
         flops=8 * rows * tower * width * hidden,
     )(inputs, matrix, far_matrix, both, far_both)
     got = spread(msg)
-    msg, inputs2, over = lax.optimization_barrier((msg, inputs, over))
-    far_inputs, far_over = swap(inputs2), swap(over)
+    msg, inputs2 = lax.optimization_barrier((msg, inputs))
+    far_inputs = swap(inputs2)
     back_slots, resid = call(
         functools.partial(back_kernel, arms),
         (sds((total, width), BF16), sds((8, packed), F32)),
@@ -349,11 +337,11 @@
             sds((1, hidden), F32),
             sds((1,), F32),
         ),
-        ins=[SMEM] + [VMEM] * 6,
+        ins=[SMEM] + [VMEM] * 5,
         outs=[VMEM, VMEM, VMEM, SMEM],
-        flops=2 * packed * tower * width * hidden,
+        flops=4 * packed * tower * width * hidden,
         nbytes=5 * 2**20,
-    )(core, inputs, far_inputs, act, g, far_over, resid)
+    )(core, inputs, far_inputs, matrix, both, resid)
     grad_rep, predicted = call(
         functools.partial(unpack_kernel, arms),
         (sds((rows, width), BF16), sds((rows,), BF16)),

time: 113 us -> 111 us (0.982)
  starting transfers between devices: 38.3 us -> 36.2 us
  waiting for transfers between devices: 59 us -> 57.4 us
  Pallas kernels: 13.5 us -> 14.8 us
    ppermute x4 -> x3, waiting for transfers between devices: 2.51 us -> 0.01 us  [swap(): return lax.ppermute(value, 'tower', [(i, i ^ 1) for i in range(tower)])]
    ppermute x4 -> x3, starting transfers between devices: 8.55 us -> 6.63 us  [swap(): return lax.ppermute(value, 'tower', [(i, i ^ 1) for i in range(tower)])]
    all_to_all x2, waiting for transfers between devices: 30.7 us -> 32.5 us  [exchange(): lax.all_to_all(cut, 'dp', split_axis=0, concat_axis=0, tiled=True)]
    pallas_call x7, Pallas kernels: 13.5 us -> 14.8 us  [run(): pl.pallas_call(kernel, out_shape=[forced[m](o.shape, o.dtype) if m in for...]
  transfers between devices with their start and end apart: 8 -> 7, of which waited for: 6 -> 4; matrix products, arithmetic and copies ran while one was open for 0% -> 0% of each run, Pallas kernels for 6% -> 8%
where the time goes in v4:
time: 111 us
  waiting for transfers between devices  57.4 us (52%)
  starting transfers between devices  36.2 us (33%)
  Pallas kernels  14.8 us (13%)
  between operations  1.47 us (1%)
    all_to_all x2, waiting for transfers between devices, exchange(): lax.all_to_all(cut, 'dp', split_axis=0, concat_axis=0, tiled=True)  32.5 us
    all_to_all x2, waiting for transfers between devices, spread(): lax.all_to_all(blocks, 'tower', split_axis=0, concat_axis=0, tiled=True)  24.9 us
    all_to_all x2, starting transfers between devices, exchange(): lax.all_to_all(cut, 'dp', split_axis=0, concat_axis=0, tiled=True)  21.7 us
    pallas_call x7, Pallas kernels, run(): pl.pallas_call(kernel, out_shape=[forced[m](o.shape, o.dtype) if m in for...  14.8 us
    all_to_all x2, starting transfers between devices, spread(): lax.all_to_all(blocks, 'tower', split_axis=0, concat_axis=0, tiled=True)  7.89 us
    ppermute x3, starting transfers between devices, swap(): return lax.ppermute(value, 'tower', [(i, i ^ 1) for i in range(tower)])  6.63 us
  transfers between devices with their start and end apart: 7, of which 4 were waited for; matrix products, arithmetic and copies ran while one was open for 0% of the time, Pallas kernels for 8%

profile of v4, /device:TPU:16, one launch (start us, length us, event | category | flops | bytes accessed | tf_op | source)
XLA Modules:
  0.0 110.9 jit_solution(1099870301956963037)
XLA Ops:
  0.6 2.4 %shard_map.127 = (bf16[1024,256]{1,0:T(8,128)(2,1)}, s32[8,256]{1,0:T(8,128)S(1)}) custom-call(s32[1,256]{1,0:T(1,128)} %bitcast.13, bf16[256]{0:T(256)(128)(2,1)} %outcome_hbm.1, bf16[256]{0:T(256)(128)(2,1)} %weight_hbm.1, bf16[256,256]{1,0:T(8,128)(2,1)} %rep_hbm.1), custom_call_target="tpu_custom_call" | custom-call | flops 134217728 | tf_op jit(solution)/shard_map/pallas_call | solution.py:45
  3.0 16.5 %all-to-all-start = ((bf16[64,16,256]{2,1,0:T(8,128)(2,1)}), bf16[64,16,256]{2,1,0:T(8,128)(2,1)S(1)}, u32[]{:S(2)}, u32[]{:S(2)}) async-start(bf16[64,16,256]{2,1,0:T(8,128)(2,1)} %bitcast.12), calls=%async_computation | async-start | bytes 1048576 | tf_op jit(solution)/shard_map/all_to_all | solution.py:274
  19.5 1.9 %collective-permute-start = (bf16[8,256,256]{2,1,0:T(8,128)(2,1)S(1)}, bf16[8,256,256]{2,1,0:T(8,128)(2,1)S(1)}, u32[]{:S(2)}, u32[]{:S(2)}) collective-permute-start(bf16[8,256,256]{2,1,0:T(8,128)(2,1)S(1)} %bitcast.8), channel_id=1, source_target_pairs={{0,1},{1,0},{2,3},{3,2},{4,5},{5,4},{6,7},{7,6},{8,9},{9,8},{10,11... | collective-permute-start | bytes 3145736 | tf_op jit(solution)/shard_map/ppermute | solution.py:270
  21.4 17.5 %all-to-all-done.slots_ref = bf16[64,16,256]{2,1,0:T(8,128)(2,1)S(1)} async-done(((bf16[64,16,256]{2,1,0:T(8,128)(2,1)}), bf16[64,16,256]{2,1,0:T(8,128)(2,1)S(1)}, u32[]{:S(2)}, u32[]{:S(2)}) %all-to-all-start) | async-done | bytes 524320 | tf_op jit(solution)/shard_map/all_to_all | solution.py:274
  38.9 1.9 %shard_map.128 = (bf16[8,256,256]{2,1,0:T(8,128)(2,1)}, s32[8,1024]{1,0:T(8,128)S(1)}, bf16[64,256]{1,0:T(8,128)(2,1)S(1)}) custom-call(bf16[64,16,256]{2,1,0:T(8,128)(2,1)S(1)} %all-to-all-done.slots_ref), custom_call_target="tpu_custom_call" | custom-call | flops 268435456 | tf_op jit(solution)/shard_map/pallas_call | solution.py:45
  40.8 0.0 copy-start.2
  40.8 0.0 copy-start.3
  40.8 4.3 %all-to-all-start.1 = ((bf16[8,256,256]{2,1,0:T(8,128)(2,1)}), bf16[8,256,256]{2,1,0:T(8,128)(2,1)S(1)}, u32[]{:S(2)}, u32[]{:S(2)}) async-start(bf16[8,256,256]{2,1,0:T(8,128)(2,1)} %get-tuple-element.23), calls=%async_computation.1 | async-start | bytes 2097152 | tf_op jit(solution)/shard_map/all_to_all | solution.py:277
  45.2 2.4 %collective-permute-start.1 = (f32[2,256]{1,0:T(2,128)S(1)}, f32[2,256]{1,0:T(2,128)S(1)}, u32[]{:S(2)}, u32[]{:S(2)}) collective-permute-start(f32[2,256]{1,0:T(2,128)S(1)} %pad_maximum_fusion.bh_ref), channel_id=1, source_target_pairs={{0,1},{1,0},{2,3},{3,2},{4,5},{5,4},{6,7},{7,6},{8,9},{9,8},{10,11... | collective-permute-start | bytes 6152 | tf_op jit(solution)/shard_map/ppermute | solution.py:270
  47.6 0.0 collective-permute-done.far_hbm
  47.6 1.0 copy-done.1
  48.6 1.2 %shard_map.129 = (f32[8,512]{1,0:T(8,128)S(1)}, bf16[8,256,256]{2,1,0:T(8,128)(2,1)S(1)}) custom-call(bf16[64,256]{1,0:T(8,128)(2,1)S(1)} %get-tuple-element.24.given_ref, s32[8,1024]{1,0:T(8,128)S(1)} %get-tuple-element.25.pos_ref, bf16[8,256,256]{2,1,0:T(8,128)(2,1)} %copy-done.1), custom_call_target="tpu_custom_call" | custom-call | flops 134217728 | tf_op jit(solution)/shard_map/pallas_call | solution.py:45
  49.8 0.0 collective-permute-done.1.far_bh_ref
  49.8 11.3 %all-to-all-done.1.x_ref = bf16[8,256,256]{2,1,0:T(8,128)(2,1)S(1)} async-done(((bf16[8,256,256]{2,1,0:T(8,128)(2,1)}), bf16[8,256,256]{2,1,0:T(8,128)(2,1)S(1)}, u32[]{:S(2)}, u32[]{:S(2)}) %all-to-all-start.1) | async-done | bytes 1048608 | tf_op jit(solution)/shard_map/all_to_all | solution.py:277
  61.1 2.3 %shard_map.130 = bf16[8,272,256]{2,1,0:T(8,128)(2,1)} custom-call(bf16[8,256,256]{2,1,0:T(8,128)(2,1)S(1)} %all-to-all-done.1.x_ref, bf16[8,256,256]{2,1,0:T(8,128)(2,1)S(1)} %bitcast.9, bf16[8,256,256]{2,1,0:T(8,128)(2,1)S(1)} %get-tuple-element.26.far_ref, f32[2,256]{1,0:T(2,128)S(1)} %pad_maximum_fusion.bh_ref, f32[2,256]{1,0:T(2,128)S(1)} %collective-permute-done.1.far_bh_ref), custom_call_target="tpu_custom_call" | custom-call | flops 1073741824 | tf_op jit(solution)/shard_map/pallas_call | solution.py:45
  63.4 3.6 %all-to-all-start.2 = ((bf16[8,272,256]{2,1,0:T(8,128)(2,1)}), bf16[8,272,256]{2,1,0:T(8,128)(2,1)S(1)}, u32[]{:S(2)}, u32[]{:S(2)}) async-start(bf16[8,272,256]{2,1,0:T(8,128)(2,1)} %shard_map.130), calls=%async_computation.2 | async-start | bytes 2228224 | tf_op jit(solution)/shard_map/all_to_all | solution.py:277
  67.0 2.3 %collective-permute-start.2 = (bf16[8,256,256]{2,1,0:T(8,128)(2,1)S(1)}, bf16[8,256,256]{2,1,0:T(8,128)(2,1)}, u32[]{:S(2)}, u32[]{:S(2)}) collective-permute-start(bf16[8,256,256]{2,1,0:T(8,128)(2,1)S(1)} %all-to-all-done.1.x_ref), channel_id=1, source_target_pairs={{0,1},{1,0},{2,3},{3,2},{4,5},{5,4},{6,7},{7,6},{8,9},{9,8},{10,11... | collective-permute-start | bytes 3145736 | tf_op jit(solution)/shard_map/ppermute | solution.py:270
  69.9 13.6 %all-to-all-done.2.got_ref = bf16[8,272,256]{2,1,0:T(8,128)(2,1)S(1)} async-done(((bf16[8,272,256]{2,1,0:T(8,128)(2,1)}), bf16[8,272,256]{2,1,0:T(8,128)(2,1)S(1)}, u32[]{:S(2)}, u32[]{:S(2)}) %all-to-all-start.2) | async-done | bytes 1114144 | tf_op jit(solution)/shard_map/all_to_all | solution.py:277
  83.5 1.8 %shard_map.131 = (bf16[1024,256]{1,0:T(8,128)(2,1)}, f32[8,512]{1,0:T(8,128)S(1)}) custom-call(f32[1]{0:T(128)S(6)} %copy.14.bias_ref, bf16[8,272,256]{2,1,0:T(8,128)(2,1)S(1)} %all-to-all-done.2.got_ref, f32[8,512]{1,0:T(8,128)S(1)} %get-tuple-element.28.side_ref, s32[8,1024]{1,0:T(8,128)S(1)} %get-tuple-element.25.pos_ref), custom_call_target="tpu_custom_call" | custom-call | flops 268435456 | tf_op jit(solution)/shard_map/pallas_call | solution.py:45
  85.4 5.2 %all-to-all-start.3 = ((bf16[64,16,256]{2,1,0:T(8,128)(2,1)}), bf16[64,16,256]{2,1,0:T(8,128)(2,1)S(1)}, u32[]{:S(2)}, u32[]{:S(2)}) async-start(bf16[64,16,256]{2,1,0:T(8,128)(2,1)} %bitcast.11), calls=%async_computation.3 | async-start | bytes 1048576 | tf_op jit(solution)/shard_map/all_to_all | solution.py:274
  90.6 0.0 collective-permute-done.2.far_x_ref
  90.6 4.1 %shard_map.132 = (f32[8,256,256]{2,1,0:T(8,128)}, f32[1,256]{1,0:T(1,128)}, f32[1,256]{1,0:T(1,128)}, f32[1]{0:T(128)}) custom-call(s32[1]{0:T(128)} %bitcast.core_ref, bf16[8,256,256]{2,1,0:T(8,128)(2,1)S(1)} %all-to-all-done.1.x_ref, bf16[8,256,256]{2,1,0:T(8,128)(2,1)} %collective-permute-done.2.far_x_ref, bf16[8,256,256]{2,1,0:T(8,128)(2,1)S(1)} %bitcast.10, ...), custom_call_target="tpu_custom_call" | custom-call | flops 1073741824 | bytes 5242880 | tf_op jit(solution)/shard_map/pallas_call | solution.py:45
  94.8 15.0 %all-to-all-done.3 = bf16[64,16,256]{2,1,0:T(8,128)(2,1)S(1)} async-done(((bf16[64,16,256]{2,1,0:T(8,128)(2,1)}), bf16[64,16,256]{2,1,0:T(8,128)(2,1)S(1)}, u32[]{:S(2)}, u32[]{:S(2)}) %all-to-all-start.3) | async-done | bytes 524320 | tf_op jit(solution)/shard_map/all_to_all | solution.py:274
  109.8 1.1 shard_map.133
  (6 shorter events, 0.0 us)
Async XLA Ops:
  0.6 18.9 %copy-start = (bf16[1,2048,256]{2,1,0:T(8,128)(2,1)S(1)}, bf16[1,2048,256]{2,1,0:T(8,128)(2,1)}, u32[]{:S(2)}) copy-start(bf16[1,2048,256]{2,1,0:T(8,128)(2,1)} %param.12) | copy-start | bytes 3145732
  3.0 35.9 %all-to-all-start = ((bf16[64,16,256]{2,1,0:T(8,128)(2,1)}), bf16[64,16,256]{2,1,0:T(8,128)(2,1)S(1)}, u32[]{:S(2)}, u32[]{:S(2)}) async-start(bf16[64,16,256]{2,1,0:T(8,128)(2,1)} %bitcast.12), calls=%async_computation | async-start | bytes 1048576 | tf_op jit(solution)/shard_map/all_to_all | solution.py:274
  19.5 28.1 %collective-permute-start = (bf16[8,256,256]{2,1,0:T(8,128)(2,1)S(1)}, bf16[8,256,256]{2,1,0:T(8,128)(2,1)S(1)}, u32[]{:S(2)}, u32[]{:S(2)}) collective-permute-start(bf16[8,256,256]{2,1,0:T(8,128)(2,1)S(1)} %bitcast.8), channel_id=1, source_target_pairs={{0,1},{1,0},{2,3},{3,2},{4,5},{5,4},{6,7},{7,6},{8,9},{9,8},{10,11... | collective-permute-start | bytes 3145736 | tf_op jit(solution)/shard_map/ppermute | solution.py:270
  40.8 4.3 %copy-start.2 = (f32[1,256]{1,0:T(1,128)S(1)}, f32[1,256]{1,0:T(1,128)}, u32[]{:S(2)}) copy-start(f32[1,256]{1,0:T(1,128)} %param.14) | copy-start | bytes 3076
  40.8 4.3 %copy-start.3 = (f32[1,256]{1,0:T(1,128)S(1)}, f32[1,256]{1,0:T(1,128)}, u32[]{:S(2)}) copy-start(f32[1,256]{1,0:T(1,128)} %param.13) | copy-start | bytes 3076
  40.8 20.3 %all-to-all-start.1 = ((bf16[8,256,256]{2,1,0:T(8,128)(2,1)}), bf16[8,256,256]{2,1,0:T(8,128)(2,1)S(1)}, u32[]{:S(2)}, u32[]{:S(2)}) async-start(bf16[8,256,256]{2,1,0:T(8,128)(2,1)} %get-tuple-element.23), calls=%async_computation.1 | async-start | bytes 2097152 | tf_op jit(solution)/shard_map/all_to_all | solution.py:277
  45.2 4.7 %collective-permute-start.1 = (f32[2,256]{1,0:T(2,128)S(1)}, f32[2,256]{1,0:T(2,128)S(1)}, u32[]{:S(2)}, u32[]{:S(2)}) collective-permute-start(f32[2,256]{1,0:T(2,128)S(1)} %pad_maximum_fusion.bh_ref), channel_id=1, source_target_pairs={{0,1},{1,0},{2,3},{3,2},{4,5},{5,4},{6,7},{7,6},{8,9},{9,8},{10,11... | collective-permute-start | bytes 6152 | tf_op jit(solution)/shard_map/ppermute | solution.py:270
  47.6 1.0 copy-start.1
  63.4 20.2 %all-to-all-start.2 = ((bf16[8,272,256]{2,1,0:T(8,128)(2,1)}), bf16[8,272,256]{2,1,0:T(8,128)(2,1)S(1)}, u32[]{:S(2)}, u32[]{:S(2)}) async-start(bf16[8,272,256]{2,1,0:T(8,128)(2,1)} %shard_map.130), calls=%async_computation.2 | async-start | bytes 2228224 | tf_op jit(solution)/shard_map/all_to_all | solution.py:277
  67.0 23.7 %collective-permute-start.2 = (bf16[8,256,256]{2,1,0:T(8,128)(2,1)S(1)}, bf16[8,256,256]{2,1,0:T(8,128)(2,1)}, u32[]{:S(2)}, u32[]{:S(2)}) collective-permute-start(bf16[8,256,256]{2,1,0:T(8,128)(2,1)S(1)} %all-to-all-done.1.x_ref), channel_id=1, source_target_pairs={{0,1},{1,0},{2,3},{3,2},{4,5},{5,4},{6,7},{7,6},{8,9},{9,8},{10,11... | collective-permute-start | bytes 3145736 | tf_op jit(solution)/shard_map/ppermute | solution.py:270
  85.4 24.4 %all-to-all-start.3 = ((bf16[64,16,256]{2,1,0:T(8,128)(2,1)}), bf16[64,16,256]{2,1,0:T(8,128)(2,1)S(1)}, u32[]{:S(2)}, u32[]{:S(2)}) async-start(bf16[64,16,256]{2,1,0:T(8,128)(2,1)} %bitcast.11), calls=%async_computation.3 | async-start | bytes 1048576 | tf_op jit(solution)/shard_map/all_to_all | solution.py:274

commit v5 on v4

--- a/solution.py
+++ b/solution.py
@@ -114,7 +114,7 @@
     return mm(pick_side(arms), slots)
 
 
-def compact_kernel(arms, packed, slots_ref, send_hbm, pos_ref, side_ref, rows_ref, sem):
+def compact_kernel(arms, packed, slots_ref, send_ref, pos_ref, side_ref):
     total, width = arms * SLOT, slots_ref.shape[2]
     side = slots_ref[:, SIDE, :].astype(F32)
     slots = slots_ref[...].reshape(total, width)
@@ -129,21 +129,14 @@
     pos = jnp.where(depth < count.astype(I32), start.astype(I32) + depth, 2 * packed)
     pos_ref[...] = pos
     half = packed // 2
-    blocks = send_hbm.shape[0]
-    stores = []
     for h in range(2):
         gather = ones_where(iota((half, total), 0) + h * half == pos[0:1])
-        rows_ref[h] = mm(gather, slots).astype(BF16)
-        for d in range(h, blocks, 2):
-            stores.append(pltpu.make_async_copy(rows_ref.at[h], send_hbm.at[d], sem.at[d]))
-            stores[-1].start()
-    for store in stores:
-        store.wait()
-
-
-def prepare_kernel(arms, packed, given_ref, pos_ref, far_hbm, side_ref, far_ref, sem):
-    copy = pltpu.make_async_copy(far_hbm, far_ref, sem)
-    copy.start()
+        rows = mm(gather, slots).astype(BF16)
+        for d in range(h, send_ref.shape[0], 2):
+            send_ref[d] = rows
+
+
+def prepare_kernel(arms, packed, given_ref, pos_ref, side_ref):
     total, width = arms * SLOT, given_ref.shape[1]
     side = given_ref[...]
     gather = ones_where(iota((packed, total), 0) == pos_ref[0:1])
@@ -155,7 +148,6 @@
     weight = jnp.sum(jnp.where(same, weight, 0.0), axis=0, keepdims=True)
     both = jnp.where(iota((8, total), 0) == 0, target, weight)
     side_ref[...] = mm(both.astype(BF16), gather, NT)
-    copy.wait()
 
 
 def unit(pre, head):
@@ -287,30 +279,22 @@
         ],
         flops=2 * total * rows * width,
     )(arm_ids.reshape(1, rows), outcome, weight, rep)
+    matrix = w_hidden.reshape(tower, width, hidden)
+    both = jnp.concatenate([b_hidden, w_head], axis=0)
+    far_matrix, far_both = swap(matrix), swap(both)
     arrived = exchange(slots)
+    arrived, far_both = lax.optimization_barrier((arrived, far_both))
     send, pos, given = call(
         functools.partial(compact_kernel, arms, packed),
         (sds((tower, rows, width), BF16), sds((8, total), I32), sds((arms, width), BF16)),
-        outs=[HBM, VMEM, VMEM],
-        scratch=[VMEM((2, rows, width), BF16), DMA((tower,))],
         flops=2 * total * packed * width,
     )(arrived.reshape(arms, SLOT, width))
-    matrix = w_hidden.reshape(tower, width, hidden)
-    both = jnp.concatenate([b_hidden, w_head], axis=0)
+    send, far_matrix = lax.optimization_barrier((send, far_matrix))
     inputs = spread(send)
-    far_matrix, far_both = swap(matrix), swap(both)
-    side, far_matrix = call(
-        functools.partial(prepare_kernel, arms, packed),
-        (sds((8, packed), F32), sds((tower, width, hidden), BF16)),
-        ins=[VMEM, VMEM, HBM],
-        outs=[VMEM, PIN],
-        scratch=[DMA],
-        flops=4 * total * packed * arms,
-    )(given, pos, far_matrix)
     (msg,) = call(
         forward_kernel,
         (sds((tower, rows + EXTRA, width), BF16),),
-        ins=[VMEM, VMEM, PIN, VMEM, VMEM],
+        ins=[VMEM] * 5,
         outs=[HBM],
         scratch=[
             VMEM((tower, rows + EXTRA, width), BF16), DMA((tower,)),
@@ -318,8 +302,13 @@
         flops=8 * rows * tower * width * hidden,
     )(inputs, matrix, far_matrix, both, far_both)
     got = spread(msg)
-    msg, inputs2 = lax.optimization_barrier((msg, inputs))
-    far_inputs = swap(inputs2)
+    msg, later, pos, given = lax.optimization_barrier((msg, inputs, pos, given))
+    far_inputs = swap(later)
+    (side,) = call(
+        functools.partial(prepare_kernel, arms, packed),
+        (sds((8, packed), F32),),
+        flops=4 * total * packed * arms,
+    )(given, pos)
     back_slots, resid = call(
         functools.partial(back_kernel, arms),
         (sds((total, width), BF16), sds((8, packed), F32)),

time: 111 us -> 110 us (level)
  blocking collectives: 0 us -> 20.2 us
  waiting for transfers between devices: 57.4 us -> 43.2 us
  starting transfers between devices: 36.2 us -> 31.9 us
  Pallas kernels: 14.8 us -> 13 us
    all_to_all x0 -> x1, blocking collectives: none -> 20.2 us  [spread(): lax.all_to_all(blocks, 'tower', split_axis=0, concat_axis=0, tiled=True)]
    all_to_all x2 -> x1, waiting for transfers between devices: 24.9 us -> 13.1 us  [spread(): lax.all_to_all(blocks, 'tower', split_axis=0, concat_axis=0, tiled=True)]
    all_to_all x2 -> x1, starting transfers between devices: 7.89 us -> 3.57 us  [spread(): lax.all_to_all(blocks, 'tower', split_axis=0, concat_axis=0, tiled=True)]
    all_to_all x2, waiting for transfers between devices: 32.5 us -> 29.3 us  [exchange(): lax.all_to_all(cut, 'dp', split_axis=0, concat_axis=0, tiled=True)]
    pallas_call x7, Pallas kernels: 14.8 us -> 13 us  [run(): pl.pallas_call(kernel, out_shape=[forced[m](o.shape, o.dtype) if m in for...]
  transfers between devices with their start and end apart: 7 -> 6, of which waited for: 4 -> 4; matrix products, arithmetic and copies ran while one was open for 0% -> 0% of each run, Pallas kernels for 8% -> 7%
where the time goes in v5:
time: 110 us
  waiting for transfers between devices  43.2 us (39%)
  starting transfers between devices  31.9 us (29%)
  blocking collectives  20.2 us (18%)
  Pallas kernels  13 us (12%)
  between operations  1.45 us (1%)
    all_to_all x2, waiting for transfers between devices, exchange(): lax.all_to_all(cut, 'dp', split_axis=0, concat_axis=0, tiled=True)  29.3 us
    all_to_all x2, starting transfers between devices, exchange(): lax.all_to_all(cut, 'dp', split_axis=0, concat_axis=0, tiled=True)  21.7 us
    all_to_all x1, blocking collectives, spread(): lax.all_to_all(blocks, 'tower', split_axis=0, concat_axis=0, tiled=True)  20.2 us
    all_to_all x1, waiting for transfers between devices, spread(): lax.all_to_all(blocks, 'tower', split_axis=0, concat_axis=0, tiled=True)  13.1 us
    pallas_call x7, Pallas kernels, run(): pl.pallas_call(kernel, out_shape=[forced[m](o.shape, o.dtype) if m in for...  13 us
    ppermute x3, starting transfers between devices, swap(): return lax.ppermute(value, 'tower', [(i, i ^ 1) for i in range(tower)])  6.63 us
    all_to_all x1, starting transfers between devices, spread(): lax.all_to_all(blocks, 'tower', split_axis=0, concat_axis=0, tiled=True)  3.57 us
  transfers between devices with their start and end apart: 6, of which 4 were waited for; matrix products, arithmetic and copies ran while one was open for 0% of the time, Pallas kernels for 7%

profile of v5, /device:TPU:16, one launch (start us, length us, event | category | flops | bytes accessed | tf_op | source)
XLA Modules:
  0.0 109.8 jit_solution(10929268242740078447)
XLA Ops:
  0.6 0.0 copy-start
  0.6 0.0 copy-start.1
  0.7 0.0 copy-start.2
  0.7 2.3 %shard_map.127 = (bf16[1024,256]{1,0:T(8,128)(2,1)}, s32[8,256]{1,0:T(8,128)S(1)}) custom-call(s32[1,256]{1,0:T(1,128)} %bitcast.15, bf16[256]{0:T(256)(128)(2,1)} %outcome_hbm.1, bf16[256]{0:T(256)(128)(2,1)} %weight_hbm.1, bf16[256,256]{1,0:T(8,128)(2,1)} %rep_hbm.1), custom_call_target="tpu_custom_call" | custom-call | flops 134217728 | tf_op jit(solution)/shard_map/pallas_call | solution.py:45
  3.0 16.5 %all-to-all-start = ((bf16[64,16,256]{2,1,0:T(8,128)(2,1)}), bf16[64,16,256]{2,1,0:T(8,128)(2,1)S(1)}, u32[]{:S(2)}, u32[]{:S(2)}) async-start(bf16[64,16,256]{2,1,0:T(8,128)(2,1)} %bitcast.14), calls=%async_computation | async-start | bytes 1048576 | tf_op jit(solution)/shard_map/all_to_all | solution.py:266
  19.5 0.0 copy-done
  19.5 1.9 %collective-permute-start.1 = (bf16[8,256,256]{2,1,0:T(8,128)(2,1)S(1)}, bf16[8,256,256]{2,1,0:T(8,128)(2,1)S(1)}, u32[]{:S(2)}, u32[]{:S(2)}) collective-permute-start(bf16[8,256,256]{2,1,0:T(8,128)(2,1)S(1)} %bitcast.10), channel_id=1, source_target_pairs={{0,1},{1,0},{2,3},{3,2},{4,5},{5,4},{6,7},{7,6},{8,9},{9,8},{10,11... | collective-permute-start | bytes 3145736 | tf_op jit(solution)/shard_map/ppermute | solution.py:262
  21.5 2.4 %collective-permute-start = (f32[2,256]{1,0:T(2,128)S(1)}, f32[2,256]{1,0:T(2,128)S(1)}, u32[]{:S(2)}, u32[]{:S(2)}) collective-permute-start(f32[2,256]{1,0:T(2,128)S(1)} %pad_maximum_fusion.bh_ref), channel_id=1, source_target_pairs={{0,1},{1,0},{2,3},{3,2},{4,5},{5,4},{6,7},{7,6},{8,9},{9,8},{10,11... | collective-permute-start | bytes 6152 | tf_op jit(solution)/shard_map/ppermute | solution.py:262
  23.9 0.8 collective-permute-done.far_bh_ref
  24.7 14.2 %all-to-all-done = bf16[64,16,256]{2,1,0:T(8,128)(2,1)S(1)} async-done(((bf16[64,16,256]{2,1,0:T(8,128)(2,1)}), bf16[64,16,256]{2,1,0:T(8,128)(2,1)S(1)}, u32[]{:S(2)}, u32[]{:S(2)}) %all-to-all-start) | async-done | bytes 524320 | tf_op jit(solution)/shard_map/all_to_all | solution.py:266
  38.9 0.9 shard_map.128
  39.8 0.0 collective-permute-done.1.far_ref
  39.8 20.2 %all_to_all.20.x_ref = bf16[8,256,256]{2,1,0:T(8,128)(2,1)S(1)} all-to-all(bf16[8,256,256]{2,1,0:T(8,128)(2,1)S(1)} %get-tuple-element.29), channel_id=1, replica_groups=mesh['dp'=64,'tower'=8] {'tower'}, dimensions={0} | all-to-all | bytes 2097152 | tf_op jit(solution)/shard_map/all_to_all | solution.py:269
  60.0 2.3 %shard_map.129 = bf16[8,272,256]{2,1,0:T(8,128)(2,1)} custom-call(bf16[8,256,256]{2,1,0:T(8,128)(2,1)S(1)} %all_to_all.20.x_ref, bf16[8,256,256]{2,1,0:T(8,128)(2,1)S(1)} %bitcast.11, bf16[8,256,256]{2,1,0:T(8,128)(2,1)S(1)} %collective-permute-done.1.far_ref, f32[2,256]{1,0:T(2,128)S(1)} %pad_maximum_fusion.bh_ref, f32[2,256]{1,0:T(2,128)S(1)} %collective-permute-done.far_bh_ref), custom_call_target="tpu_custom_call" | custom-call | flops 1073741824 | tf_op jit(solution)/shard_map/pallas_call | solution.py:45
  62.3 3.6 %all-to-all-start.2 = ((bf16[8,272,256]{2,1,0:T(8,128)(2,1)}), bf16[8,272,256]{2,1,0:T(8,128)(2,1)S(1)}, u32[]{:S(2)}, u32[]{:S(2)}) async-start(bf16[8,272,256]{2,1,0:T(8,128)(2,1)} %shard_map.129), calls=%async_computation.2 | async-start | bytes 2228224 | tf_op jit(solution)/shard_map/all_to_all | solution.py:269
  65.9 2.3 %collective-permute-start.2 = (bf16[8,256,256]{2,1,0:T(8,128)(2,1)S(1)}, bf16[8,256,256]{2,1,0:T(8,128)(2,1)}, u32[]{:S(2)}, u32[]{:S(2)}) collective-permute-start(bf16[8,256,256]{2,1,0:T(8,128)(2,1)S(1)} %all_to_all.20.x_ref), channel_id=1, source_target_pairs={{0,1},{1,0},{2,3},{3,2},{4,5},{5,4},{6,7},{7,6},{8,9},{9,8},{10,11... | collective-permute-start | bytes 3145736 | tf_op jit(solution)/shard_map/ppermute | solution.py:262
  68.8 0.5 shard_map.130.side_ref
  69.3 13.1 %all-to-all-done.2.got_ref = bf16[8,272,256]{2,1,0:T(8,128)(2,1)S(1)} async-done(((bf16[8,272,256]{2,1,0:T(8,128)(2,1)}), bf16[8,272,256]{2,1,0:T(8,128)(2,1)S(1)}, u32[]{:S(2)}, u32[]{:S(2)}) %all-to-all-start.2) | async-done | bytes 1114144 | tf_op jit(solution)/shard_map/all_to_all | solution.py:269
  82.4 1.8 %shard_map.131 = (bf16[1024,256]{1,0:T(8,128)(2,1)}, f32[8,512]{1,0:T(8,128)S(1)}) custom-call(f32[1]{0:T(128)S(6)} %copy.14.bias_ref, bf16[8,272,256]{2,1,0:T(8,128)(2,1)S(1)} %all-to-all-done.2.got_ref, f32[8,512]{1,0:T(8,128)S(1)} %shard_map.130.side_ref, s32[8,1024]{1,0:T(8,128)S(1)} %get-tuple-element.36.pos_ref), custom_call_target="tpu_custom_call" | custom-call | flops 268435456 | tf_op jit(solution)/shard_map/pallas_call | solution.py:45
  84.3 5.2 %all-to-all-start.3 = ((bf16[64,16,256]{2,1,0:T(8,128)(2,1)}), bf16[64,16,256]{2,1,0:T(8,128)(2,1)S(1)}, u32[]{:S(2)}, u32[]{:S(2)}) async-start(bf16[64,16,256]{2,1,0:T(8,128)(2,1)} %bitcast.13), calls=%async_computation.3 | async-start | bytes 1048576 | tf_op jit(solution)/shard_map/all_to_all | solution.py:266
  89.5 0.0 collective-permute-done.2.far_x_ref
  89.5 4.1 %shard_map.132 = (f32[8,256,256]{2,1,0:T(8,128)}, f32[1,256]{1,0:T(1,128)}, f32[1,256]{1,0:T(1,128)}, f32[1]{0:T(128)}) custom-call(s32[1]{0:T(128)} %bitcast.core_ref, bf16[8,256,256]{2,1,0:T(8,128)(2,1)S(1)} %all_to_all.20.x_ref, bf16[8,256,256]{2,1,0:T(8,128)(2,1)} %collective-permute-done.2.far_x_ref, bf16[8,256,256]{2,1,0:T(8,128)(2,1)S(1)} %bitcast.12, ...), custom_call_target="tpu_custom_call" | custom-call | flops 1073741824 | bytes 5242880 | tf_op jit(solution)/shard_map/pallas_call | solution.py:45
  93.7 15.0 %all-to-all-done.3 = bf16[64,16,256]{2,1,0:T(8,128)(2,1)S(1)} async-done(((bf16[64,16,256]{2,1,0:T(8,128)(2,1)}), bf16[64,16,256]{2,1,0:T(8,128)(2,1)S(1)}, u32[]{:S(2)}, u32[]{:S(2)}) %all-to-all-start.3) | async-done | bytes 524320 | tf_op jit(solution)/shard_map/all_to_all | solution.py:266
  108.7 1.1 %shard_map.133 = (bf16[256,256]{1,0:T(8,128)(2,1)}, bf16[256]{0:T(256)(128)(2,1)}) custom-call(bf16[1024,256]{1,0:T(8,128)(2,1)S(1)} %bitcast.9, s32[8,256]{1,0:T(8,128)S(1)} %get-tuple-element.43.aux_ref), custom_call_target="tpu_custom_call" | custom-call | flops 134217728 | tf_op jit(solution)/shard_map/pallas_call | solution.py:45
  (3 shorter events, 0.0 us)
Async XLA Ops:
  0.6 18.9 %copy-start = (bf16[1,2048,256]{2,1,0:T(8,128)(2,1)S(1)}, bf16[1,2048,256]{2,1,0:T(8,128)(2,1)}, u32[]{:S(2)}) copy-start(bf16[1,2048,256]{2,1,0:T(8,128)(2,1)} %param.12) | copy-start | bytes 3145732
  0.6 20.8 %copy-start.1 = (f32[1,256]{1,0:T(1,128)S(1)}, f32[1,256]{1,0:T(1,128)}, u32[]{:S(2)}) copy-start(f32[1,256]{1,0:T(1,128)} %param.14) | copy-start | bytes 3076
  0.7 20.8 %copy-start.2 = (f32[1,256]{1,0:T(1,128)S(1)}, f32[1,256]{1,0:T(1,128)}, u32[]{:S(2)}) copy-start(f32[1,256]{1,0:T(1,128)} %param.13) | copy-start | bytes 3076
  3.0 35.9 %all-to-all-start = ((bf16[64,16,256]{2,1,0:T(8,128)(2,1)}), bf16[64,16,256]{2,1,0:T(8,128)(2,1)S(1)}, u32[]{:S(2)}, u32[]{:S(2)}) async-start(bf16[64,16,256]{2,1,0:T(8,128)(2,1)} %bitcast.14), calls=%async_computation | async-start | bytes 1048576 | tf_op jit(solution)/shard_map/all_to_all | solution.py:266
  19.5 20.3 %collective-permute-start.1 = (bf16[8,256,256]{2,1,0:T(8,128)(2,1)S(1)}, bf16[8,256,256]{2,1,0:T(8,128)(2,1)S(1)}, u32[]{:S(2)}, u32[]{:S(2)}) collective-permute-start(bf16[8,256,256]{2,1,0:T(8,128)(2,1)S(1)} %bitcast.10), channel_id=1, source_target_pairs={{0,1},{1,0},{2,3},{3,2},{4,5},{5,4},{6,7},{7,6},{8,9},{9,8},{10,11... | collective-permute-start | bytes 3145736 | tf_op jit(solution)/shard_map/ppermute | solution.py:262
  21.5 3.2 %collective-permute-start = (f32[2,256]{1,0:T(2,128)S(1)}, f32[2,256]{1,0:T(2,128)S(1)}, u32[]{:S(2)}, u32[]{:S(2)}) collective-permute-start(f32[2,256]{1,0:T(2,128)S(1)} %pad_maximum_fusion.bh_ref), channel_id=1, source_target_pairs={{0,1},{1,0},{2,3},{3,2},{4,5},{5,4},{6,7},{7,6},{8,9},{9,8},{10,11... | collective-permute-start | bytes 6152 | tf_op jit(solution)/shard_map/ppermute | solution.py:262
  62.3 20.2 %all-to-all-start.2 = ((bf16[8,272,256]{2,1,0:T(8,128)(2,1)}), bf16[8,272,256]{2,1,0:T(8,128)(2,1)S(1)}, u32[]{:S(2)}, u32[]{:S(2)}) async-start(bf16[8,272,256]{2,1,0:T(8,128)(2,1)} %shard_map.129), calls=%async_computation.2 | async-start | bytes 2228224 | tf_op jit(solution)/shard_map/all_to_all | solution.py:269
  65.9 23.7 %collective-permute-start.2 = (bf16[8,256,256]{2,1,0:T(8,128)(2,1)S(1)}, bf16[8,256,256]{2,1,0:T(8,128)(2,1)}, u32[]{:S(2)}, u32[]{:S(2)}) collective-permute-start(bf16[8,256,256]{2,1,0:T(8,128)(2,1)S(1)} %all_to_all.20.x_ref), channel_id=1, source_target_pairs={{0,1},{1,0},{2,3},{3,2},{4,5},{5,4},{6,7},{7,6},{8,9},{9,8},{10,11... | collective-permute-start | bytes 3145736 | tf_op jit(solution)/shard_map/ppermute | solution.py:262
  84.3 24.4 %all-to-all-start.3 = ((bf16[64,16,256]{2,1,0:T(8,128)(2,1)}), bf16[64,16,256]{2,1,0:T(8,128)(2,1)S(1)}, u32[]{:S(2)}, u32[]{:S(2)}) async-start(bf16[64,16,256]{2,1,0:T(8,128)(2,1)} %bitcast.13), calls=%async_computation.3 | async-start | bytes 1048576 | tf_op jit(solution)/shard_map/all_to_all | solution.py:266

commit v6 on v5

--- a/solution.py
+++ b/solution.py
@@ -10,7 +10,6 @@
 F32, BF16, I32 = jnp.float32, jnp.bfloat16, jnp.int32
 SLOT = 16
 SIDE = 14
-EXTRA = 16
 INTERPRET = False
 VMEM, SMEM, HBM = pltpu.VMEM, pltpu.SMEM, pltpu.HBM
 PIN = object()
@@ -101,9 +100,10 @@
     part = arms * SLOT // PARTS
     for i in range(PARTS):
         place = ones_where(iota((part, rows), 0) + i * part == slot)
-        mark = ones_where(iota((part, arms), 0) + i * part == iota((part, arms), 1) * SLOT + SIDE)
         cut = pl.ds(i * part, part)
-        slots_ref[cut, :] = (mm(place, rep) + mm(mark, side)).astype(BF16)
+        slots_ref[cut, :] = mm(place, rep).astype(BF16)
+        few = part // SLOT
+        slots_ref.reshape(arms, SLOT, width)[i * few : (i + 1) * few, SIDE, :] = side[i * few : (i + 1) * few]
         stores.append(pltpu.make_async_copy(slots_ref.at[cut], slots_hbm.at[cut], out_sem.at[i]))
         stores[-1].start()
     for store in stores:
@@ -136,8 +136,12 @@
             send_ref[d] = rows
 
 
-def prepare_kernel(arms, packed, given_ref, pos_ref, side_ref):
+def plan_kernel(arms, core_ref, bias_ref, mine_ref, other_ref, given_ref, pos_ref, resid_ref, pred_ref):
+    first = core_ref[0] == 0
     total, width = arms * SLOT, given_ref.shape[1]
+    mine, other = mine_ref[0:1], other_ref[0:1]
+    pred = jnp.concatenate([jnp.where(first, mine, other), jnp.where(first, other, mine)], axis=1) + bias_ref[0]
+    packed = pred.shape[1]
     side = given_ref[...]
     gather = ones_where(iota((packed, total), 0) == pos_ref[0:1])
     same = iota((arms, total), 0) == iota((arms, total), 1) // SLOT
@@ -147,7 +151,10 @@
     target = jnp.sum(jnp.where(same, target, 0.0), axis=0, keepdims=True)
     weight = jnp.sum(jnp.where(same, weight, 0.0), axis=0, keepdims=True)
     both = jnp.where(iota((8, total), 0) == 0, target, weight)
-    side_ref[...] = mm(both.astype(BF16), gather, NT)
+    both = mm(both.astype(BF16), gather, NT)
+    resid_ref[...] = jnp.broadcast_to(both[1:2] * (pred - both[0:1]), resid_ref.shape)
+    pred_slot = mm(jnp.broadcast_to(pred, (8, packed)).astype(BF16), gather)
+    pred_ref[...] = mm(jnp.where(same, pred_slot[0:1], 0.0).astype(BF16), ones_where(lane == place), NT).astype(BF16)
 
 
 def unit(pre, head):
@@ -156,59 +163,46 @@
 
 
 def forward_kernel(
-    x_ref, near_ref, far_ref, bh_ref, far_bh_ref, msg_hbm,
+    x_ref, near_ref, far_lo_ref, far_hi_ref, bh_ref, far_bh_ref, msg_hbm, share_ref,
     msg_ref, out_sem,
 ):
     blocks, rows, width = x_ref.shape
+    half = blocks // 2
+    far = [far_lo_ref.at[j] for j in range(half)] + [far_hi_ref.at[j] for j in range(half)]
     head, far_head = bh_ref[1:2], far_bh_ref[1:2]
     pre = sum(mm(x_ref[j], near_ref[j]) for j in range(blocks)) + bh_ref[0:1]
     act, g = unit(pre, head)
     g = g.astype(BF16)
-    pre = sum(mm(x_ref[j], far_ref[j]) for j in range(blocks)) + far_bh_ref[0:1]
+    pre = sum(mm(x_ref[j], far[j][...]) for j in range(blocks)) + far_bh_ref[0:1]
     far_act, far_g = unit(pre, far_head)
     far_g = far_g.astype(BF16)
     stores = []
     share = act * head + far_act * far_head
     cut = min(LANES, width)
     share = sum(share[:, i : i + cut] for i in range(0, width, cut))
-    share = jnp.sum(jnp.transpose(share), axis=0, keepdims=True)
-    high = share.astype(BF16).astype(F32)
-    row = iota((EXTRA, rows), 0)
-    extra = jnp.where(row == 0, high, jnp.where(row == 1, share - high, 0.0)).astype(BF16)
+    share_ref[...] = jnp.broadcast_to(jnp.sum(jnp.transpose(share), axis=0, keepdims=True), share_ref.shape)
     for j in range(blocks):
-        part = mm(g, near_ref[j], NT) + mm(far_g, far_ref[j], NT)
-        msg_ref[j, pl.ds(0, rows), :] = part.astype(BF16)
-        msg_ref[j, pl.ds(rows, EXTRA), pl.ds(0, rows)] = extra
+        part = mm(g, near_ref[j], NT) + mm(far_g, far[j][...], NT)
+        msg_ref[j] = part.astype(BF16)
         stores.append(pltpu.make_async_copy(msg_ref.at[j], msg_hbm.at[j], out_sem.at[j]))
         stores[-1].start()
     for store in stores:
         store.wait()
 
 
-def back_kernel(arms, bias_ref, got_ref, side_ref, pos_ref, slots_hbm, resid_ref, slots_ref, sem):
+def back_kernel(arms, got_ref, resid_ref, pred_ref, pos_ref, slots_hbm, slots_ref, sem):
     blocks, rows, width = got_ref.shape
-    rows = rows - EXTRA
     total = arms * SLOT
-    preds, grads = [], []
-    for half in range(2):
-        extra = sum(got_ref[j, pl.ds(rows, EXTRA), pl.ds(0, rows)].astype(F32) for j in range(half, blocks, 2))
-        preds.append(extra[0:1] + extra[1:2])
-        grads.append(sum(got_ref[j, pl.ds(0, rows), :].astype(F32) for j in range(half, blocks, 2)))
-    pred = jnp.concatenate(preds, axis=1) + bias_ref[0]
-    resid = side_ref[1:2] * (pred - side_ref[0:1])
-    resid_ref[...] = jnp.broadcast_to(resid, resid_ref.shape)
-    grad = (jnp.concatenate(grads, axis=0) * column(resid)[:, 0:1]).astype(BF16)
-    pred = jnp.broadcast_to(pred, (8, 2 * rows)).astype(BF16)
+    grads = [sum(got_ref[j].astype(F32) for j in range(half, blocks, 2)) for half in range(2)]
+    grad = (jnp.concatenate(grads, axis=0) * column(resid_ref[0:1])[:, 0:1]).astype(BF16)
     stores = []
     part = total // PARTS
     for i in range(PARTS):
         cut = pl.ds(i * part, part)
         gather = ones_where(iota((2 * rows, part), 0) == pos_ref[0:1, i * part : (i + 1) * part])
-        pred_slot = mm(pred, gather)[0:1]
-        row, slot = iota((part, part), 0), iota((part, part), 1)
-        spread = jnp.where((row % SLOT == SIDE) & (row // SLOT == slot // SLOT), pred_slot, 0.0).astype(BF16)
-        lane = ones_where(iota((width, part), 0) == iota((width, part), 1) % SLOT)
-        slots_ref[cut, :] = (mm(gather, grad, TN) + mm(spread, lane, NT)).astype(BF16)
+        slots_ref[cut, :] = mm(gather, grad, TN).astype(BF16)
+        few = part // SLOT
+        slots_ref.reshape(arms, SLOT, width)[i * few : (i + 1) * few, SIDE, :] = pred_ref[i * few : (i + 1) * few]
         stores.append(pltpu.make_async_copy(slots_ref.at[cut], slots_hbm.at[cut], sem.at[i]))
         stores[-1].start()
     for store in stores:
@@ -221,7 +215,7 @@
     slots = slots_ref[...]
     place = ones_where(iota((total, rows), 0) == aux_ref[0:1])
     grad_ref[...] = mm(place, slots, TN).astype(BF16)
-    pred_side = side_of(slots, arms).astype(BF16)
+    pred_side = slots_ref.reshape(arms, SLOT, width)[:, SIDE, :]
     by_arm = mm(pred_side, ones_where(iota((width, rows), 0) == aux_ref[1:2]))
     hot = iota((arms, rows), 0) == aux_ref[2:3]
     pred = jnp.sum(jnp.where(hot, by_arm, 0.0), axis=0, keepdims=True)
@@ -258,6 +252,9 @@
     hidden = w_hidden.shape[2]
     core = (lax.axis_index("tower") % 2).astype(I32).reshape(1)
 
+    def hop(value, by):
+        return lax.ppermute(value, "tower", [(i, (i + 2 * by) % tower) for i in range(tower)])
+
     def swap(value):
         return lax.ppermute(value, "tower", [(i, i ^ 1) for i in range(tower)])
 
@@ -281,42 +278,42 @@
     )(arm_ids.reshape(1, rows), outcome, weight, rep)
     matrix = w_hidden.reshape(tower, width, hidden)
     both = jnp.concatenate([b_hidden, w_head], axis=0)
-    far_matrix, far_both = swap(matrix), swap(both)
+    far_lo, far_hi, far_both = swap(matrix[: tower // 2]), swap(matrix[tower // 2 :]), swap(both)
     arrived = exchange(slots)
-    arrived, far_both = lax.optimization_barrier((arrived, far_both))
+    arrived, far_lo, far_hi, far_both = lax.optimization_barrier((arrived, far_lo, far_hi, far_both))
     send, pos, given = call(
         functools.partial(compact_kernel, arms, packed),
         (sds((tower, rows, width), BF16), sds((8, total), I32), sds((arms, width), BF16)),
         flops=2 * total * packed * width,
     )(arrived.reshape(arms, SLOT, width))
-    send, far_matrix = lax.optimization_barrier((send, far_matrix))
     inputs = spread(send)
-    (msg,) = call(
+    msg, share = call(
         forward_kernel,
-        (sds((tower, rows + EXTRA, width), BF16),),
-        ins=[VMEM] * 5,
-        outs=[HBM],
+        (sds((tower, rows, width), BF16), sds((8, rows), F32)),
+        ins=[VMEM] * 6,
+        outs=[HBM, VMEM],
         scratch=[
-            VMEM((tower, rows + EXTRA, width), BF16), DMA((tower,)),
+            VMEM((tower, rows, width), BF16), DMA((tower,)),
         ],
         flops=8 * rows * tower * width * hidden,
-    )(inputs, matrix, far_matrix, both, far_both)
+    )(inputs, matrix, far_lo, far_hi, both, far_both)
     got = spread(msg)
-    msg, later, pos, given = lax.optimization_barrier((msg, inputs, pos, given))
+    msg, later, pos, given, share = lax.optimization_barrier((msg, inputs, pos, given, share))
+    mine = (share + hop(share, 2)) + (hop(share, 1) + hop(share, -1))
+    resid, pred_side = call(
+        functools.partial(plan_kernel, arms),
+        (sds((8, packed), F32), sds((arms, width), BF16)),
+        ins=[SMEM, SMEM] + [VMEM] * 4,
+        flops=4 * total * packed * arms,
+    )(core, b_head, mine, swap(mine), given, pos)
     far_inputs = swap(later)
-    (side,) = call(
-        functools.partial(prepare_kernel, arms, packed),
-        (sds((8, packed), F32),),
-        flops=4 * total * packed * arms,
-    )(given, pos)
-    back_slots, resid = call(
+    (back_slots,) = call(
         functools.partial(back_kernel, arms),
-        (sds((total, width), BF16), sds((8, packed), F32)),
-        ins=[SMEM, VMEM, VMEM, VMEM],
-        outs=[HBM, VMEM],
+        (sds((total, width), BF16),),
+        outs=[HBM],
         scratch=[VMEM((total, width), BF16), DMA((PARTS,))],
         flops=2 * total * packed * width,
-    )(b_head, got, side, pos)
+    )(got, resid, pred_side, pos)
     returned = exchange(back_slots)
     grad_matrix, grad_bias, grad_vector, grad_scalar = call(
         grads_kernel,

time: 110 us -> 114 us (1.036)
  starting transfers between devices: 31.9 us -> 46.5 us
  waiting for transfers between devices: 43.2 us -> 32.2 us
    all_to_all x1, waiting for transfers between devices: 13.1 us -> 0.01 us  [spread(): lax.all_to_all(blocks, 'tower', split_axis=0, concat_axis=0, tiled=True)]
    ppermute x0 -> x3, starting transfers between devices: none -> 11.2 us  [hop(): lax.ppermute(value, 'tower', [(i, (i + 2 * by) % tower) for i in range(to...]
    ppermute x3 -> x5, starting transfers between devices: 6.63 us -> 10.1 us  [swap(): return lax.ppermute(value, 'tower', [(i, i ^ 1) for i in range(tower)])]
    ppermute x0 -> x3, waiting for transfers between devices: none -> 3.1 us  [hop(): lax.ppermute(value, 'tower', [(i, (i + 2 * by) % tower) for i in range(to...]
    all_to_all x2, waiting for transfers between devices: 29.3 us -> 27.5 us  [exchange(): lax.all_to_all(cut, 'dp', split_axis=0, concat_axis=0, tiled=True)]
  transfers between devices with their start and end apart: 6 -> 11, of which waited for: 4 -> 6; matrix products, arithmetic and copies ran while one was open for 0% -> 0% of each run, Pallas kernels for 7% -> 6%
where the time goes in v6:
time: 114 us; the launch traced here: 113 us
  starting transfers between devices  46.5 us (41%)
  waiting for transfers between devices  32.2 us (28%)
  blocking collectives  20.3 us (18%)
  Pallas kernels  12.8 us (11%)
  between operations  1.53 us (1%)
    all_to_all x2, waiting for transfers between devices, exchange(): lax.all_to_all(cut, 'dp', split_axis=0, concat_axis=0, tiled=True)  27.5 us
    all_to_all x2, starting transfers between devices, exchange(): lax.all_to_all(cut, 'dp', split_axis=0, concat_axis=0, tiled=True)  21.7 us
    all_to_all x1, blocking collectives, spread(): lax.all_to_all(blocks, 'tower', split_axis=0, concat_axis=0, tiled=True)  20.3 us
    pallas_call x7, Pallas kernels, run(): pl.pallas_call(kernel, out_shape=[forced[m](o.shape, o.dtype) if m in for...  12.8 us
    ppermute x3, starting transfers between devices, hop(): lax.ppermute(value, 'tower', [(i, (i + 2 * by) % tower) for i in range(to...  11.2 us
    ppermute x5, starting transfers between devices, swap(): return lax.ppermute(value, 'tower', [(i, i ^ 1) for i in range(tower)])  10.1 us
    all_to_all x1, starting transfers between devices, spread(): lax.all_to_all(blocks, 'tower', split_axis=0, concat_axis=0, tiled=True)  3.57 us
    ppermute x3, waiting for transfers between devices, hop(): lax.ppermute(value, 'tower', [(i, (i + 2 * by) % tower) for i in range(to...  3.1 us
  transfers between devices with their start and end apart: 11, of which 6 were waited for; matrix products, arithmetic and copies ran while one was open for 0% of the time, Pallas kernels for 6%

profile of v6, /device:TPU:16, one launch (start us, length us, event | category | flops | bytes accessed | tf_op | source)
XLA Modules:
  0.0 113.5 jit_solution(4383145348350658954)
XLA Ops:
  0.7 2.3 %shard_map.127 = (bf16[1024,256]{1,0:T(8,128)(2,1)}, s32[8,256]{1,0:T(8,128)S(1)}) custom-call(s32[1,256]{1,0:T(1,128)} %bitcast.18, bf16[256]{0:T(256)(128)(2,1)} %outcome_hbm.1, bf16[256]{0:T(256)(128)(2,1)} %weight_hbm.1, bf16[256,256]{1,0:T(8,128)(2,1)} %rep_hbm.1), custom_call_target="tpu_custom_call" | custom-call | flops 134217728 | tf_op jit(solution)/shard_map/pallas_call | solution.py:44
  2.9 16.5 %all-to-all-start = ((bf16[64,16,256]{2,1,0:T(8,128)(2,1)}), bf16[64,16,256]{2,1,0:T(8,128)(2,1)S(1)}, u32[]{:S(2)}, u32[]{:S(2)}) async-start(bf16[64,16,256]{2,1,0:T(8,128)(2,1)} %bitcast.15), calls=%async_computation | async-start | bytes 1048576 | tf_op jit(solution)/shard_map/all_to_all | solution.py:263
  19.5 1.9 %collective-permute-start = (bf16[4,256,256]{2,1,0:T(8,128)(2,1)S(1)}, bf16[4,256,256]{2,1,0:T(8,128)(2,1)S(1)}, u32[]{:S(2)}, u32[]{:S(2)}) collective-permute-start(bf16[4,256,256]{2,1,0:T(8,128)(2,1)S(1)} %bitcast.17), channel_id=1, source_target_pairs={{0,1},{1,0},{2,3},{3,2},{4,5},{5,4},{6,7},{7,6},{8,9},{9,8},{10,11... | collective-permute-start | bytes 1572872 | tf_op jit(solution)/shard_map/ppermute | solution.py:259
  21.5 2.4 %collective-permute-start.1 = (bf16[4,256,256]{2,1,0:T(8,128)(2,1)S(1)}, bf16[4,256,256]{2,1,0:T(8,128)(2,1)S(1)}, u32[]{:S(2)}, u32[]{:S(2)}) collective-permute-start(bf16[4,256,256]{2,1,0:T(8,128)(2,1)S(1)} %bitcast.16), channel_id=1, source_target_pairs={{0,1},{1,0},{2,3},{3,2},{4,5},{5,4},{6,7},{7,6},{8,9},{9,8},{10,11... | collective-permute-start | bytes 1572872 | tf_op jit(solution)/shard_map/ppermute | solution.py:259
  23.9 1.9 %collective-permute-start.2 = (f32[2,256]{1,0:T(2,128)S(1)}, f32[2,256]{1,0:T(2,128)S(1)}, u32[]{:S(2)}, u32[]{:S(2)}) collective-permute-start(f32[2,256]{1,0:T(2,128)S(1)} %pad_maximum_fusion.bh_ref), channel_id=1, source_target_pairs={{0,1},{1,0},{2,3},{3,2},{4,5},{5,4},{6,7},{7,6},{8,9},{9,8},{10,11... | collective-permute-start | bytes 6152 | tf_op jit(solution)/shard_map/ppermute | solution.py:259
  25.8 1.1 collective-permute-done.2.far_bh_ref
  27.0 11.9 %all-to-all-done = bf16[64,16,256]{2,1,0:T(8,128)(2,1)S(1)} async-done(((bf16[64,16,256]{2,1,0:T(8,128)(2,1)}), bf16[64,16,256]{2,1,0:T(8,128)(2,1)S(1)}, u32[]{:S(2)}, u32[]{:S(2)}) %all-to-all-start) | async-done | bytes 524320 | tf_op jit(solution)/shard_map/all_to_all | solution.py:263
  38.9 0.9 shard_map.128
  39.7 20.3 %all_to_all.20.x_ref = bf16[8,256,256]{2,1,0:T(8,128)(2,1)S(1)} all-to-all(bf16[8,256,256]{2,1,0:T(8,128)(2,1)S(1)} %get-tuple-element.31), channel_id=1, replica_groups=mesh['dp'=64,'tower'=8] {'tower'}, dimensions={0} | all-to-all | bytes 2097152 | tf_op jit(solution)/shard_map/all_to_all | solution.py:266
  60.1 2.3 %shard_map.129 = (bf16[8,256,256]{2,1,0:T(8,128)(2,1)}, f32[8,256]{1,0:T(8,128)S(1)}) custom-call(bf16[8,256,256]{2,1,0:T(8,128)(2,1)S(1)} %all_to_all.20.x_ref, bf16[8,256,256]{2,1,0:T(8,128)(2,1)S(1)} %bitcast.12, bf16[4,256,256]{2,1,0:T(8,128)(2,1)S(1)} %collective-permute-done.far_lo_ref, bf16[4,256,256]{2,1,0:T(8,128)(2,1)S(1)} %copy-done.2, ...), custom_call_target="tpu_custom_call" | custom-call | flops 1073741824 | tf_op jit(solution)/shard_map/pallas_call | solution.py:44
  62.3 3.6 %all-to-all-start.2 = ((bf16[8,256,256]{2,1,0:T(8,128)(2,1)}), bf16[8,256,256]{2,1,0:T(8,128)(2,1)S(1)}, u32[]{:S(2)}, u32[]{:S(2)}) async-start(bf16[8,256,256]{2,1,0:T(8,128)(2,1)} %get-tuple-element.35), calls=%async_computation.2 | async-start | bytes 2097152 | tf_op jit(solution)/shard_map/all_to_all | solution.py:266
  65.9 5.1 %collective-permute-start.6 = (f32[8,256]{1,0:T(8,128)S(1)}, f32[8,256]{1,0:T(8,128)S(1)}, u32[]{:S(2)}, u32[]{:S(2)}) collective-permute-start(f32[8,256]{1,0:T(8,128)S(1)} %get-tuple-element.40), channel_id=1, source_target_pairs={{0,6},{1,7},{2,0},{3,1},{4,2},{5,3},{6,4},{7,5},{8,14},{9,15},{10,... | collective-permute-start | bytes 24584 | tf_op jit(solution)/shard_map/ppermute | solution.py:256
  71.0 1.9 %collective-permute-start.5 = (f32[8,256]{1,0:T(8,128)S(1)}, f32[8,256]{1,0:T(8,128)S(1)}, u32[]{:S(2)}, u32[]{:S(2)}) collective-permute-start(f32[8,256]{1,0:T(8,128)S(1)} %get-tuple-element.40), channel_id=1, source_target_pairs={{0,2},{1,3},{2,4},{3,5},{4,6},{5,7},{6,0},{7,1},{8,10},{9,11},{10,... | collective-permute-start | bytes 24584 | tf_op jit(solution)/shard_map/ppermute | solution.py:256
  72.9 4.2 %collective-permute-start.4 = (f32[8,256]{1,0:T(8,128)S(1)}, f32[8,256]{1,0:T(8,128)S(1)}, u32[]{:S(2)}, u32[]{:S(2)}) collective-permute-start(f32[8,256]{1,0:T(8,128)S(1)} %get-tuple-element.40), channel_id=1, source_target_pairs={{0,4},{1,5},{2,6},{3,7},{4,0},{5,1},{6,2},{7,3},{8,12},{9,13},{10,... | collective-permute-start | bytes 24584 | tf_op jit(solution)/shard_map/ppermute | solution.py:256
  77.1 1.9 %collective-permute-start.3 = (bf16[8,256,256]{2,1,0:T(8,128)(2,1)S(1)}, bf16[8,256,256]{2,1,0:T(8,128)(2,1)}, u32[]{:S(2)}, u32[]{:S(2)}) collective-permute-start(bf16[8,256,256]{2,1,0:T(8,128)(2,1)S(1)} %all_to_all.20.x_ref), channel_id=1, source_target_pairs={{0,1},{1,0},{2,3},{3,2},{4,5},{5,4},{6,7},{7,6},{8,9},{9,8},{10,11... | collective-permute-start | bytes 3145736 | tf_op jit(solution)/shard_map/ppermute | solution.py:259
  79.0 1.5 %collective-permute-done.6 = f32[8,256]{1,0:T(8,128)S(1)} collective-permute-done((f32[8,256]{1,0:T(8,128)S(1)}, f32[8,256]{1,0:T(8,128)S(1)}, u32[]{:S(2)}, u32[]{:S(2)}) %collective-permute-start.6) | collective-permute-done | bytes 8224 | tf_op jit(solution)/shard_map/ppermute | solution.py:256
  80.5 1.6 %collective-permute-done.4 = f32[8,256]{1,0:T(8,128)S(1)} collective-permute-done((f32[8,256]{1,0:T(8,128)S(1)}, f32[8,256]{1,0:T(8,128)S(1)}, u32[]{:S(2)}, u32[]{:S(2)}) %collective-permute-start.4) | collective-permute-done | bytes 8224 | tf_op jit(solution)/shard_map/ppermute | solution.py:256
  82.1 1.9 %collective-permute-start.7 = (f32[8,256]{1,0:T(8,128)S(1)}, f32[8,256]{1,0:T(8,128)S(1)}, u32[]{:S(2)}, u32[]{:S(2)}) collective-permute-start(f32[8,256]{1,0:T(8,128)S(1)} %add_add_fusion.mine_ref), channel_id=1, source_target_pairs={{0,1},{1,0},{2,3},{3,2},{4,5},{5,4},{6,7},{7,6},{8,9},{9,8},{10,11... | collective-permute-start | bytes 24584 | tf_op jit(solution)/shard_map/ppermute | solution.py:259
  85.2 0.8 shard_map.130
  86.0 1.5 %shard_map.132 = bf16[1024,256]{1,0:T(8,128)(2,1)} custom-call(bf16[8,256,256]{2,1,0:T(8,128)(2,1)S(1)} %all-to-all-done.2.got_ref, f32[8,512]{1,0:T(8,128)S(1)} %get-tuple-element.43.resid_ref, bf16[64,256]{1,0:T(8,128)(2,1)S(1)} %get-tuple-element.48.pred_ref, s32[8,1024]{1,0:T(8,128)S(1)} %get-tuple-element.42.pos_ref), custom_call_target="tpu_custom_call" | custom-call | flops 268435456 | tf_op jit(solution)/shard_map/pallas_call | solution.py:44
  87.5 5.2 %all-to-all-start.3 = ((bf16[64,16,256]{2,1,0:T(8,128)(2,1)}), bf16[64,16,256]{2,1,0:T(8,128)(2,1)S(1)}, u32[]{:S(2)}, u32[]{:S(2)}) async-start(bf16[64,16,256]{2,1,0:T(8,128)(2,1)} %bitcast.14), calls=%async_computation.3 | async-start | bytes 1048576 | tf_op jit(solution)/shard_map/all_to_all | solution.py:263
  92.7 4.1 %shard_map.131 = (f32[8,256,256]{2,1,0:T(8,128)}, f32[1,256]{1,0:T(1,128)}, f32[1,256]{1,0:T(1,128)}, f32[1]{0:T(128)}) custom-call(s32[1]{0:T(128)} %bitcast.core_ref, bf16[8,256,256]{2,1,0:T(8,128)(2,1)S(1)} %all_to_all.20.x_ref, bf16[8,256,256]{2,1,0:T(8,128)(2,1)} %collective-permute-done.3.far_x_ref, bf16[8,256,256]{2,1,0:T(8,128)(2,1)S(1)} %bitcast.13, ...), custom_call_target="tpu_custom_call" | custom-call | flops 1073741824 | bytes 5242880 | tf_op jit(solution)/shard_map/pallas_call | solution.py:44
  96.9 15.6 %all-to-all-done.3 = bf16[64,16,256]{2,1,0:T(8,128)(2,1)S(1)} async-done(((bf16[64,16,256]{2,1,0:T(8,128)(2,1)}), bf16[64,16,256]{2,1,0:T(8,128)(2,1)S(1)}, u32[]{:S(2)}, u32[]{:S(2)}) %all-to-all-start.3) | async-done | bytes 524320 | tf_op jit(solution)/shard_map/all_to_all | solution.py:263
  112.4 1.0 shard_map.133
  (19 shorter events, 0.6 us)
Async XLA Ops:
  0.6 18.8 %copy-start = (bf16[1,2048,256]{2,1,0:T(8,128)(2,1)S(1)}, bf16[1,2048,256]{2,1,0:T(8,128)(2,1)}, u32[]{:S(2)}) copy-start(bf16[1,2048,256]{2,1,0:T(8,128)(2,1)} %param.12) | copy-start | bytes 3145732
  0.6 23.2 %copy-start.3 = (f32[1,256]{1,0:T(1,128)S(1)}, f32[1,256]{1,0:T(1,128)}, u32[]{:S(2)}) copy-start(f32[1,256]{1,0:T(1,128)} %param.14) | copy-start | bytes 3076
  0.7 23.2 %copy-start.4 = (f32[1,256]{1,0:T(1,128)S(1)}, f32[1,256]{1,0:T(1,128)}, u32[]{:S(2)}) copy-start(f32[1,256]{1,0:T(1,128)} %param.13) | copy-start | bytes 3076
  2.9 35.9 %all-to-all-start = ((bf16[64,16,256]{2,1,0:T(8,128)(2,1)}), bf16[64,16,256]{2,1,0:T(8,128)(2,1)S(1)}, u32[]{:S(2)}, u32[]{:S(2)}) async-start(bf16[64,16,256]{2,1,0:T(8,128)(2,1)} %bitcast.15), calls=%async_computation | async-start | bytes 1048576 | tf_op jit(solution)/shard_map/all_to_all | solution.py:263
  19.5 7.4 %collective-permute-start = (bf16[4,256,256]{2,1,0:T(8,128)(2,1)S(1)}, bf16[4,256,256]{2,1,0:T(8,128)(2,1)S(1)}, u32[]{:S(2)}, u32[]{:S(2)}) collective-permute-start(bf16[4,256,256]{2,1,0:T(8,128)(2,1)S(1)} %bitcast.17), channel_id=1, source_target_pairs={{0,1},{1,0},{2,3},{3,2},{4,5},{5,4},{6,7},{7,6},{8,9},{9,8},{10,11... | collective-permute-start | bytes 1572872 | tf_op jit(solution)/shard_map/ppermute | solution.py:259
  21.5 5.5 %collective-permute-start.1 = (bf16[4,256,256]{2,1,0:T(8,128)(2,1)S(1)}, bf16[4,256,256]{2,1,0:T(8,128)(2,1)S(1)}, u32[]{:S(2)}, u32[]{:S(2)}) collective-permute-start(bf16[4,256,256]{2,1,0:T(8,128)(2,1)S(1)} %bitcast.16), channel_id=1, source_target_pairs={{0,1},{1,0},{2,3},{3,2},{4,5},{5,4},{6,7},{7,6},{8,9},{9,8},{10,11... | collective-permute-start | bytes 1572872 | tf_op jit(solution)/shard_map/ppermute | solution.py:259
  23.9 3.1 %collective-permute-start.2 = (f32[2,256]{1,0:T(2,128)S(1)}, f32[2,256]{1,0:T(2,128)S(1)}, u32[]{:S(2)}, u32[]{:S(2)}) collective-permute-start(f32[2,256]{1,0:T(2,128)S(1)} %pad_maximum_fusion.bh_ref), channel_id=1, source_target_pairs={{0,1},{1,0},{2,3},{3,2},{4,5},{5,4},{6,7},{7,6},{8,9},{9,8},{10,11... | collective-permute-start | bytes 6152 | tf_op jit(solution)/shard_map/ppermute | solution.py:259
  27.0 12.8 %copy-start.1 = (bf16[4,256,256]{2,1,0:T(8,128)(2,1)}, bf16[4,256,256]{2,1,0:T(8,128)(2,1)S(1)}, u32[]{:S(2)}) copy-start(bf16[4,256,256]{2,1,0:T(8,128)(2,1)S(1)} %collective-permute-done.1.far_hi_ref) | copy-start | bytes 1572868
  39.7 20.3 %copy-start.2 = (bf16[4,256,256]{2,1,0:T(8,128)(2,1)S(1)}, bf16[4,256,256]{2,1,0:T(8,128)(2,1)}, u32[]{:S(2)}) copy-start(bf16[4,256,256]{2,1,0:T(8,128)(2,1)} %copy-done.1) | copy-start | bytes 1572868
  62.3 23.7 %all-to-all-start.2 = ((bf16[8,256,256]{2,1,0:T(8,128)(2,1)}), bf16[8,256,256]{2,1,0:T(8,128)(2,1)S(1)}, u32[]{:S(2)}, u32[]{:S(2)}) async-start(bf16[8,256,256]{2,1,0:T(8,128)(2,1)} %get-tuple-element.35), calls=%async_computation.2 | async-start | bytes 2097152 | tf_op jit(solution)/shard_map/all_to_all | solution.py:266
  65.9 14.6 %collective-permute-start.6 = (f32[8,256]{1,0:T(8,128)S(1)}, f32[8,256]{1,0:T(8,128)S(1)}, u32[]{:S(2)}, u32[]{:S(2)}) collective-permute-start(f32[8,256]{1,0:T(8,128)S(1)} %get-tuple-element.40), channel_id=1, source_target_pairs={{0,6},{1,7},{2,0},{3,1},{4,2},{5,3},{6,4},{7,5},{8,14},{9,15},{10,... | collective-permute-start | bytes 24584 | tf_op jit(solution)/shard_map/ppermute | solution.py:256
  71.0 9.6 %collective-permute-start.5 = (f32[8,256]{1,0:T(8,128)S(1)}, f32[8,256]{1,0:T(8,128)S(1)}, u32[]{:S(2)}, u32[]{:S(2)}) collective-permute-start(f32[8,256]{1,0:T(8,128)S(1)} %get-tuple-element.40), channel_id=1, source_target_pairs={{0,2},{1,3},{2,4},{3,5},{4,6},{5,7},{6,0},{7,1},{8,10},{9,11},{10,... | collective-permute-start | bytes 24584 | tf_op jit(solution)/shard_map/ppermute | solution.py:256
  72.9 9.2 %collective-permute-start.4 = (f32[8,256]{1,0:T(8,128)S(1)}, f32[8,256]{1,0:T(8,128)S(1)}, u32[]{:S(2)}, u32[]{:S(2)}) collective-permute-start(f32[8,256]{1,0:T(8,128)S(1)} %get-tuple-element.40), channel_id=1, source_target_pairs={{0,4},{1,5},{2,6},{3,7},{4,0},{5,1},{6,2},{7,3},{8,12},{9,13},{10,... | collective-permute-start | bytes 24584 | tf_op jit(solution)/shard_map/ppermute | solution.py:256
  77.1 15.6 %collective-permute-start.3 = (bf16[8,256,256]{2,1,0:T(8,128)(2,1)S(1)}, bf16[8,256,256]{2,1,0:T(8,128)(2,1)}, u32[]{:S(2)}, u32[]{:S(2)}) collective-permute-start(bf16[8,256,256]{2,1,0:T(8,128)(2,1)S(1)} %all_to_all.20.x_ref), channel_id=1, source_target_pairs={{0,1},{1,0},{2,3},{3,2},{4,5},{5,4},{6,7},{7,6},{8,9},{9,8},{10,11... | collective-permute-start | bytes 3145736 | tf_op jit(solution)/shard_map/ppermute | solution.py:259
  82.1 3.1 %collective-permute-start.7 = (f32[8,256]{1,0:T(8,128)S(1)}, f32[8,256]{1,0:T(8,128)S(1)}, u32[]{:S(2)}, u32[]{:S(2)}) collective-permute-start(f32[8,256]{1,0:T(8,128)S(1)} %add_add_fusion.mine_ref), channel_id=1, source_target_pairs={{0,1},{1,0},{2,3},{3,2},{4,5},{5,4},{6,7},{7,6},{8,9},{9,8},{10,11... | collective-permute-start | bytes 24584 | tf_op jit(solution)/shard_map/ppermute | solution.py:259
  87.5 25.0 %all-to-all-start.3 = ((bf16[64,16,256]{2,1,0:T(8,128)(2,1)}), bf16[64,16,256]{2,1,0:T(8,128)(2,1)S(1)}, u32[]{:S(2)}, u32[]{:S(2)}) async-start(bf16[64,16,256]{2,1,0:T(8,128)(2,1)} %bitcast.14), calls=%async_computation.3 | async-start | bytes 1048576 | tf_op jit(solution)/shard_map/all_to_all | solution.py:263

commit v7 on v5

--- a/solution.py
+++ b/solution.py
@@ -101,9 +101,10 @@
     part = arms * SLOT // PARTS
     for i in range(PARTS):
         place = ones_where(iota((part, rows), 0) + i * part == slot)
-        mark = ones_where(iota((part, arms), 0) + i * part == iota((part, arms), 1) * SLOT + SIDE)
         cut = pl.ds(i * part, part)
-        slots_ref[cut, :] = (mm(place, rep) + mm(mark, side)).astype(BF16)
+        slots_ref[cut, :] = mm(place, rep).astype(BF16)
+        few = part // SLOT
+        slots_ref.reshape(arms, SLOT, width)[i * few : (i + 1) * few, SIDE, :] = side[i * few : (i + 1) * few]
         stores.append(pltpu.make_async_copy(slots_ref.at[cut], slots_hbm.at[cut], out_sem.at[i]))
         stores[-1].start()
     for store in stores:
@@ -221,7 +222,7 @@
     slots = slots_ref[...]
     place = ones_where(iota((total, rows), 0) == aux_ref[0:1])
     grad_ref[...] = mm(place, slots, TN).astype(BF16)
-    pred_side = side_of(slots, arms).astype(BF16)
+    pred_side = slots_ref.reshape(arms, SLOT, width)[:, SIDE, :]
     by_arm = mm(pred_side, ones_where(iota((width, rows), 0) == aux_ref[1:2]))
     hot = iota((arms, rows), 0) == aux_ref[2:3]
     pred = jnp.sum(jnp.where(hot, by_arm, 0.0), axis=0, keepdims=True)

time: 110 us -> 110 us (level)
  no operation moved by 1% of the time
where the time goes in v7:
time: 110 us
  waiting for transfers between devices  43.2 us (39%)
  starting transfers between devices  31.9 us (29%)
  blocking collectives  20.2 us (18%)
  Pallas kernels  12.9 us (12%)
  between operations  1.45 us (1%)
    all_to_all x2, waiting for transfers between devices, exchange(): lax.all_to_all(cut, 'dp', split_axis=0, concat_axis=0, tiled=True)  29.3 us
    all_to_all x2, starting transfers between devices, exchange(): lax.all_to_all(cut, 'dp', split_axis=0, concat_axis=0, tiled=True)  21.7 us
    all_to_all x1, blocking collectives, spread(): lax.all_to_all(blocks, 'tower', split_axis=0, concat_axis=0, tiled=True)  20.2 us
    all_to_all x1, waiting for transfers between devices, spread(): lax.all_to_all(blocks, 'tower', split_axis=0, concat_axis=0, tiled=True)  13.1 us
    pallas_call x7, Pallas kernels, run(): pl.pallas_call(kernel, out_shape=[forced[m](o.shape, o.dtype) if m in for...  12.9 us
    ppermute x3, starting transfers between devices, swap(): return lax.ppermute(value, 'tower', [(i, i ^ 1) for i in range(tower)])  6.63 us
    all_to_all x1, starting transfers between devices, spread(): lax.all_to_all(blocks, 'tower', split_axis=0, concat_axis=0, tiled=True)  3.57 us
  transfers between devices with their start and end apart: 6, of which 4 were waited for; matrix products, arithmetic and copies ran while one was open for 0% of the time, Pallas kernels for 7%

profile of v7, /device:TPU:16, one launch (start us, length us, event | category | flops | bytes accessed | tf_op | source)
XLA Modules:
  0.0 109.6 jit_solution(17732580804648802386)
XLA Ops:
  0.6 0.0 copy-start
  0.6 0.0 copy-start.1
  0.7 2.3 %shard_map.127 = (bf16[1024,256]{1,0:T(8,128)(2,1)}, s32[8,256]{1,0:T(8,128)S(1)}) custom-call(s32[1,256]{1,0:T(1,128)} %bitcast.15, bf16[256]{0:T(256)(128)(2,1)} %outcome_hbm.1, bf16[256]{0:T(256)(128)(2,1)} %weight_hbm.1, bf16[256,256]{1,0:T(8,128)(2,1)} %rep_hbm.1), custom_call_target="tpu_custom_call" | custom-call | flops 134217728 | tf_op jit(solution)/shard_map/pallas_call | solution.py:45
  2.9 16.5 %all-to-all-start = ((bf16[64,16,256]{2,1,0:T(8,128)(2,1)}), bf16[64,16,256]{2,1,0:T(8,128)(2,1)S(1)}, u32[]{:S(2)}, u32[]{:S(2)}) async-start(bf16[64,16,256]{2,1,0:T(8,128)(2,1)} %bitcast.14), calls=%async_computation | async-start | bytes 1048576 | tf_op jit(solution)/shard_map/all_to_all | solution.py:267
  19.4 1.9 %collective-permute-start.1 = (bf16[8,256,256]{2,1,0:T(8,128)(2,1)S(1)}, bf16[8,256,256]{2,1,0:T(8,128)(2,1)S(1)}, u32[]{:S(2)}, u32[]{:S(2)}) collective-permute-start(bf16[8,256,256]{2,1,0:T(8,128)(2,1)S(1)} %bitcast.10), channel_id=1, source_target_pairs={{0,1},{1,0},{2,3},{3,2},{4,5},{5,4},{6,7},{7,6},{8,9},{9,8},{10,11... | collective-permute-start | bytes 3145736 | tf_op jit(solution)/shard_map/ppermute | solution.py:263
  21.4 0.0 copy-done.1
  21.4 0.0 copy-done.2
  21.4 2.4 %collective-permute-start = (f32[2,256]{1,0:T(2,128)S(1)}, f32[2,256]{1,0:T(2,128)S(1)}, u32[]{:S(2)}, u32[]{:S(2)}) collective-permute-start(f32[2,256]{1,0:T(2,128)S(1)} %pad_maximum_fusion.bh_ref), channel_id=1, source_target_pairs={{0,1},{1,0},{2,3},{3,2},{4,5},{5,4},{6,7},{7,6},{8,9},{9,8},{10,11... | collective-permute-start | bytes 6152 | tf_op jit(solution)/shard_map/ppermute | solution.py:263
  23.8 0.8 collective-permute-done.far_bh_ref
  24.6 14.2 %all-to-all-done = bf16[64,16,256]{2,1,0:T(8,128)(2,1)S(1)} async-done(((bf16[64,16,256]{2,1,0:T(8,128)(2,1)}), bf16[64,16,256]{2,1,0:T(8,128)(2,1)S(1)}, u32[]{:S(2)}, u32[]{:S(2)}) %all-to-all-start) | async-done | bytes 524320 | tf_op jit(solution)/shard_map/all_to_all | solution.py:267
  38.9 0.9 shard_map.128
  39.7 0.0 collective-permute-done.1.far_ref
  39.7 20.2 %all_to_all.20.x_ref = bf16[8,256,256]{2,1,0:T(8,128)(2,1)S(1)} all-to-all(bf16[8,256,256]{2,1,0:T(8,128)(2,1)S(1)} %get-tuple-element.29), channel_id=1, replica_groups=mesh['dp'=64,'tower'=8] {'tower'}, dimensions={0} | all-to-all | bytes 2097152 | tf_op jit(solution)/shard_map/all_to_all | solution.py:270
  59.9 2.3 %shard_map.129 = bf16[8,272,256]{2,1,0:T(8,128)(2,1)} custom-call(bf16[8,256,256]{2,1,0:T(8,128)(2,1)S(1)} %all_to_all.20.x_ref, bf16[8,256,256]{2,1,0:T(8,128)(2,1)S(1)} %bitcast.11, bf16[8,256,256]{2,1,0:T(8,128)(2,1)S(1)} %collective-permute-done.1.far_ref, f32[2,256]{1,0:T(2,128)S(1)} %pad_maximum_fusion.bh_ref, f32[2,256]{1,0:T(2,128)S(1)} %collective-permute-done.far_bh_ref), custom_call_target="tpu_custom_call" | custom-call | flops 1073741824 | tf_op jit(solution)/shard_map/pallas_call | solution.py:45
  62.2 3.6 %all-to-all-start.2 = ((bf16[8,272,256]{2,1,0:T(8,128)(2,1)}), bf16[8,272,256]{2,1,0:T(8,128)(2,1)S(1)}, u32[]{:S(2)}, u32[]{:S(2)}) async-start(bf16[8,272,256]{2,1,0:T(8,128)(2,1)} %shard_map.129), calls=%async_computation.2 | async-start | bytes 2228224 | tf_op jit(solution)/shard_map/all_to_all | solution.py:270
  65.8 2.3 %collective-permute-start.2 = (bf16[8,256,256]{2,1,0:T(8,128)(2,1)S(1)}, bf16[8,256,256]{2,1,0:T(8,128)(2,1)}, u32[]{:S(2)}, u32[]{:S(2)}) collective-permute-start(bf16[8,256,256]{2,1,0:T(8,128)(2,1)S(1)} %all_to_all.20.x_ref), channel_id=1, source_target_pairs={{0,1},{1,0},{2,3},{3,2},{4,5},{5,4},{6,7},{7,6},{8,9},{9,8},{10,11... | collective-permute-start | bytes 3145736 | tf_op jit(solution)/shard_map/ppermute | solution.py:263
  68.7 0.5 shard_map.130.side_ref
  69.2 13.1 %all-to-all-done.2.got_ref = bf16[8,272,256]{2,1,0:T(8,128)(2,1)S(1)} async-done(((bf16[8,272,256]{2,1,0:T(8,128)(2,1)}), bf16[8,272,256]{2,1,0:T(8,128)(2,1)S(1)}, u32[]{:S(2)}, u32[]{:S(2)}) %all-to-all-start.2) | async-done | bytes 1114144 | tf_op jit(solution)/shard_map/all_to_all | solution.py:270
  82.4 1.8 %shard_map.131 = (bf16[1024,256]{1,0:T(8,128)(2,1)}, f32[8,512]{1,0:T(8,128)S(1)}) custom-call(f32[1]{0:T(128)S(6)} %copy.14.bias_ref, bf16[8,272,256]{2,1,0:T(8,128)(2,1)S(1)} %all-to-all-done.2.got_ref, f32[8,512]{1,0:T(8,128)S(1)} %shard_map.130.side_ref, s32[8,1024]{1,0:T(8,128)S(1)} %get-tuple-element.36.pos_ref), custom_call_target="tpu_custom_call" | custom-call | flops 268435456 | tf_op jit(solution)/shard_map/pallas_call | solution.py:45
  84.2 5.2 %all-to-all-start.3 = ((bf16[64,16,256]{2,1,0:T(8,128)(2,1)}), bf16[64,16,256]{2,1,0:T(8,128)(2,1)S(1)}, u32[]{:S(2)}, u32[]{:S(2)}) async-start(bf16[64,16,256]{2,1,0:T(8,128)(2,1)} %bitcast.13), calls=%async_computation.3 | async-start | bytes 1048576 | tf_op jit(solution)/shard_map/all_to_all | solution.py:267
  89.4 0.0 collective-permute-done.2.far_x_ref
  89.4 4.1 %shard_map.132 = (f32[8,256,256]{2,1,0:T(8,128)}, f32[1,256]{1,0:T(1,128)}, f32[1,256]{1,0:T(1,128)}, f32[1]{0:T(128)}) custom-call(s32[1]{0:T(128)} %bitcast.core_ref, bf16[8,256,256]{2,1,0:T(8,128)(2,1)S(1)} %all_to_all.20.x_ref, bf16[8,256,256]{2,1,0:T(8,128)(2,1)} %collective-permute-done.2.far_x_ref, bf16[8,256,256]{2,1,0:T(8,128)(2,1)S(1)} %bitcast.12, ...), custom_call_target="tpu_custom_call" | custom-call | flops 1073741824 | bytes 5242880 | tf_op jit(solution)/shard_map/pallas_call | solution.py:45
  93.6 15.0 %all-to-all-done.3 = bf16[64,16,256]{2,1,0:T(8,128)(2,1)S(1)} async-done(((bf16[64,16,256]{2,1,0:T(8,128)(2,1)}), bf16[64,16,256]{2,1,0:T(8,128)(2,1)S(1)}, u32[]{:S(2)}, u32[]{:S(2)}) %all-to-all-start.3) | async-done | bytes 524320 | tf_op jit(solution)/shard_map/all_to_all | solution.py:267
  108.6 1.0 shard_map.133
  (3 shorter events, 0.0 us)
Async XLA Ops:
  0.6 18.8 %copy-start = (bf16[1,2048,256]{2,1,0:T(8,128)(2,1)S(1)}, bf16[1,2048,256]{2,1,0:T(8,128)(2,1)}, u32[]{:S(2)}) copy-start(bf16[1,2048,256]{2,1,0:T(8,128)(2,1)} %param.12) | copy-start | bytes 3145732
  0.6 20.7 %copy-start.1 = (f32[1,256]{1,0:T(1,128)S(1)}, f32[1,256]{1,0:T(1,128)}, u32[]{:S(2)}) copy-start(f32[1,256]{1,0:T(1,128)} %param.14) | copy-start | bytes 3076
  0.7 20.7 %copy-start.2 = (f32[1,256]{1,0:T(1,128)S(1)}, f32[1,256]{1,0:T(1,128)}, u32[]{:S(2)}) copy-start(f32[1,256]{1,0:T(1,128)} %param.13) | copy-start | bytes 3076
  2.9 35.9 %all-to-all-start = ((bf16[64,16,256]{2,1,0:T(8,128)(2,1)}), bf16[64,16,256]{2,1,0:T(8,128)(2,1)S(1)}, u32[]{:S(2)}, u32[]{:S(2)}) async-start(bf16[64,16,256]{2,1,0:T(8,128)(2,1)} %bitcast.14), calls=%async_computation | async-start | bytes 1048576 | tf_op jit(solution)/shard_map/all_to_all | solution.py:267
  19.4 20.3 %collective-permute-start.1 = (bf16[8,256,256]{2,1,0:T(8,128)(2,1)S(1)}, bf16[8,256,256]{2,1,0:T(8,128)(2,1)S(1)}, u32[]{:S(2)}, u32[]{:S(2)}) collective-permute-start(bf16[8,256,256]{2,1,0:T(8,128)(2,1)S(1)} %bitcast.10), channel_id=1, source_target_pairs={{0,1},{1,0},{2,3},{3,2},{4,5},{5,4},{6,7},{7,6},{8,9},{9,8},{10,11... | collective-permute-start | bytes 3145736 | tf_op jit(solution)/shard_map/ppermute | solution.py:263
  21.4 3.2 %collective-permute-start = (f32[2,256]{1,0:T(2,128)S(1)}, f32[2,256]{1,0:T(2,128)S(1)}, u32[]{:S(2)}, u32[]{:S(2)}) collective-permute-start(f32[2,256]{1,0:T(2,128)S(1)} %pad_maximum_fusion.bh_ref), channel_id=1, source_target_pairs={{0,1},{1,0},{2,3},{3,2},{4,5},{5,4},{6,7},{7,6},{8,9},{9,8},{10,11... | collective-permute-start | bytes 6152 | tf_op jit(solution)/shard_map/ppermute | solution.py:263
  62.2 20.2 %all-to-all-start.2 = ((bf16[8,272,256]{2,1,0:T(8,128)(2,1)}), bf16[8,272,256]{2,1,0:T(8,128)(2,1)S(1)}, u32[]{:S(2)}, u32[]{:S(2)}) async-start(bf16[8,272,256]{2,1,0:T(8,128)(2,1)} %shard_map.129), calls=%async_computation.2 | async-start | bytes 2228224 | tf_op jit(solution)/shard_map/all_to_all | solution.py:270
  65.8 23.6 %collective-permute-start.2 = (bf16[8,256,256]{2,1,0:T(8,128)(2,1)S(1)}, bf16[8,256,256]{2,1,0:T(8,128)(2,1)}, u32[]{:S(2)}, u32[]{:S(2)}) collective-permute-start(bf16[8,256,256]{2,1,0:T(8,128)(2,1)S(1)} %all_to_all.20.x_ref), channel_id=1, source_target_pairs={{0,1},{1,0},{2,3},{3,2},{4,5},{5,4},{6,7},{7,6},{8,9},{9,8},{10,11... | collective-permute-start | bytes 3145736 | tf_op jit(solution)/shard_map/ppermute | solution.py:263
  84.2 24.4 %all-to-all-start.3 = ((bf16[64,16,256]{2,1,0:T(8,128)(2,1)}), bf16[64,16,256]{2,1,0:T(8,128)(2,1)S(1)}, u32[]{:S(2)}, u32[]{:S(2)}) async-start(bf16[64,16,256]{2,1,0:T(8,128)(2,1)} %bitcast.13), calls=%async_computation.3 | async-start | bytes 1048576 | tf_op jit(solution)/shard_map/all_to_all | solution.py:267
